TPU v7x, 256 devices: a whole 4x4x8 slice. The times are simulated.
256 devices in a mesh: tm: 16 (over z_hi, x, core), sx: 4 (over y), sy: 4 (over z_lo).
Axes of the slice: x: 4, y: 4, z: 8 (z_hi: 2, z_lo: 4; z = z_hi * 4 + z_lo), core: 2. Of those that a mesh axis runs over, the one named last changes fastest.
Arguments:
- depth_start: float32 [16, 256, 4096], P('tm', 'sx', 'sy'), may hold values from 0 to 0.3
- flux_start: float32 [16, 2, 256, 4096], P('tm', None, 'sx', 'sy'), may hold values from -0.45 to 0.45
- elevation: float32 [256, 4096], P('sx', 'sy'), may hold values from 0 to 0.3
- roughness_class: int32 [256, 4096], P('sx', 'sy'), may hold values from 0 to 7
- building: int32 [256, 4096], P('sx', 'sy'), may hold values 0 or 1
- manning: float32 [8], replicated, may hold values from 0.03 to 0.3
- radar_rates: float32 [64], replicated, may hold values from 1e-05 to 0.0005
- tile_index: int32 [16, 8, 4, 64], P('tm'), may hold values from 0 to 63
Outputs:
- depth_end: float32 [16, 256, 4096], P('tm', 'sx', 'sy')
- flux_end: float32 [16, 2, 256, 4096], P('tm', None, 'sx', 'sy')
All inputs are finite; a program needn't handle non-finite values. No bound on the sum of `building` on one device may be relied on, other than what follows from the above.
Results may differ from a plain program's by a relative error of at most 0.00002.
Values sent between devices are 32-bit elements; how exact they have to be, the bound alone decides.
No kernel may reach another device: no remote copies, remote signals or barrier semaphores. Data moves between devices by JAX's collectives and lax.ppermute only.
A program may use at most 128 MiB of HBM per device.

v0:
```python
import jax
import jax.numpy as jnp
from jax import lax
from jax.sharding import PartitionSpec as P

FINE_STEPS = 8
COARSE_STEPS = 2
COARSENING = 4
RAIN_BLOCK = 64


GRAVITY = 9.81
DEPTH_FLOOR = 0.05
CELL_SIDE = 2.0
TIME_STEP = 0.25
SEVEN_THIRDS = 7.0 / 3.0


def padded_2(block, sides, width):
    for axis, dim in sides:
        count = lax.axis_size(axis)
        forward = [(i, i + 1) for i in range(count - 1)]
        backward = [(target, source) for source, target in forward]
        low = lax.ppermute(
            lax.slice_in_dim(block, block.shape[dim] - width, None, axis=dim), axis, forward
        )
        high = lax.ppermute(lax.slice_in_dim(block, 0, width, axis=dim), axis, backward)
        block = jnp.concatenate([low, block, high], axis=dim)
    return block


def passed_along(block, axis, distance):
    devices = range(lax.axis_size(axis))
    route = [(i - distance, i) for i in devices if i - distance in devices]
    return lax.ppermute(block, axis, route)


def face_flux(
    flux_in,
    level_a,
    level_b,
    ground_a,
    ground_b,
    rough_a,
    rough_b,
    open_a,
    open_b,
    spacing,
    seconds,
):
    flow_depth = jnp.maximum(jnp.maximum(level_a, level_b) - jnp.maximum(ground_a, ground_b), 0.0)
    surface_slope = (level_b - level_a) / spacing
    face_rough = 0.5 * (rough_a + rough_b)
    depth_power = jnp.exp(SEVEN_THIRDS * jnp.log(jnp.maximum(flow_depth, DEPTH_FLOOR)))
    return (
        open_a
        * open_b
        * (flux_in - GRAVITY * seconds * flow_depth * surface_slope)
        / (1.0 + GRAVITY * seconds * face_rough * face_rough * jnp.abs(flux_in) / depth_power)
    )


def advance(fields, ground, rainfall, spacing, seconds):
    surface = ground[0] + fields[0]
    heights, frictions, openness = (ground[0], ground[1], ground[2])
    east_flux = face_flux(
        fields[1][:-1, :],
        surface[:-1, :],
        surface[1:, :],
        heights[:-1, :],
        heights[1:, :],
        frictions[:-1, :],
        frictions[1:, :],
        openness[:-1, :],
        openness[1:, :],
        spacing,
        seconds,
    )
    north_flux = face_flux(
        fields[2][:, :-1],
        surface[:, :-1],
        surface[:, 1:],
        heights[:, :-1],
        heights[:, 1:],
        frictions[:, :-1],
        frictions[:, 1:],
        openness[:, :-1],
        openness[:, 1:],
        spacing,
        seconds,
    )
    inflow = (
        east_flux[:-1, 1:-1] - east_flux[1:, 1:-1] + (north_flux[1:-1, :-1] - north_flux[1:-1, 1:])
    )
    new_depth = fields[0][1:-1, 1:-1] + seconds * (inflow / spacing + rainfall)
    return jnp.stack([new_depth, east_flux[1:, 1:-1], north_flux[1:-1, 1:]])


def restrict(fields):
    return fields.reshape(
        fields.shape[0],
        fields.shape[1] // COARSENING,
        COARSENING,
        fields.shape[2] // COARSENING,
        COARSENING,
    ).mean(axis=(2, 4))


def spread(blocks, factor):
    return jnp.repeat(jnp.repeat(blocks, factor, axis=-2), factor, axis=-1)


def lookup(indices, values_table):
    entries = jnp.arange(values_table.shape[0], dtype=jnp.int32)
    return jnp.sum(jnp.where(indices[..., None] == entries, values_table, 0.0), axis=-1)


def on_device(
    depth_start, flux_start, elevation, roughness_class, building, manning, radar_rates, tile_index
):
    open_cells = 1.0 - building.astype(jnp.float32)
    friction = lookup(roughness_class, manning)
    ground = jnp.stack([elevation, friction, open_cells])
    cells_x = elevation.shape[0]
    cells_y = elevation.shape[1]
    blocks_x = cells_x // RAIN_BLOCK
    blocks_y = cells_y // RAIN_BLOCK
    row_place = lax.axis_index("sx")
    col_place = lax.axis_index("sy")
    anchor = jnp.zeros((), jnp.int32)
    index_pad = jnp.pad(tile_index[0], ((0, 0), (1, 1), (1, 1)))
    index_window = lax.dynamic_slice(
        index_pad,
        (anchor, row_place * blocks_x, col_place * blocks_y),
        (FINE_STEPS, blocks_x + 2, blocks_y + 2),
    )
    rates_pad = lookup(index_window, radar_rates)
    rates_own = rates_pad[:, 1:-1, 1:-1]
    margin = 1
    ground_pad = padded_2(ground, (("sx", 1), ("sy", 2)), margin)
    fields = jnp.concatenate([depth_start[0][None], flux_start[0]], axis=0)
    start_coarse = restrict(fields)
    for moment in range(FINE_STEPS):
        padded = padded_2(fields, (("sx", 1), ("sy", 2)), 1)
        fields = advance(
            padded, ground_pad, spread(rates_own[moment], RAIN_BLOCK), CELL_SIDE, TIME_STEP
        )
    coarse_ground_own = restrict(ground)
    coarse_pad = padded_2(coarse_ground_own, (("sx", 1), ("sy", 2)), 1)
    coarse_seconds = TIME_STEP * FINE_STEPS / COARSE_STEPS
    coarse_rates = rates_own.reshape(
        COARSE_STEPS, FINE_STEPS // COARSE_STEPS, rates_own.shape[1], rates_own.shape[2]
    ).mean(axis=1)
    rain_coarse = spread(coarse_rates, RAIN_BLOCK // COARSENING)

    def coarse_run(current, rain_now):
        for moment in range(COARSE_STEPS):
            padded = padded_2(current, (("sx", 1), ("sy", 2)), 1)
            current = advance(
                padded, coarse_pad, rain_now[moment], CELL_SIDE * COARSENING, coarse_seconds
            )
        return current

    coarse_old = coarse_run(start_coarse, rain_coarse)
    correction = restrict(fields) - coarse_old
    slices = lax.axis_size("tm")
    myself = lax.axis_index("tm")

    def sweep_turn(moment, current):
        advanced = passed_along(coarse_run(current, rain_coarse) + correction, "tm", 1)
        return jnp.where(myself == 0, current, advanced)

    current = lax.fori_loop(0, slices - 1, sweep_turn, start_coarse)
    newest = coarse_run(current, rain_coarse)
    result = fields + spread(newest - coarse_old, COARSENING)
    return (result[0][None], result[1:][None])


def solution(mesh):
    placed = (
        P("tm", "sx", "sy"),
        P("tm", None, "sx", "sy"),
        P("sx", "sy"),
        P("sx", "sy"),
        P("sx", "sy"),
        P(),
        P(),
        P("tm", None, None, None),
    )
    return jax.shard_map(
        on_device,
        mesh=mesh,
        in_specs=placed,
        out_specs=(P("tm", "sx", "sy"), P("tm", None, "sx", "sy")),
        check_vma=False,
    )
```

profile of v0, /device:TPU:248, one launch (start us, length us, event | category | flops | bytes accessed | tf_op | source)
XLA Modules:
  0.0 1067.7 jit_solution(13979816648184236559)
XLA Ops:
  0.6 19.5 %concatenate.144 = f32[2,16,4,256,4]{4,3,2,1,0:T(8,128)} reshape(f32[1,2,64,1024]{3,2,1,0:T(8,128)} %param.11) | data formatting | bytes 1048576 | tf_op jit(solution)/shard_map/concatenate | solution.py:141
  20.1 10.1 copy.104
  30.2 10.0 concatenate.143
  49.7 10.0 stack.266
  65.7 10.0 stack.265
  81.1 10.0 stack.264
  335.0 10.0 stack.270
  350.2 10.0 stack.269
  365.5 10.0 stack.268
  381.0 651.4 %while.13 = (s32[]{:T(128)}, f32[3,16,256]{2,1,0:T(8,128)S(1)}, pred[]{:T(512)}, f32[3,18,258]{2,1,0:T(8,128)S(1)}, f32[17,258]{1,0:T(8,128)S(1)}, /*index=5*/f3...) while((s32[]{:T(128)}, f32[3,16,256]{2,1,0:T(8,128)S(1)}, ...), condition=%wide.region_7.8_spmd, body=%wide.region_6.7_spmd.sunk | while | flops 675386 | bytes 2117670 | solution.py:173
  418.9 9.5 collective-permute-done.8
  463.9 9.5 collective-permute-done.8
  506.9 9.5 collective-permute-done.8
  549.8 9.5 collective-permute-done.8
  592.8 9.5 collective-permute-done.8
  635.8 9.5 collective-permute-done.8
  678.7 9.5 collective-permute-done.8
  721.7 9.5 collective-permute-done.8
  764.7 9.5 collective-permute-done.8
  807.7 9.5 collective-permute-done.8
  850.8 9.5 collective-permute-done.8
  893.8 9.5 collective-permute-done.8
  936.8 9.5 collective-permute-done.8
  979.7 9.5 collective-permute-done.8
  (916 shorter events, 829.3 us)
Async XLA Ops:
  45.6 69.6 %collective-permute-start.50 = (f32[3,1,256]{2,1,0:T(1,128)S(1)}, f32[3,1,256]{2,1,0:T(1,128)S(1)}, u32[]{:S(2)}, u32[]{:S(2)}) collective-permute-start(f32[3,1,256]{2,1,0:T(1,128)S(1)} %get-tuple-element.330), channel_id=1, source_target_pairs={{4,0},{8,4},{12,8},{5,1},{9,5},{13,9},{6,2},{10,6},{14,10},{7,3},{... | collective-permute-start | bytes 9224 | tf_op jit(solution)/shard_map/ppermute | solution.py:27
  48.3 68.3 %collective-permute-start.49 = (f32[3,1,256]{2,1,0:T(1,128)S(1)}, f32[3,1,256]{2,1,0:T(1,128)S(1)}, u32[]{:S(2)}, u32[]{:S(2)}) collective-permute-start(f32[3,1,256]{2,1,0:T(1,128)S(1)} %get-tuple-element.329), channel_id=1, source_target_pairs={{0,4},{4,8},{8,12},{1,5},{5,9},{9,13},{2,6},{6,10},{10,14},{3,7},{... | collective-permute-start | bytes 9224 | tf_op jit(solution)/shard_map/ppermute | solution.py:24
  96.5 20.2 %collective-permute-start.46 = (f32[3,1,256]{2,1,0:T(1,128)S(1)}, f32[3,1,256]{2,1,0:T(1,128)S(1)}, u32[]{:S(2)}, u32[]{:S(2)}) collective-permute-start(f32[3,1,256]{2,1,0:T(1,128)S(1)} %get-tuple-element.328), channel_id=1, source_target_pairs={{4,0},{8,4},{12,8},{5,1},{9,5},{13,9},{6,2},{10,6},{14,10},{7,3},{... | collective-permute-start | bytes 9224 | tf_op jit(solution)/shard_map/ppermute | solution.py:27
  101.0 15.6 %collective-permute-start.45 = (f32[3,1,256]{2,1,0:T(1,128)S(1)}, f32[3,1,256]{2,1,0:T(1,128)S(1)}, u32[]{:S(2)}, u32[]{:S(2)}) collective-permute-start(f32[3,1,256]{2,1,0:T(1,128)S(1)} %get-tuple-element.327), channel_id=1, source_target_pairs={{0,4},{4,8},{8,12},{1,5},{5,9},{9,13},{2,6},{6,10},{10,14},{3,7},{... | collective-permute-start | bytes 9224 | tf_op jit(solution)/shard_map/ppermute | solution.py:24
  110.7 23.6 %collective-permute-start.10 = (f32[3,1,1024]{2,1,0:T(1,128)S(1)}, f32[3,1,1024]{2,1,0:T(1,128)S(1)}, u32[]{:S(2)}, u32[]{:S(2)}) collective-permute-start(f32[3,1,1024]{2,1,0:T(1,128)S(1)} %get-tuple-element.271), channel_id=1, source_target_pairs={{4,0},{8,4},{12,8},{5,1},{9,5},{13,9},{6,2},{10,6},{14,10},{7,3},{... | collective-permute-start | bytes 36872 | tf_op jit(solution)/shard_map/ppermute | solution.py:27
  115.3 19.0 %collective-permute-start.9 = (f32[3,1,1024]{2,1,0:T(1,128)S(1)}, f32[3,1,1024]{2,1,0:T(1,128)S(1)}, u32[]{:S(2)}, u32[]{:S(2)}) collective-permute-start(f32[3,1,1024]{2,1,0:T(1,128)S(1)} %get-tuple-element.270), channel_id=1, source_target_pairs={{0,4},{4,8},{8,12},{1,5},{5,9},{9,13},{2,6},{6,10},{10,14},{3,7},{... | collective-permute-start | bytes 36872 | tf_op jit(solution)/shard_map/ppermute | solution.py:24
  127.6 13.4 %collective-permute-start.14 = (f32[3,1,1024]{2,1,0:T(1,128)S(1)}, f32[3,1,1024]{2,1,0:T(1,128)S(1)}, u32[]{:S(2)}, u32[]{:S(2)}) collective-permute-start(f32[3,1,1024]{2,1,0:T(1,128)S(1)} %get-tuple-element.269), channel_id=1, source_target_pairs={{4,0},{8,4},{12,8},{5,1},{9,5},{13,9},{6,2},{10,6},{14,10},{7,3},{... | collective-permute-start | bytes 36872 | tf_op jit(solution)/shard_map/ppermute | solution.py:27
  134.5 14.2 %collective-permute-start.11 = (f32[3,66,1]{2,1,0:T(8,128)S(1)}, f32[3,66,1]{2,1,0:T(8,128)S(1)}, u32[]{:S(2)}, u32[]{:S(2)}) collective-permute-start(f32[3,66,1]{2,1,0:T(8,128)S(1)} %get-tuple-element.253), channel_id=1, source_target_pairs={{0,1},{1,2},{2,3},{4,5},{5,6},{6,7},{8,9},{9,10},{10,11},{12,13},{... | collective-permute-start | bytes 2384 | tf_op jit(solution)/shard_map/ppermute | solution.py:24
  135.8 12.9 %collective-permute-start.12 = (f32[3,66,1]{2,1,0:T(8,128)S(1)}, f32[3,66,1]{2,1,0:T(8,128)S(1)}, u32[]{:S(2)}, u32[]{:S(2)}) collective-permute-start(f32[3,66,1]{2,1,0:T(8,128)S(1)} %get-tuple-element.252), channel_id=1, source_target_pairs={{1,0},{2,1},{3,2},{5,4},{6,5},{7,6},{9,8},{10,9},{11,10},{13,12},{... | collective-permute-start | bytes 2384 | tf_op jit(solution)/shard_map/ppermute | solution.py:27
  221.9 16.2 %collective-permute-start.54 = (f32[3,1,256]{2,1,0:T(1,128)}, f32[3,1,256]{2,1,0:T(1,128)S(1)}, u32[]{:S(2)}, u32[]{:S(2)}) collective-permute-start(f32[3,1,256]{2,1,0:T(1,128)} %get-tuple-element.326), channel_id=1, source_target_pairs={{4,0},{8,4},{12,8},{5,1},{9,5},{13,9},{6,2},{10,6},{14,10},{7,3},{... | collective-permute-start | bytes 9224 | tf_op jit(solution)/shard_map/ppermute | solution.py:27
  223.8 14.3 %collective-permute-start.53 = (f32[3,1,256]{2,1,0:T(1,128)}, f32[3,1,256]{2,1,0:T(1,128)S(1)}, u32[]{:S(2)}, u32[]{:S(2)}) collective-permute-start(f32[3,1,256]{2,1,0:T(1,128)} %get-tuple-element.325), channel_id=1, source_target_pairs={{0,4},{4,8},{8,12},{1,5},{5,9},{9,13},{2,6},{6,10},{10,14},{3,7},{... | collective-permute-start | bytes 9224 | tf_op jit(solution)/shard_map/ppermute | solution.py:24
  243.4 11.7 %collective-permute-start.31 = (f32[3,66,1]{2,1,0:T(8,128)S(1)}, f32[3,66,1]{2,1,0:T(8,128)S(1)}, u32[]{:S(2)}, u32[]{:S(2)}) collective-permute-start(f32[3,66,1]{2,1,0:T(8,128)S(1)} %get-tuple-element.243), channel_id=1, source_target_pairs={{0,1},{1,2},{2,3},{4,5},{5,6},{6,7},{8,9},{9,10},{10,11},{12,13},{... | collective-permute-start | bytes 2384 | tf_op jit(solution)/shard_map/ppermute | solution.py:24
  250.6 14.9 %collective-permute-start.56 = (f32[3,18,1]{2,1,0:T(8,128)}, f32[3,18,1]{2,1,0:T(8,128)}, u32[]{:S(2)}, u32[]{:S(2)}) collective-permute-start(f32[3,18,1]{2,1,0:T(8,128)} %get-tuple-element.316), channel_id=1, source_target_pairs={{1,0},{2,1},{3,2},{5,4},{6,5},{7,6},{9,8},{10,9},{11,10},{13,12},{... | collective-permute-start | bytes 656 | tf_op jit(solution)/shard_map/ppermute | solution.py:27
  253.9 11.7 %collective-permute-start.55 = (f32[3,18,1]{2,1,0:T(8,128)}, f32[3,18,1]{2,1,0:T(8,128)}, u32[]{:S(2)}, u32[]{:S(2)}) collective-permute-start(f32[3,18,1]{2,1,0:T(8,128)} %get-tuple-element.315), channel_id=1, source_target_pairs={{0,1},{1,2},{2,3},{4,5},{5,6},{6,7},{8,9},{9,10},{10,11},{12,13},{... | collective-permute-start | bytes 656 | tf_op jit(solution)/shard_map/ppermute | solution.py:24
  417.0 11.4 %collective-permute-start.8 = (f32[3,16,256]{2,1,0:T(8,128)S(1)}, f32[3,16,256]{2,1,0:T(8,128)S(1)}, u32[]{:S(2)}, u32[]{:S(2)}) collective-permute-start(f32[3,16,256]{2,1,0:T(8,128)S(1)} %maximum_add_fusion.3), channel_id=1, source_target_pairs={{0,16},{16,32},{32,48},{48,64},{64,80},{80,96},{96,112},{112,128},... | collective-permute-start | bytes 147464 | tf_op jit(solution)/shard_map/while/body/eval_jaxpr/ppermute | solution.py:35
  462.0 11.4 %collective-permute-start.8 = (f32[3,16,256]{2,1,0:T(8,128)S(1)}, f32[3,16,256]{2,1,0:T(8,128)S(1)}, u32[]{:S(2)}, u32[]{:S(2)}) collective-permute-start(f32[3,16,256]{2,1,0:T(8,128)S(1)} %maximum_add_fusion.3), channel_id=1, source_target_pairs={{0,16},{16,32},{32,48},{48,64},{64,80},{80,96},{96,112},{112,128},... | collective-permute-start | bytes 147464 | tf_op jit(solution)/shard_map/while/body/eval_jaxpr/ppermute | solution.py:35
  504.9 11.4 %collective-permute-start.8 = (f32[3,16,256]{2,1,0:T(8,128)S(1)}, f32[3,16,256]{2,1,0:T(8,128)S(1)}, u32[]{:S(2)}, u32[]{:S(2)}) collective-permute-start(f32[3,16,256]{2,1,0:T(8,128)S(1)} %maximum_add_fusion.3), channel_id=1, source_target_pairs={{0,16},{16,32},{32,48},{48,64},{64,80},{80,96},{96,112},{112,128},... | collective-permute-start | bytes 147464 | tf_op jit(solution)/shard_map/while/body/eval_jaxpr/ppermute | solution.py:35
  547.9 11.4 %collective-permute-start.8 = (f32[3,16,256]{2,1,0:T(8,128)S(1)}, f32[3,16,256]{2,1,0:T(8,128)S(1)}, u32[]{:S(2)}, u32[]{:S(2)}) collective-permute-start(f32[3,16,256]{2,1,0:T(8,128)S(1)} %maximum_add_fusion.3), channel_id=1, source_target_pairs={{0,16},{16,32},{32,48},{48,64},{64,80},{80,96},{96,112},{112,128},... | collective-permute-start | bytes 147464 | tf_op jit(solution)/shard_map/while/body/eval_jaxpr/ppermute | solution.py:35
  590.9 11.4 %collective-permute-start.8 = (f32[3,16,256]{2,1,0:T(8,128)S(1)}, f32[3,16,256]{2,1,0:T(8,128)S(1)}, u32[]{:S(2)}, u32[]{:S(2)}) collective-permute-start(f32[3,16,256]{2,1,0:T(8,128)S(1)} %maximum_add_fusion.3), channel_id=1, source_target_pairs={{0,16},{16,32},{32,48},{48,64},{64,80},{80,96},{96,112},{112,128},... | collective-permute-start | bytes 147464 | tf_op jit(solution)/shard_map/while/body/eval_jaxpr/ppermute | solution.py:35
  633.8 11.4 %collective-permute-start.8 = (f32[3,16,256]{2,1,0:T(8,128)S(1)}, f32[3,16,256]{2,1,0:T(8,128)S(1)}, u32[]{:S(2)}, u32[]{:S(2)}) collective-permute-start(f32[3,16,256]{2,1,0:T(8,128)S(1)} %maximum_add_fusion.3), channel_id=1, source_target_pairs={{0,16},{16,32},{32,48},{48,64},{64,80},{80,96},{96,112},{112,128},... | collective-permute-start | bytes 147464 | tf_op jit(solution)/shard_map/while/body/eval_jaxpr/ppermute | solution.py:35
  676.8 11.4 %collective-permute-start.8 = (f32[3,16,256]{2,1,0:T(8,128)S(1)}, f32[3,16,256]{2,1,0:T(8,128)S(1)}, u32[]{:S(2)}, u32[]{:S(2)}) collective-permute-start(f32[3,16,256]{2,1,0:T(8,128)S(1)} %maximum_add_fusion.3), channel_id=1, source_target_pairs={{0,16},{16,32},{32,48},{48,64},{64,80},{80,96},{96,112},{112,128},... | collective-permute-start | bytes 147464 | tf_op jit(solution)/shard_map/while/body/eval_jaxpr/ppermute | solution.py:35
  762.7 11.4 %collective-permute-start.8 = (f32[3,16,256]{2,1,0:T(8,128)S(1)}, f32[3,16,256]{2,1,0:T(8,128)S(1)}, u32[]{:S(2)}, u32[]{:S(2)}) collective-permute-start(f32[3,16,256]{2,1,0:T(8,128)S(1)} %maximum_add_fusion.3), channel_id=1, source_target_pairs={{0,16},{16,32},{32,48},{48,64},{64,80},{80,96},{96,112},{112,128},... | collective-permute-start | bytes 147464 | tf_op jit(solution)/shard_map/while/body/eval_jaxpr/ppermute | solution.py:35
  891.9 11.4 %collective-permute-start.8 = (f32[3,16,256]{2,1,0:T(8,128)S(1)}, f32[3,16,256]{2,1,0:T(8,128)S(1)}, u32[]{:S(2)}, u32[]{:S(2)}) collective-permute-start(f32[3,16,256]{2,1,0:T(8,128)S(1)} %maximum_add_fusion.3), channel_id=1, source_target_pairs={{0,16},{16,32},{32,48},{48,64},{64,80},{80,96},{96,112},{112,128},... | collective-permute-start | bytes 147464 | tf_op jit(solution)/shard_map/while/body/eval_jaxpr/ppermute | solution.py:35
  934.8 11.4 %collective-permute-start.8 = (f32[3,16,256]{2,1,0:T(8,128)S(1)}, f32[3,16,256]{2,1,0:T(8,128)S(1)}, u32[]{:S(2)}, u32[]{:S(2)}) collective-permute-start(f32[3,16,256]{2,1,0:T(8,128)S(1)} %maximum_add_fusion.3), channel_id=1, source_target_pairs={{0,16},{16,32},{32,48},{48,64},{64,80},{80,96},{96,112},{112,128},... | collective-permute-start | bytes 147464 | tf_op jit(solution)/shard_map/while/body/eval_jaxpr/ppermute | solution.py:35
  (204 other events, 2679.4 us)
where the time goes:
time: 1070 us
  waiting for transfers between devices  449 us (42%)
  starting transfers between devices  370 us (35%)
  local copies, waits for them, and re-layouts  192 us (18%)
  other arithmetic  50.9 us (5%)
    ppermute x88, waiting for transfers between devices, padded_2(): lax.ppermute(lax.slice_in_dim(block, block.shape[dim] - width, None, axis...  295 us
    ppermute x88, starting transfers between devices, padded_2(): lax.ppermute(lax.slice_in_dim(block, 0, width, axis=dim), axis, backward)  228 us
    ppermute x15, waiting for transfers between devices, passed_along(): return lax.ppermute(block, axis, route)  142 us
    ppermute x88, starting transfers between devices, padded_2(): lax.ppermute(lax.slice_in_dim(block, block.shape[dim] - width, None, axis...  114 us
    another operation x6, local copies, waits for them, and re-layouts, on_device(): ground = jnp.stack([elevation, friction, open_cells])  45.9 us
    another operation x6, local copies, waits for them, and re-layouts, advance(): return jnp.stack([new_depth, east_flux[1:, 1:-1], north_flux[1:-1, 1:]])  45.9 us
    concatenate x4, local copies, waits for them, and re-layouts, on_device(): fields = jnp.concatenate([depth_start[0][None], flux_start[0]], axis=0)  44.8 us
    ppermute x15, starting transfers between devices, passed_along(): return lax.ppermute(block, axis, route)  28.8 us
  transfers between devices with their start and end apart: 191, of which 124 were waited for; matrix products, arithmetic and copies ran while one was open for 8% of the time, Pallas kernels for 0%

commit v1 on v0

v1 whole, which is shorter than its diff:
```python
import math

import jax
import jax.numpy as jnp
from jax import lax
from jax.experimental import pallas as pl
from jax.experimental.pallas import tpu as pltpu
from jax.sharding import PartitionSpec as P

FINE_STEPS = 8
COARSE_STEPS = 2
COARSENING = 4
RAIN_BLOCK = 64
RADAR_TILES = 64
ROUGH_CLASSES = 8
SLICES = 16

GRAVITY = 9.81
DEPTH_FLOOR = 0.05
CELL_SIDE = 2.0
TIME_STEP = 0.25
COARSE_SECONDS = TIME_STEP * FINE_STEPS / COARSE_STEPS
COARSE_SIDE = CELL_SIDE * COARSENING
POWER = -7.0 / 3.0 / math.log(2.0)

ROWS, COLS = 64, 1024
EDGE = 128
HALO = 8
HIGH, WIDE = ROWS + 2 * HALO, COLS + 2 * EDGE
C_ROWS, C_COLS = ROWS // COARSENING, COLS // COARSENING
C_HIGH, C_WIDE = 32, 384
BLOCK = 3 * C_ROWS + 8
F32 = jnp.float32
BF16 = jnp.bfloat16
VMEM_LIMIT = 40 * 1024 * 1024


def face(level, level_next, flux, sill, drag, gate, pull):
    depth = jnp.maximum(jnp.maximum(level, level_next) - sill, 0.0)
    power = jnp.exp2(POWER * jnp.log(jnp.maximum(depth, DEPTH_FLOOR)))
    below = 1.0 + drag * jnp.abs(flux) * power
    inverse = pl.reciprocal(below, approx=True)
    inverse = inverse * (2.0 - below * inverse)
    return gate * inverse * (flux - pull * (level_next - level) * depth)


def split_dot(values, weights):
    first = values.astype(BF16)
    rest = values - first.astype(F32)
    second = rest.astype(BF16)
    third = (rest - second.astype(F32)).astype(BF16)
    dot = lambda part: jnp.dot(part, weights, preferred_element_type=F32)
    return dot(third) + dot(second) + dot(first)


def turn(values, shift, axis):
    return pltpu.roll(values, shift % values.shape[axis], axis)


def static_faces(elev, friction, opened, axis, seconds):
    sill = jnp.maximum(elev, turn(elev, -1, axis))
    rough = 0.5 * (friction + turn(friction, -1, axis))
    gate = opened * turn(opened, -1, axis)
    return sill, GRAVITY * seconds * rough * rough, gate


def whole_step(level, flux_x, flux_y, faces_x, faces_y, rain, side, seconds):
    pull = GRAVITY * seconds / side
    flux_x = face(level, turn(level, -1, 0), flux_x, *faces_x, pull)
    flux_y = face(level, turn(level, -1, 1), flux_y, *faces_y, pull)
    gain = (turn(flux_x, 1, 0) - flux_x) + (turn(flux_y, 1, 1) - flux_y)
    return level + (seconds / side) * gain + seconds * rain, flux_x, flux_y


def columns_kernel(*refs):
    ins, outs = refs[:10], refs[10:]
    even = lax.axis_index("sy") % 2 == 0

    def put(index, left, right):
        outs[0][pl.ds(index * ROWS, ROWS), :] = jnp.where(even, right, left)
        outs[1][pl.ds(index * ROWS, ROWS), :] = jnp.where(even, left, right)

    dl, dr, fl, fr, el, er, rl, rr, bl, br = ins
    put(0, dl[0], dr[0])
    put(1, fl[0, 0], fr[0, 0])
    put(2, fl[0, 1], fr[0, 1])
    put(3, el[...], er[...])
    put(4, rl[...].astype(F32), rr[...].astype(F32))
    put(5, bl[...].astype(F32), br[...].astype(F32))


def pack_columns(depth, flux, elevation, roughness, building):
    last = COLS // EDGE - 1
    specs, args = [], []
    for array, shape in (
        (depth, (1, ROWS, EDGE)),
        (flux, (1, 2, ROWS, EDGE)),
        (elevation, (ROWS, EDGE)),
        (roughness, (ROWS, EDGE)),
        (building, (ROWS, EDGE)),
    ):
        for place in (0, last):
            zeros = (0,) * (len(shape) - 1)
            specs.append(pl.BlockSpec(shape, lambda i, zeros=zeros, place=place: zeros + (place,)))
            args.append(array)
    out = jax.ShapeDtypeStruct((6 * ROWS, EDGE), F32)
    whole = pl.BlockSpec((6 * ROWS, EDGE), lambda i: (0, 0))
    return pl.pallas_call(
        columns_kernel, grid=(1,), in_specs=specs, out_specs=(whole, whole), out_shape=(out, out)
    )(*args)


def rows_kernel(*refs):
    ins, first, second, outs = refs[:10], refs[10], refs[11], refs[12:]
    even = lax.axis_index("sy") % 2 == 0
    dt, db, ft, fb, et, eb, rt, rb, bt, bb = ins
    fields = (
        (dt[0], db[0]),
        (ft[0, 0], fb[0, 0]),
        (ft[0, 1], fb[0, 1]),
        (et[...], eb[...]),
        (rt[...].astype(F32), rb[...].astype(F32)),
        (bt[...].astype(F32), bb[...].astype(F32)),
    )
    for index, pair in enumerate(fields):
        for side, values in enumerate(pair):
            row = index * ROWS + side * (ROWS - HALO)
            a = first[pl.ds(row, HALO), :]
            b = second[pl.ds(row, HALO), :]
            here = pl.ds(index * HALO, HALO)
            outs[side][here, 0:EDGE] = jnp.where(even, b, a)
            outs[side][here, EDGE : EDGE + COLS] = values
            outs[side][here, EDGE + COLS : WIDE] = jnp.where(even, a, b)


def pack_rows(depth, flux, elevation, roughness, building, first, second):
    last = ROWS // HALO - 1
    specs, args = [], []
    for array, shape in (
        (depth, (1, HALO, COLS)),
        (flux, (1, 2, HALO, COLS)),
        (elevation, (HALO, COLS)),
        (roughness, (HALO, COLS)),
        (building, (HALO, COLS)),
    ):
        for place in (0, last):
            zeros = (0,) * (len(shape) - 2)
            specs.append(pl.BlockSpec(shape, lambda i, zeros=zeros, place=place: zeros + (place, 0)))
            args.append(array)
    for array in (first, second):
        specs.append(pl.BlockSpec((6 * ROWS, EDGE), lambda i: (0, 0)))
        args.append(array)
    out = jax.ShapeDtypeStruct((6 * HALO, WIDE), F32)
    whole = pl.BlockSpec((6 * HALO, WIDE), lambda i: (0, 0))
    return pl.pallas_call(
        rows_kernel, grid=(1,), in_specs=specs, out_specs=(whole, whole), out_shape=(out, out)
    )(*args)


def fine_kernel(
    manning, radar, depth, flux, elevation, roughness, building, tiles, first, second, above, below,
    depth_out, flux_out, old_out, to0, to1, to2, to3, ground_out,
    level, flow_x, flow_y, elev, friction, opened,
    sill_x, drag_x, gate_x, sill_y, drag_y, gate_y,
    index_s, rain_s, pooled, coarse,
):
    row_place = lax.axis_index("sx")
    col_place = lax.axis_index("sy")
    time_place = lax.axis_index("tm")
    x_place = (time_place // 2) % 4
    even = col_place % 2 == 0

    def fill(target, index, own):
        target[0:8, :] = jnp.zeros((8, WIDE), F32)
        target[88:96, :] = jnp.zeros((8, WIDE), F32)
        a = first[pl.ds(index * ROWS, ROWS), :]
        b = second[pl.ds(index * ROWS, ROWS), :]
        target[16:80, 0:EDGE] = jnp.where(even, b, a)
        target[16:80, EDGE : EDGE + COLS] = own
        target[16:80, EDGE + COLS : WIDE] = jnp.where(even, a, b)
        target[8:16, :] = above[pl.ds(index * HALO, HALO), :]
        target[80:88, :] = below[pl.ds(index * HALO, HALO), :]

    fill(level, 0, depth[0])
    fill(flow_x, 1, flux[0, 0])
    fill(flow_y, 2, flux[0, 1])
    fill(elev, 3, elevation[...])
    fill(friction, 4, roughness[...].astype(F32))
    fill(opened, 5, building[...].astype(F32))

    lane = lax.broadcasted_iota(jnp.int32, (8, WIDE), 1)
    inside = jnp.where(
        ((col_place == 0) & (lane < EDGE)) | ((col_place == 3) & (lane >= EDGE + COLS)), 0.0, 1.0
    )
    for k in range(12):
        here = pl.ds(8 * k, 8)
        classes = friction[here, :]
        value = jnp.full((8, WIDE), manning[0], F32)
        for entry in range(1, ROUGH_CLASSES):
            value = jnp.where(classes == float(entry), manning[entry], value)
        friction[here, :] = value
        if k in (0, 11):
            opened[here, :] = jnp.zeros((8, WIDE), F32)
            continue
        free = (1.0 - opened[here, :]) * inside
        if k == 1:
            free = free * jnp.where(row_place == 0, 0.0, 1.0)
        if k == 10:
            free = free * jnp.where(row_place == 3, 0.0, 1.0)
        opened[here, :] = free

    for k in range(10):
        rows, after, out = pl.ds(8 + 8 * k, 8), pl.ds(9 + 8 * k, 8), pl.ds(8 * k, 8)
        e, f, o = elev[rows, :], friction[rows, :], opened[rows, :]
        sill_x[out, :] = jnp.maximum(e, elev[after, :])
        rough = 0.5 * (f + friction[after, :])
        drag_x[out, :] = GRAVITY * TIME_STEP * rough * rough
        gate_x[out, :] = o * opened[after, :]
        s, d, g = static_faces(e, f, o, 1, TIME_STEP)
        sill_y[out, :], drag_y[out, :], gate_y[out, :] = s, d, g

    index_s[...] = jnp.full((32, 128), -1, jnp.int32)
    for step in range(FINE_STEPS):
        index_s[4 * step : 4 * step + 4, 0:64] = tiles[0, step]
    index = index_s[...]
    rates = jnp.zeros((32, 128), F32)
    for entry in range(RADAR_TILES):
        rates = jnp.where(index == entry, radar[entry], rates)
    block = lax.broadcasted_iota(jnp.int32, (128, WIDE), 0)
    column = lax.broadcasted_iota(jnp.int32, (128, WIDE), 1) + (COLS * col_place - EDGE)
    rain_s[0:32, :] = TIME_STEP * split_dot(rates, jnp.where((column >> 6) == block, 1.0, 0.0).astype(BF16))
    means = []
    for half in range(COARSE_STEPS):
        part = rates[16 * half : 16 * half + 16, :]
        means.append(0.25 * (part[0:4] + part[4:8] + part[8:12] + part[12:16]))
    coarse_rates = jnp.concatenate(means, axis=0)
    block = lax.broadcasted_iota(jnp.int32, (128, C_WIDE), 0)
    column = lax.broadcasted_iota(jnp.int32, (128, C_WIDE), 1) + (C_COLS * col_place - EDGE // COARSENING)
    padded = jnp.concatenate([coarse_rates, jnp.zeros((8, 128), F32)], axis=0)
    rain_s[32:40, 0:C_WIDE] = split_dot(
        padded, jnp.where((column >> 4) == block, 1.0, 0.0).astype(BF16)
    )[0:8]
    row_above = jnp.maximum(row_place - 1, 0)
    row_below = jnp.minimum(row_place + 1, 3)

    pool = jnp.where(
        lax.broadcasted_iota(jnp.int32, (512, 128), 0) // COARSENING
        == lax.broadcasted_iota(jnp.int32, (512, 128), 1),
        1.0 / 16.0,
        0.0,
    ).astype(BF16)

    def restrict(source, slot):
        values = source if isinstance(source, jax.Array) else source[8:88, :]
        for part in range(3):
            take = values[:, 512 * part : min(512 * part + 512, WIDE)]
            pooled[part, :, :] = split_dot(take, pool[0 : take.shape[1], :])
        for part in range(3):
            cols = slice(128 * part, 128 * part + 128)
            for target, start, count in ((6, 0, 2), (8, 8, 16), (24, 72, 2)):
                total = pooled[part, pl.ds(start, count, stride=4), :]
                for q in range(1, 4):
                    total = total + pooled[part, pl.ds(start + q, count, stride=4), :]
                coarse[slot, target : target + count, cols] = total

    coarse[...] = jnp.zeros(coarse.shape, F32)
    for slot, source in enumerate((level, flow_x, flow_y, elev, friction, opened)):
        restrict(source, slot)

    for k in range(12):
        here = pl.ds(8 * k, 8)
        level[here, :] = level[here, :] + elev[here, :]
    sub = lax.broadcasted_iota(jnp.int32, (8, WIDE), 0)
    pull = GRAVITY * TIME_STEP / CELL_SIDE

    def fine_step(step, carry):
        rains = [rain_s[pl.ds(4 * step + place, 1), :] for place in (row_above, row_place, row_below)]
        now = level[8:16, :]
        up = turn(now, -1, 0)
        west = jnp.zeros((8, WIDE), F32)
        for k in range(10):
            rows, out = pl.ds(8 + 8 * k, 8), pl.ds(8 * k, 8)
            after = level[pl.ds(16 + 8 * k, 8), :]
            up_after = turn(after, -1, 0)
            north = jnp.where(sub == 7, up_after, up)
            qx = face(now, north, flow_x[rows, :], sill_x[out, :], drag_x[out, :], gate_x[out, :], pull)
            qy = face(
                now, turn(now, -1, 1), flow_y[rows, :], sill_y[out, :], drag_y[out, :], gate_y[out, :], pull
            )
            flow_x[rows, :] = qx
            flow_y[rows, :] = qy
            down = turn(qx, 1, 0)
            gain = (jnp.where(sub == 0, west, down) - qx) + (turn(qy, 1, 1) - qy)
            rain = rains[0 if k == 0 else 2 if k == 9 else 1]
            level[rows, :] = now + ((TIME_STEP / CELL_SIDE) * gain + rain)
            now, up, west = after, up_after, down
        return carry

    lax.fori_loop(0, FINE_STEPS, fine_step, 0)

    c_elev, c_friction, c_open = coarse[3], coarse[4], coarse[5]
    faces_x = static_faces(c_elev, c_friction, c_open, 0, COARSE_SECONDS)
    faces_y = static_faces(c_elev, c_friction, c_open, 1, COARSE_SECONDS)
    state = (coarse[0] + c_elev, coarse[1], coarse[2])
    row = lax.broadcasted_iota(jnp.int32, (C_HIGH, C_WIDE), 0)
    for step in range(COARSE_STEPS):
        parts = [rain_s[pl.ds(32 + 4 * step + place, 1), 0:C_WIDE] for place in (row_above, row_place, row_below)]
        rain = jnp.where(row < 8, parts[0], jnp.where(row < 24, parts[1], parts[2]))
        state = whole_step(*state, faces_x, faces_y, rain, COARSE_SIDE, COARSE_SECONDS)
    old = (state[0] - c_elev, state[1], state[2])

    for k in range(10):
        rows = pl.ds(8 + 8 * k, 8)
        level[rows, :] = level[rows, :] - elev[rows, :]
    depth_out[0] = level[16:80, EDGE : EDGE + COLS]
    flux_out[0, 0] = flow_x[16:80, EDGE : EDGE + COLS]
    flux_out[0, 1] = flow_y[16:80, EDGE : EDGE + COLS]
    for slot, source in enumerate((level, flow_x, flow_y)):
        restrict(source, slot)
    factor = jnp.where(time_place == 0, 0.0, 1.0)
    side = EDGE // COARSENING
    outs = (to0, to1, to2, to3)
    for slot in range(3):
        mine = old[slot][8:24, :]
        old_out[C_ROWS * slot : C_ROWS * slot + C_ROWS, :] = turn(mine, -side, 1)[:, 0:C_COLS]
        value = coarse[slot, 8:24, :] - factor * mine
        for d, out in enumerate(outs):
            window = (x_place + d) % 4
            moved = pltpu.roll(value, (C_WIDE - 64 * window) % C_WIDE, 1)
            out[C_ROWS * slot : C_ROWS * slot + C_ROWS, :] = moved[:, 0:128]
        fixed = pltpu.roll(coarse[3 + slot, 8:24, :], (C_WIDE - 64 * x_place) % C_WIDE, 1)
        ground_out[C_ROWS * slot : C_ROWS * slot + C_ROWS, :] = fixed[:, 0:128]
    for out in outs:
        out[3 * C_ROWS : BLOCK, :] = coarse_rates


def fine(manning, radar, depth, flux, elevation, roughness, building, tiles, first, second, above, below):
    smem = pl.BlockSpec(memory_space=pltpu.SMEM)
    vmem = pl.BlockSpec(memory_space=pltpu.VMEM)
    message = jax.ShapeDtypeStruct((BLOCK, 128), F32)
    padded = pltpu.VMEM((HIGH + 16, WIDE), F32)
    faces = pltpu.VMEM((HIGH, WIDE), F32)
    return pl.pallas_call(
        fine_kernel,
        in_specs=[smem, smem] + [vmem] * 10,
        out_specs=[vmem] * 8,
        out_shape=(
            jax.ShapeDtypeStruct(depth.shape, F32),
            jax.ShapeDtypeStruct(flux.shape, F32),
            jax.ShapeDtypeStruct((3 * C_ROWS, C_COLS), F32),
            message,
            message,
            message,
            message,
            jax.ShapeDtypeStruct((3 * C_ROWS, 128), F32),
        ),
        scratch_shapes=[padded] * 6
        + [faces] * 6
        + [
            pltpu.VMEM((32, 128), jnp.int32),
            pltpu.VMEM((40, WIDE), F32),
            pltpu.VMEM((3, HIGH, 128), F32),
            pltpu.VMEM((6, C_HIGH, C_WIDE), F32),
        ],
        compiler_params=pltpu.CompilerParams(vmem_limit_bytes=VMEM_LIMIT),
    )(manning, radar, depth, flux, elevation, roughness, building, tiles, first, second, above, below)


def sweep_kernel(*refs):
    ins, outs = refs[:8], refs[8:12]
    change, rates, rain, ground, newest = refs[12:]
    row_place = lax.axis_index("sx")
    col_place = lax.axis_index("sy")
    time_place = lax.axis_index("tm")
    z_place, x_place, core = time_place // 8, (time_place // 2) % 4, time_place % 2

    for other in range(2):
        for e in range(4):
            ref = ins[4 * other + e]
            start = pl.multiple_of(C_ROWS * ((row_place + 4 - e) % 4), C_ROWS)
            rows = pl.ds(start, C_ROWS)
            for z_rel in range(2):
                for d in range(4):
                    base = (4 * z_rel + d) * BLOCK
                    slice_of = ((z_place + z_rel) % 2) * 8 + ((x_place + 4 - d) % 4) * 2 + (core + other) % 2
                    for field in range(3):
                        change[3 * slice_of + field, rows, :] = ref[
                            base + C_ROWS * field : base + C_ROWS * field + C_ROWS, :
                        ]
                    if e == 0:
                        rates[pl.ds(pl.multiple_of(8 * slice_of, 8), 8), :] = ref[
                            base + 3 * C_ROWS : base + BLOCK, :
                        ]
            if other == 0:
                for field in range(3):
                    base = 8 * BLOCK + C_ROWS * field
                    ground[field, rows, :] = ref[base : base + C_ROWS, :]

    block = lax.broadcasted_iota(jnp.int32, (128, 128), 0)
    column = lax.broadcasted_iota(jnp.int32, (128, 128), 1)
    column = column + (C_COLS * col_place + 64 * x_place - EDGE // COARSENING)
    rain[...] = split_dot(rates[...], jnp.where((column >> 4) == block, 1.0, 0.0).astype(BF16))

    tall = 4 * C_ROWS
    elev = ground[0]
    edge = jnp.where(lax.broadcasted_iota(jnp.int32, (tall, 128), 0) == tall - 1, 0.0, 1.0)
    sill, drag, gate = static_faces(elev, ground[1], ground[2], 0, COARSE_SECONDS)
    faces_x = (sill, drag, gate * edge)
    faces_y = static_faces(elev, ground[1], ground[2], 1, COARSE_SECONDS)
    mine = pl.ds(pl.multiple_of(C_ROWS * row_place, C_ROWS), C_ROWS)

    def one_slice(moment, state):
        for step in range(COARSE_STEPS):
            wet = jnp.concatenate(
                [
                    jnp.broadcast_to(rain[pl.ds(8 * moment + 4 * step + b, 1), :], (C_ROWS, 128))
                    for b in range(4)
                ],
                axis=0,
            )
            state = whole_step(*state, faces_x, faces_y, wet, COARSE_SIDE, COARSE_SECONDS)
        for field in range(3):
            newest[3 * moment + field] = state[field]
        return tuple(state[field] + change[3 * moment + field] for field in range(3))

    lax.fori_loop(1, SLICES, one_slice, (change[0] + elev, change[1], change[2]))
    for d, out in enumerate(outs):
        slice_of = z_place * 8 + ((x_place + d) % 4) * 2 + core
        out[0:C_ROWS, :] = newest[3 * slice_of, mine, :] - ground[0, mine, :]
        out[C_ROWS : 2 * C_ROWS, :] = newest[3 * slice_of + 1, mine, :]
        out[2 * C_ROWS : 3 * C_ROWS, :] = newest[3 * slice_of + 2, mine, :]


def sweep(arrays):
    vmem = pl.BlockSpec(memory_space=pltpu.VMEM)
    out = jax.ShapeDtypeStruct((3 * C_ROWS, 128), F32)
    return pl.pallas_call(
        sweep_kernel,
        in_specs=[vmem] * 8,
        out_specs=[vmem] * 4,
        out_shape=(out,) * 4,
        scratch_shapes=[
            pltpu.VMEM((3 * SLICES, 4 * C_ROWS, 128), F32),
            pltpu.VMEM((8 * SLICES, 128), F32),
            pltpu.VMEM((8 * SLICES, 128), F32),
            pltpu.VMEM((3, 4 * C_ROWS, 128), F32),
            pltpu.VMEM((3 * SLICES, 4 * C_ROWS, 128), F32),
        ],
        compiler_params=pltpu.CompilerParams(vmem_limit_bytes=VMEM_LIMIT),
    )(*arrays)


def finish_kernel(depth, flux, old, new0, new1, new2, new3, depth_out, flux_out, parts, spread):
    time_place = lax.axis_index("tm")
    x_place = (time_place // 2) % 4
    for d, ref in enumerate((new0, new1, new2, new3)):
        parts[(x_place + 4 - d) % 4] = ref[...]
    lane = lax.broadcasted_iota(jnp.int32, (3 * C_ROWS, 128), 1)
    halves = [jnp.where(lane < 64, turn(parts[b], -32, 1), turn(parts[b + 1], 32, 1)) for b in (0, 2)]
    delta = jnp.concatenate(halves, axis=1) - old[...]
    delta = jnp.where(time_place == 0, 0.0, delta)
    copies = jnp.where(
        lax.broadcasted_iota(jnp.int32, (C_COLS, COLS), 0)
        == lax.broadcasted_iota(jnp.int32, (C_COLS, COLS), 1) // COARSENING,
        1.0,
        0.0,
    ).astype(BF16)
    spread[...] = split_dot(delta, copies)
    low = lax.broadcasted_iota(jnp.int32, (8, COLS), 0) < 4
    for field in range(3):
        for k in range(ROWS // 8):
            row = C_ROWS * field + 2 * k
            add = jnp.where(low, spread[row : row + 1, :], spread[row + 1 : row + 2, :])
            rows = slice(8 * k, 8 * k + 8)
            if field == 0:
                depth_out[0, rows, :] = depth[0, rows, :] + add
            else:
                flux_out[0, field - 1, rows, :] = flux[0, field - 1, rows, :] + add


def finish(depth, flux, old, news):
    vmem = pl.BlockSpec(memory_space=pltpu.VMEM)
    return pl.pallas_call(
        finish_kernel,
        in_specs=[vmem] * 7,
        out_specs=[vmem] * 2,
        out_shape=(jax.ShapeDtypeStruct(depth.shape, F32), jax.ShapeDtypeStruct(flux.shape, F32)),
        scratch_shapes=[pltpu.VMEM((4, 3 * C_ROWS, 128), F32), pltpu.VMEM((3 * C_ROWS, COLS), F32)],
        compiler_params=pltpu.CompilerParams(vmem_limit_bytes=VMEM_LIMIT),
    )(depth, flux, old, *news)


def time_route(move):
    route = []
    for source in range(SLICES):
        z, x, core = move(source // 8, (source // 2) % 4, source % 2)
        route.append((source, (z % 2) * 8 + (x % 4) * 2 + core % 2))
    return route


def ring(values, distance):
    return lax.ppermute(values, "sx", [(i, (i + distance) % 4) for i in range(4)])


def over_x(values, distance):
    return lax.ppermute(values, "tm", time_route(lambda z, x, core: (z, x + distance, core)))


def on_device(
    depth_start, flux_start, elevation, roughness_class, building, manning, radar_rates, tile_index
):
    fields = (depth_start, flux_start, elevation, roughness_class, building)
    first, second = pack_columns(*fields)
    first = lax.ppermute(first, "sy", [(0, 1), (1, 0), (2, 3), (3, 2)])
    second = lax.ppermute(second, "sy", [(1, 2), (2, 1)])
    top, bottom = pack_rows(*fields, first, second)
    above = ring(bottom, 1)
    below = ring(top, 3)
    depth, flux, old, own, *away, ground = fine(
        manning, radar_rates, *fields, tile_index, first, second, above, below
    )
    half = jnp.concatenate([own] + [over_x(away[d - 1], d) for d in (1, 2, 3)], axis=0)
    across = lax.ppermute(half, "tm", time_route(lambda z, x, core: (z + 1, x, core)))
    mine = jnp.concatenate([half, across, ground], axis=0)
    column = [mine] + [ring(mine, distance) for distance in (1, 2, 3)]
    sibling = time_route(lambda z, x, core: (z, x, core + 1))
    twins = [lax.ppermute(part, "tm", sibling) for part in column]
    news = sweep(column + twins)
    news = [news[0]] + [over_x(news[d], d) for d in (1, 2, 3)]
    return finish(depth, flux, old, news)


def solution(mesh):
    placed = (
        P("tm", "sx", "sy"),
        P("tm", None, "sx", "sy"),
        P("sx", "sy"),
        P("sx", "sy"),
        P("sx", "sy"),
        P(),
        P(),
        P("tm", None, None, None),
    )
    return jax.shard_map(
        on_device,
        mesh=mesh,
        in_specs=placed,
        out_specs=(P("tm", "sx", "sy"), P("tm", None, "sx", "sy")),
        check_vma=False,
    )
```

time: 1070 us -> 84.3 us (0.08)
  the two profiles are of different devices: /device:TPU:248 before, /device:TPU:32 now
where the time goes in v1:
time: 84.3 us; the launch traced here: 84 us
  waiting for transfers between devices  30.2 us (36%)
  starting transfers between devices  29.1 us (35%)
  Pallas kernels  21.4 us (25%)
  local copies, waits for them, and re-layouts  2.59 us (3%)
    ppermute x5, waiting for transfers between devices, ring(): lax.ppermute(values, 'sx', [(i, (i + distance) % 4) for i in range(4)])  13.5 us
    pallas_call x1, Pallas kernels, fine(): pl.pallas_call(fine_kernel, in_specs=[smem, smem] + [vmem] * 10, out_spec...  10.8 us
    ppermute x6, starting transfers between devices, over_x(): lax.ppermute(values, 'tm', time_route(lambda z, x, core: (z, x + distance...  10.2 us
    ppermute x5, starting transfers between devices, ring(): lax.ppermute(values, 'sx', [(i, (i + distance) % 4) for i in range(4)])  8.03 us
    ppermute x6, waiting for transfers between devices, over_x(): lax.ppermute(values, 'tm', time_route(lambda z, x, core: (z, x + distance...  5.98 us
    pallas_call x1, Pallas kernels, sweep(): pl.pallas_call(sweep_kernel, in_specs=[vmem] * 8, out_specs=[vmem] * 4, o...  5.55 us
    ppermute x1, starting transfers between devices, on_device(): lax.ppermute(half, 'tm', time_route(lambda z, x, core: (z + 1, x, core)))  4.97 us
    ppermute x1, waiting for transfers between devices, on_device(): lax.ppermute(half, 'tm', time_route(lambda z, x, core: (z + 1, x, core)))  4.34 us
  transfers between devices with their start and end apart: 18, of which 13 were waited for; matrix products, arithmetic and copies ran while one was open for 0% of the time, Pallas kernels for 0%

profile of v1, /device:TPU:32, one launch (start us, length us, event | category | flops | bytes accessed | tf_op | source)
XLA Modules:
  0.0 84.0 jit_solution(12932530059768523758)
XLA Ops:
  0.6 1.7 %shard_map.95 = (f32[384,128]{1,0:T(8,128)}, f32[384,128]{1,0:T(8,128)}) custom-call(f32[1,64,1024]{2,1,0:T(8,128)} %depth.1, f32[1,64,1024]{2,1,0:T(8,128)} %depth.1, f32[1,2,64,1024]{3,2,1,0:T(8,128)} %flux.1, f32[1,2,64,1024]{3,2,1,0:T(8,128)} %flux.1, f32[64,1024]{1,0:T(8,128)} %elevation.1, f32[64,1024]{1,0:T(8,128)} %elevation.1, ...), custom_call_target="tpu_custom_call" | custom-call | tf_op jit(solution)/shard_map/pallas_call | solution.py:108
  2.4 1.8 %collective-permute-start = (f32[384,128]{1,0:T(8,128)}, f32[384,128]{1,0:T(8,128)S(1)}, u32[]{:S(2)}, u32[]{:S(2)}) collective-permute-start(f32[384,128]{1,0:T(8,128)} %get-tuple-element.18), channel_id=1, source_target_pairs={{0,1},{1,0},{2,3},{3,2},{4,5},{5,4},{6,7},{7,6},{8,9},{9,8},{10,11... | collective-permute-start | bytes 589832 | tf_op jit(solution)/shard_map/ppermute | solution.py:514
  4.3 4.0 %collective-permute-start.1 = (f32[384,128]{1,0:T(8,128)}, f32[384,128]{1,0:T(8,128)S(1)}, u32[]{:S(2)}, u32[]{:S(2)}) collective-permute-start(f32[384,128]{1,0:T(8,128)} %get-tuple-element.19), channel_id=1, source_target_pairs={{1,2},{2,1},{5,6},{6,5},{9,10},{10,9},{13,14},{14,13},{17,18},{18,... | collective-permute-start | bytes 589832 | tf_op jit(solution)/shard_map/ppermute | solution.py:515
  9.2 3.9 %collective-permute-done.1.refs_11_.second = f32[384,128]{1,0:T(8,128)S(1)} collective-permute-done((f32[384,128]{1,0:T(8,128)}, f32[384,128]{1,0:T(8,128)S(1)}, u32[]{:S(2)}, u32[]{:S(2)}) %collective-permute-start.1) | collective-permute-done | bytes 196640 | tf_op jit(solution)/shard_map/ppermute | solution.py:515
  13.8 2.0 %shard_map.96 = (f32[48,1280]{1,0:T(8,128)}, f32[48,1280]{1,0:T(8,128)}) custom-call(f32[1,64,1024]{2,1,0:T(8,128)} %depth.1, f32[1,64,1024]{2,1,0:T(8,128)} %depth.1, f32[1,2,64,1024]{3,2,1,0:T(8,128)} %flux.1, f32[1,2,64,1024]{3,2,1,0:T(8,128)} %flux.1, f32[64,1024]{1,0:T(8,128)} %elevation.1, f32[64,1024]{1,0:T(8,128)} %elevation.1, ...), custom_call_target="tpu_custom_call" | custom-call | tf_op jit(solution)/shard_map/pallas_call | solution.py:155
  15.8 1.7 %collective-permute-start.2 = (f32[48,1280]{1,0:T(8,128)}, f32[48,1280]{1,0:T(8,128)S(1)}, u32[]{:S(2)}, u32[]{:S(2)}) collective-permute-start(f32[48,1280]{1,0:T(8,128)} %get-tuple-element.20), channel_id=1, source_target_pairs={{0,4},{4,8},{8,12},{12,0},{1,5},{5,9},{9,13},{13,1},{2,6},{6,10},{... | collective-permute-start | bytes 737288 | tf_op jit(solution)/shard_map/ppermute | solution.py:502
  17.5 1.7 %collective-permute-start.3 = (f32[48,1280]{1,0:T(8,128)}, f32[48,1280]{1,0:T(8,128)S(1)}, u32[]{:S(2)}, u32[]{:S(2)}) collective-permute-start(f32[48,1280]{1,0:T(8,128)} %get-tuple-element.21), channel_id=1, source_target_pairs={{0,12},{4,0},{8,4},{12,8},{1,13},{5,1},{9,5},{13,9},{2,14},{6,2},{... | collective-permute-start | bytes 737288 | tf_op jit(solution)/shard_map/ppermute | solution.py:502
  19.2 5.1 %collective-permute-done.2.above = f32[48,1280]{1,0:T(8,128)S(1)} collective-permute-done((f32[48,1280]{1,0:T(8,128)}, f32[48,1280]{1,0:T(8,128)S(1)}, u32[]{:S(2)}, u32[]{:S(2)}) %collective-permute-start.2) | collective-permute-done | bytes 245792 | tf_op jit(solution)/shard_map/ppermute | solution.py:502
  26.2 10.8 %shard_map.97 = (f32[1,64,1024]{2,1,0:T(8,128)S(1)}, f32[1,2,64,1024]{3,2,1,0:T(8,128)S(1)}, f32[48,256]{1,0:T(8,128)S(1)}, f32[56,128]{1,0:T(8,128)S(1)}, f32[5...) custom-call(f32[8]{0:T(128)S(1)} %copy-done.10, f32[64]{0:T(128)S(1)} %copy-done.11, ...), custom_call_target="tpu_custom_call" | custom-call | tf_op jit(solution)/shard_map/pallas_call | solution.py:343
  36.9 1.6 %collective-permute-start.4 = (f32[56,128]{1,0:T(8,128)S(1)}, f32[56,128]{1,0:T(8,128)S(1)}, u32[]{:S(2)}, u32[]{:S(2)}) collective-permute-start(f32[56,128]{1,0:T(8,128)S(1)} %get-tuple-element.26), channel_id=1, source_target_pairs={{0,32},{16,48},{32,64},{48,80},{64,96},{80,112},{96,0},{112,16},{1... | collective-permute-start | bytes 86024 | tf_op jit(solution)/shard_map/ppermute | solution.py:506
  38.5 2.7 %collective-permute-start.5 = (f32[56,128]{1,0:T(8,128)S(1)}, f32[56,128]{1,0:T(8,128)S(1)}, u32[]{:S(2)}, u32[]{:S(2)}) collective-permute-start(f32[56,128]{1,0:T(8,128)S(1)} %get-tuple-element.27), channel_id=1, source_target_pairs={{0,64},{16,80},{32,96},{48,112},{64,0},{80,16},{96,32},{112,48},{1... | collective-permute-start | bytes 86024 | tf_op jit(solution)/shard_map/ppermute | solution.py:506
  41.2 1.4 %collective-permute-start.6 = (f32[56,128]{1,0:T(8,128)S(1)}, f32[56,128]{1,0:T(8,128)S(1)}, u32[]{:S(2)}, u32[]{:S(2)}) collective-permute-start(f32[56,128]{1,0:T(8,128)S(1)} %get-tuple-element.28), channel_id=1, source_target_pairs={{0,96},{16,112},{32,0},{48,16},{64,32},{80,48},{96,64},{112,80},{1... | collective-permute-start | bytes 86024 | tf_op jit(solution)/shard_map/ppermute | solution.py:506
  43.9 1.2 %collective-permute-done.6 = f32[56,128]{1,0:T(8,128)S(1)} collective-permute-done((f32[56,128]{1,0:T(8,128)S(1)}, f32[56,128]{1,0:T(8,128)S(1)}, u32[]{:S(2)}, u32[]{:S(2)}) %collective-permute-start.6) | collective-permute-done | bytes 28704 | tf_op jit(solution)/shard_map/ppermute | solution.py:506
  45.1 5.0 %collective-permute-start.7 = (f32[224,128]{1,0:T(8,128)S(1)}, f32[224,128]{1,0:T(8,128)S(1)}, u32[]{:S(2)}, u32[]{:S(2)}) collective-permute-start(f32[224,128]{1,0:T(8,128)S(1)} %pad_maximum_fusion), channel_id=1, source_target_pairs={{0,128},{16,144},{32,160},{48,176},{64,192},{80,208},{96,224},{112... | collective-permute-start | bytes 344072 | tf_op jit(solution)/shard_map/ppermute | solution.py:523
  50.1 4.3 %collective-permute-done.7 = f32[224,128]{1,0:T(8,128)S(1)} collective-permute-done((f32[224,128]{1,0:T(8,128)S(1)}, f32[224,128]{1,0:T(8,128)S(1)}, u32[]{:S(2)}, u32[]{:S(2)}) %collective-permute-start.7) | collective-permute-done | bytes 114720 | tf_op jit(solution)/shard_map/ppermute | solution.py:523
  54.5 2.6 %collective-permute-start.10 = (f32[496,128]{1,0:T(8,128)S(1)}, f32[496,128]{1,0:T(8,128)S(1)}, u32[]{:S(2)}, u32[]{:S(2)}) collective-permute-start(f32[496,128]{1,0:T(8,128)S(1)} %constant_dynamic-update-slice_fusion.refs_0_), channel_id=1, source_target_pairs={{0,12},{4,0},{8,4},{12,8},{1,13},{5,1},{9,5},{13,9},{2,14},{6,2},{... | collective-permute-start | bytes 761864 | tf_op jit(solution)/shard_map/ppermute | solution.py:502
  57.1 1.4 %collective-permute-start.9 = (f32[496,128]{1,0:T(8,128)S(1)}, f32[496,128]{1,0:T(8,128)S(1)}, u32[]{:S(2)}, u32[]{:S(2)}) collective-permute-start(f32[496,128]{1,0:T(8,128)S(1)} %constant_dynamic-update-slice_fusion.refs_0_), channel_id=1, source_target_pairs={{0,8},{4,12},{8,0},{12,4},{1,9},{5,13},{9,1},{13,5},{2,10},{6,14},... | collective-permute-start | bytes 761864 | tf_op jit(solution)/shard_map/ppermute | solution.py:502
  59.2 4.6 %collective-permute-done.10.refs_3_ = f32[496,128]{1,0:T(8,128)S(1)} collective-permute-done((f32[496,128]{1,0:T(8,128)S(1)}, f32[496,128]{1,0:T(8,128)S(1)}, u32[]{:S(2)}, u32[]{:S(2)}) %collective-permute-start.10) | collective-permute-done | bytes 253984 | tf_op jit(solution)/shard_map/ppermute | solution.py:502
  65.0 2.6 %collective-permute-done.8.refs_1_ = f32[496,128]{1,0:T(8,128)S(1)} collective-permute-done((f32[496,128]{1,0:T(8,128)S(1)}, f32[496,128]{1,0:T(8,128)S(1)}, u32[]{:S(2)}, u32[]{:S(2)}) %collective-permute-start.8) | collective-permute-done | bytes 253984 | tf_op jit(solution)/shard_map/ppermute | solution.py:502
  67.6 1.5 %collective-permute-done.12.refs_5_ = f32[496,128]{1,0:T(8,128)S(1)} collective-permute-done((f32[496,128]{1,0:T(8,128)S(1)}, f32[496,128]{1,0:T(8,128)S(1)}, u32[]{:S(2)}, u32[]{:S(2)}) %collective-permute-start.12) | collective-permute-done | bytes 253984 | tf_op jit(solution)/shard_map/ppermute | solution.py:527
  69.1 5.5 %shard_map.98 = (f32[48,128]{1,0:T(8,128)S(1)}, f32[48,128]{1,0:T(8,128)S(1)}, f32[48,128]{1,0:T(8,128)S(1)}, f32[48,128]{1,0:T(8,128)S(1)}) custom-call(f32[496,128]{1,0:T(8,128)S(1)} %constant_dynamic-update-slice_fusion.refs_0_, f32[496,128]{1,0:T(8,128)S(1)} %collective-permute-done.8.refs_1_, f32[496,128]{1,0:T(8,128)S(1)} %collective-permute-done.9.refs_2_, ...), custom_call_target="tpu_custom_call" | custom-call | tf_op jit(solution)/shard_map/pallas_call | solution.py:437
  75.3 3.6 %collective-permute-start.16 = (f32[48,128]{1,0:T(8,128)S(1)}, f32[48,128]{1,0:T(8,128)S(1)}, u32[]{:S(2)}, u32[]{:S(2)}) collective-permute-start(f32[48,128]{1,0:T(8,128)S(1)} %get-tuple-element.32), channel_id=1, source_target_pairs={{0,64},{16,80},{32,96},{48,112},{64,0},{80,16},{96,32},{112,48},{1... | collective-permute-start | bytes 73736 | tf_op jit(solution)/shard_map/ppermute | solution.py:506
  80.9 1.8 %collective-permute-done.17.new3 = f32[48,128]{1,0:T(8,128)S(1)} collective-permute-done((f32[48,128]{1,0:T(8,128)S(1)}, f32[48,128]{1,0:T(8,128)S(1)}, u32[]{:S(2)}, u32[]{:S(2)}) %collective-permute-start.17) | collective-permute-done | bytes 24608 | tf_op jit(solution)/shard_map/ppermute | solution.py:506
  82.7 1.3 %shard_map.99 = (f32[1,64,1024]{2,1,0:T(8,128)}, f32[1,2,64,1024]{3,2,1,0:T(8,128)}) custom-call(f32[1,64,1024]{2,1,0:T(8,128)S(1)} %get-tuple-element.22.depth, f32[1,2,64,1024]{3,2,1,0:T(8,128)S(1)} %get-tuple-element.23.flux, f32[48,256]{1,0:T(8,128)S(1)} %get-tuple-element.24.old, f32[48,128]{1,0:T(8,128)S(1)} %get-tuple-element.30.new0, ...), custom_call_target="tpu_custom_call" | custom-call | tf_op jit(solution)/shard_map/pallas_call | solution.py:483
  (48 shorter events, 9.3 us)
Async XLA Ops:
  2.4 6.9 %collective-permute-start = (f32[384,128]{1,0:T(8,128)}, f32[384,128]{1,0:T(8,128)S(1)}, u32[]{:S(2)}, u32[]{:S(2)}) collective-permute-start(f32[384,128]{1,0:T(8,128)} %get-tuple-element.18), channel_id=1, source_target_pairs={{0,1},{1,0},{2,3},{3,2},{4,5},{5,4},{6,7},{7,6},{8,9},{9,8},{10,11... | collective-permute-start | bytes 589832 | tf_op jit(solution)/shard_map/ppermute | solution.py:514
  4.2 20.0 %copy-start = (f32[1,2,64,1024]{3,2,1,0:T(8,128)S(1)}, f32[1,2,64,1024]{3,2,1,0:T(8,128)}, u32[]{:S(2)}) copy-start(f32[1,2,64,1024]{3,2,1,0:T(8,128)} %flux.1) | copy-start | bytes 1572868
  4.2 20.0 %copy-start.1 = (f32[1,64,1024]{2,1,0:T(8,128)S(1)}, f32[1,64,1024]{2,1,0:T(8,128)}, u32[]{:S(2)}) copy-start(f32[1,64,1024]{2,1,0:T(8,128)} %depth.1) | copy-start | bytes 786436
  4.2 20.0 %copy-start.2 = (f32[64,1024]{1,0:T(8,128)S(1)}, f32[64,1024]{1,0:T(8,128)}, u32[]{:S(2)}) copy-start(f32[64,1024]{1,0:T(8,128)} %elevation.1) | copy-start | bytes 786436
  4.2 20.0 %copy-start.3 = (s32[64,1024]{1,0:T(8,128)S(1)}, s32[64,1024]{1,0:T(8,128)}, u32[]{:S(2)}) copy-start(s32[64,1024]{1,0:T(8,128)} %roughness.1) | copy-start | bytes 786436
  4.2 20.0 %copy-start.4 = (s32[64,1024]{1,0:T(8,128)S(1)}, s32[64,1024]{1,0:T(8,128)}, u32[]{:S(2)}) copy-start(s32[64,1024]{1,0:T(8,128)} %building.1) | copy-start | bytes 786436
  4.2 20.0 %copy-start.9 = (s32[1,8,4,64]{3,2,1,0:T(4,128)S(1)}, s32[1,8,4,64]{3,2,1,0:T(4,128)}, u32[]{:S(2)}) copy-start(s32[1,8,4,64]{3,2,1,0:T(4,128)} %tiles.1) | copy-start | bytes 24580
  4.3 8.9 %collective-permute-start.1 = (f32[384,128]{1,0:T(8,128)}, f32[384,128]{1,0:T(8,128)S(1)}, u32[]{:S(2)}, u32[]{:S(2)}) collective-permute-start(f32[384,128]{1,0:T(8,128)} %get-tuple-element.19), channel_id=1, source_target_pairs={{1,2},{2,1},{5,6},{6,5},{9,10},{10,9},{13,14},{14,13},{17,18},{18,... | collective-permute-start | bytes 589832 | tf_op jit(solution)/shard_map/ppermute | solution.py:515
  15.8 8.4 %collective-permute-start.2 = (f32[48,1280]{1,0:T(8,128)}, f32[48,1280]{1,0:T(8,128)S(1)}, u32[]{:S(2)}, u32[]{:S(2)}) collective-permute-start(f32[48,1280]{1,0:T(8,128)} %get-tuple-element.20), channel_id=1, source_target_pairs={{0,4},{4,8},{8,12},{12,0},{1,5},{5,9},{9,13},{13,1},{2,6},{6,10},{... | collective-permute-start | bytes 737288 | tf_op jit(solution)/shard_map/ppermute | solution.py:502
  17.5 6.8 %collective-permute-start.3 = (f32[48,1280]{1,0:T(8,128)}, f32[48,1280]{1,0:T(8,128)S(1)}, u32[]{:S(2)}, u32[]{:S(2)}) collective-permute-start(f32[48,1280]{1,0:T(8,128)} %get-tuple-element.21), channel_id=1, source_target_pairs={{0,12},{4,0},{8,4},{12,8},{1,13},{5,1},{9,5},{13,9},{2,14},{6,2},{... | collective-permute-start | bytes 737288 | tf_op jit(solution)/shard_map/ppermute | solution.py:502
  36.9 5.7 %collective-permute-start.4 = (f32[56,128]{1,0:T(8,128)S(1)}, f32[56,128]{1,0:T(8,128)S(1)}, u32[]{:S(2)}, u32[]{:S(2)}) collective-permute-start(f32[56,128]{1,0:T(8,128)S(1)} %get-tuple-element.26), channel_id=1, source_target_pairs={{0,32},{16,48},{32,64},{48,80},{64,96},{80,112},{96,0},{112,16},{1... | collective-permute-start | bytes 86024 | tf_op jit(solution)/shard_map/ppermute | solution.py:506
  38.5 5.4 %collective-permute-start.5 = (f32[56,128]{1,0:T(8,128)S(1)}, f32[56,128]{1,0:T(8,128)S(1)}, u32[]{:S(2)}, u32[]{:S(2)}) collective-permute-start(f32[56,128]{1,0:T(8,128)S(1)} %get-tuple-element.27), channel_id=1, source_target_pairs={{0,64},{16,80},{32,96},{48,112},{64,0},{80,16},{96,32},{112,48},{1... | collective-permute-start | bytes 86024 | tf_op jit(solution)/shard_map/ppermute | solution.py:506
  41.2 3.9 %collective-permute-start.6 = (f32[56,128]{1,0:T(8,128)S(1)}, f32[56,128]{1,0:T(8,128)S(1)}, u32[]{:S(2)}, u32[]{:S(2)}) collective-permute-start(f32[56,128]{1,0:T(8,128)S(1)} %get-tuple-element.28), channel_id=1, source_target_pairs={{0,96},{16,112},{32,0},{48,16},{64,32},{80,48},{96,64},{112,80},{1... | collective-permute-start | bytes 86024 | tf_op jit(solution)/shard_map/ppermute | solution.py:506
  45.1 9.3 %collective-permute-start.7 = (f32[224,128]{1,0:T(8,128)S(1)}, f32[224,128]{1,0:T(8,128)S(1)}, u32[]{:S(2)}, u32[]{:S(2)}) collective-permute-start(f32[224,128]{1,0:T(8,128)S(1)} %pad_maximum_fusion), channel_id=1, source_target_pairs={{0,128},{16,144},{32,160},{48,176},{64,192},{80,208},{96,224},{112... | collective-permute-start | bytes 344072 | tf_op jit(solution)/shard_map/ppermute | solution.py:523
  54.5 9.4 %collective-permute-start.10 = (f32[496,128]{1,0:T(8,128)S(1)}, f32[496,128]{1,0:T(8,128)S(1)}, u32[]{:S(2)}, u32[]{:S(2)}) collective-permute-start(f32[496,128]{1,0:T(8,128)S(1)} %constant_dynamic-update-slice_fusion.refs_0_), channel_id=1, source_target_pairs={{0,12},{4,0},{8,4},{12,8},{1,13},{5,1},{9,5},{13,9},{2,14},{6,2},{... | collective-permute-start | bytes 761864 | tf_op jit(solution)/shard_map/ppermute | solution.py:502
  57.1 7.9 %collective-permute-start.9 = (f32[496,128]{1,0:T(8,128)S(1)}, f32[496,128]{1,0:T(8,128)S(1)}, u32[]{:S(2)}, u32[]{:S(2)}) collective-permute-start(f32[496,128]{1,0:T(8,128)S(1)} %constant_dynamic-update-slice_fusion.refs_0_), channel_id=1, source_target_pairs={{0,8},{4,12},{8,0},{12,4},{1,9},{5,13},{9,1},{13,5},{2,10},{6,14},... | collective-permute-start | bytes 761864 | tf_op jit(solution)/shard_map/ppermute | solution.py:502
  58.5 9.1 %collective-permute-start.8 = (f32[496,128]{1,0:T(8,128)S(1)}, f32[496,128]{1,0:T(8,128)S(1)}, u32[]{:S(2)}, u32[]{:S(2)}) collective-permute-start(f32[496,128]{1,0:T(8,128)S(1)} %constant_dynamic-update-slice_fusion.refs_0_), channel_id=1, source_target_pairs={{0,4},{4,8},{8,12},{12,0},{1,5},{5,9},{9,13},{13,1},{2,6},{6,10},{... | collective-permute-start | bytes 761864 | tf_op jit(solution)/shard_map/ppermute | solution.py:502
  59.2 8.4 %collective-permute-start.11 = (f32[496,128]{1,0:T(8,128)S(1)}, f32[496,128]{1,0:T(8,128)S(1)}, u32[]{:S(2)}, u32[]{:S(2)}) collective-permute-start(f32[496,128]{1,0:T(8,128)S(1)} %constant_dynamic-update-slice_fusion.refs_0_), channel_id=1, source_target_pairs={{0,16},{16,0},{32,48},{48,32},{64,80},{80,64},{96,112},{112,96},{1... | collective-permute-start | bytes 761864 | tf_op jit(solution)/shard_map/ppermute | solution.py:527
  63.8 3.8 %collective-permute-start.14 = (f32[496,128]{1,0:T(8,128)S(1)}, f32[496,128]{1,0:T(8,128)S(1)}, u32[]{:S(2)}, u32[]{:S(2)}) collective-permute-start(f32[496,128]{1,0:T(8,128)S(1)} %collective-permute-done.10.refs_3_), channel_id=1, source_target_pairs={{0,16},{16,0},{32,48},{48,32},{64,80},{80,64},{96,112},{112,96},{1... | collective-permute-start | bytes 761864 | tf_op jit(solution)/shard_map/ppermute | solution.py:527
  65.0 2.6 %collective-permute-start.13 = (f32[496,128]{1,0:T(8,128)S(1)}, f32[496,128]{1,0:T(8,128)S(1)}, u32[]{:S(2)}, u32[]{:S(2)}) collective-permute-start(f32[496,128]{1,0:T(8,128)S(1)} %collective-permute-done.9.refs_2_), channel_id=1, source_target_pairs={{0,16},{16,0},{32,48},{48,32},{64,80},{80,64},{96,112},{112,96},{1... | collective-permute-start | bytes 761864 | tf_op jit(solution)/shard_map/ppermute | solution.py:527
  67.6 1.5 %collective-permute-start.12 = (f32[496,128]{1,0:T(8,128)S(1)}, f32[496,128]{1,0:T(8,128)S(1)}, u32[]{:S(2)}, u32[]{:S(2)}) collective-permute-start(f32[496,128]{1,0:T(8,128)S(1)} %collective-permute-done.8.refs_1_), channel_id=1, source_target_pairs={{0,16},{16,0},{32,48},{48,32},{64,80},{80,64},{96,112},{112,96},{1... | collective-permute-start | bytes 761864 | tf_op jit(solution)/shard_map/ppermute | solution.py:527
  74.7 5.1 %collective-permute-start.15 = (f32[48,128]{1,0:T(8,128)S(1)}, f32[48,128]{1,0:T(8,128)S(1)}, u32[]{:S(2)}, u32[]{:S(2)}) collective-permute-start(f32[48,128]{1,0:T(8,128)S(1)} %get-tuple-element.31), channel_id=1, source_target_pairs={{0,32},{16,48},{32,64},{48,80},{64,96},{80,112},{96,0},{112,16},{1... | collective-permute-start | bytes 73736 | tf_op jit(solution)/shard_map/ppermute | solution.py:506
  75.3 5.7 %collective-permute-start.16 = (f32[48,128]{1,0:T(8,128)S(1)}, f32[48,128]{1,0:T(8,128)S(1)}, u32[]{:S(2)}, u32[]{:S(2)}) collective-permute-start(f32[48,128]{1,0:T(8,128)S(1)} %get-tuple-element.32), channel_id=1, source_target_pairs={{0,64},{16,80},{32,96},{48,112},{64,0},{80,16},{96,32},{112,48},{1... | collective-permute-start | bytes 73736 | tf_op jit(solution)/shard_map/ppermute | solution.py:506
  78.9 3.8 %collective-permute-start.17 = (f32[48,128]{1,0:T(8,128)S(1)}, f32[48,128]{1,0:T(8,128)S(1)}, u32[]{:S(2)}, u32[]{:S(2)}) collective-permute-start(f32[48,128]{1,0:T(8,128)S(1)} %get-tuple-element.33), channel_id=1, source_target_pairs={{0,96},{16,112},{32,0},{48,16},{64,32},{80,48},{96,64},{112,80},{1... | collective-permute-start | bytes 73736 | tf_op jit(solution)/shard_map/ppermute | solution.py:506
  (6 other events, 23.3 us)

commit v2 on v1

v2 whole, which is shorter than its diff:
```python
import math

import jax
import jax.numpy as jnp
from jax import lax
from jax.experimental import pallas as pl
from jax.experimental.pallas import tpu as pltpu
from jax.sharding import PartitionSpec as P

FINE_STEPS = 8
COARSE_STEPS = 2
COARSENING = 4
RAIN_BLOCK = 64
RADAR_TILES = 64
ROUGH_CLASSES = 8
SLICES = 16

GRAVITY = 9.81
DEPTH_FLOOR = 0.05
CELL_SIDE = 2.0
TIME_STEP = 0.25
COARSE_SECONDS = TIME_STEP * FINE_STEPS / COARSE_STEPS
COARSE_SIDE = CELL_SIDE * COARSENING
POWER = -7.0 / 3.0 / math.log(2.0)

COURANT = TIME_STEP / CELL_SIDE
SCALE = COURANT * GRAVITY * TIME_STEP / CELL_SIDE
FLOW_SCALE = SCALE * COURANT
FLOOR = SCALE * DEPTH_FLOOR
FINE_DRAG = GRAVITY * TIME_STEP * SCALE ** (7.0 / 3.0) / FLOW_SCALE
COARSE_DRAG = GRAVITY * COARSE_SECONDS * SCALE ** (7.0 / 3.0) / FLOW_SCALE
CLOSED = 1e30
GROUP = 40

ROWS, COLS = 64, 1024
EDGE = 128
HALO = 8
HIGH, WIDE = ROWS + 2 * HALO, COLS + 2 * EDGE
C_ROWS, C_COLS = ROWS // COARSENING, COLS // COARSENING
C_HIGH, C_WIDE = 32, 384
PART = 3 * C_ROWS // 2
BLOCK = 3 * C_ROWS + 8
F32 = jnp.float32
BF16 = jnp.bfloat16
VMEM_LIMIT = 40 * 1024 * 1024


def face(level, level_next, flux, sill, drag, gate=None):
    raw = jnp.maximum(level, level_next) - sill
    power = jnp.exp2(POWER * jnp.log(jnp.maximum(raw, FLOOR)))
    below = 1.0 + drag * jnp.abs(flux) * power
    inverse = pl.reciprocal(below, approx=True)
    if gate is not None:
        inverse = gate * inverse
    return inverse * (flux - (level_next - level) * jnp.maximum(raw, 0.0))


def split_dot(values, weights, parts=3):
    total = None
    for part in range(parts):
        piece = values.astype(BF16)
        product = jnp.dot(piece, weights, preferred_element_type=F32)
        total = product if total is None else total + product
        if part + 1 < parts:
            values = values - piece.astype(F32)
    return total


def turn(values, shift, axis):
    return pltpu.roll(values, shift % values.shape[axis], axis)


def static_faces(elev, friction, opened, axis, drag):
    sill = jnp.maximum(elev, turn(elev, -1, axis))
    rough = 0.5 * (friction + turn(friction, -1, axis))
    gate = opened * turn(opened, -1, axis)
    return sill, drag * rough * rough, gate


def whole_step(level, flux_x, flux_y, faces_x, faces_y, rain):
    flux_x = face(level, turn(level, -1, 0), flux_x, *faces_x)
    flux_y = face(level, turn(level, -1, 1), flux_y, *faces_y)
    gain = (turn(flux_x, 1, 0) - flux_x) + (turn(flux_y, 1, 1) - flux_y)
    return level + (gain + rain), flux_x, flux_y


def edge_parts(index):
    return (
        (0, HALO, HALO * index),
        (ROWS - HALO, HALO, 6 * HALO + HALO * index),
        (HALO, ROWS - 2 * HALO, 12 * HALO + (ROWS - 2 * HALO) * index),
    )


def pack_kernel(*refs):
    ins, (first, second, row_a, row_b) = refs[:20], refs[20:]
    even = lax.axis_index("sy") % 2 == 0
    even_row = lax.axis_index("sx") % 2 == 0
    index = 0
    for array in range(5):
        left, right, top, bottom = ins[4 * array : 4 * array + 4]
        for lead in (((0,),), ((0, 0), (0, 1)), ((),), ((),), ((),))[array]:
            for row, count, place in edge_parts(index):
                where = lead + (slice(row, row + count), slice(None))
                a, b = left[where].astype(F32), right[where].astype(F32)
                first[place : place + count, :] = jnp.where(even, b, a)
                second[place : place + count, :] = jnp.where(even, a, b)
            here = slice(HALO * index, HALO * index + HALO)
            where = lead + (slice(None), slice(None))
            a, b = top[where].astype(F32), bottom[where].astype(F32)
            row_a[here, :] = jnp.where(even_row, b, a)
            row_b[here, :] = jnp.where(even_row, a, b)
            index += 1


def pack(*fields):
    specs, args = [], []
    for array in fields:
        lead = array.shape[:-2]
        zeros = (0,) * len(lead)
        for shape, place in (
            ((ROWS, EDGE), (0, 0)),
            ((ROWS, EDGE), (0, COLS // EDGE - 1)),
            ((HALO, COLS), (0, 0)),
            ((HALO, COLS), (ROWS // HALO - 1, 0)),
        ):
            specs.append(pl.BlockSpec(lead + shape, lambda i, at=zeros + place: at))
            args.append(array)
    column = jax.ShapeDtypeStruct((6 * ROWS, EDGE), F32)
    row = jax.ShapeDtypeStruct((6 * HALO, COLS), F32)
    return pl.pallas_call(
        pack_kernel,
        grid=(1,),
        in_specs=specs,
        out_specs=[pl.BlockSpec(memory_space=pltpu.VMEM)] * 4,
        out_shape=(column, column, row, row),
    )(*args)


def fine_kernel(
    manning, radar, depth, flux, elevation, roughness, building, tiles, first, second, row_a, row_b, corner_a, corner_b,
    depth_out, flux_out, old_out, to0, to1, to2, to3, ground_out,
    level, flow_x, flow_y, elev, friction, opened,
    sill_x, drag_x, sill_y, drag_y,
    index_s, rain_s, pooled, coarse, ground_s,
):
    row_place = lax.axis_index("sx")
    col_place = lax.axis_index("sy")
    time_place = lax.axis_index("tm")
    x_place, core = (time_place // 2) % 4, time_place % 2
    even = col_place % 2 == 0
    odd_row = row_place % 2 == 1

    def fill(target, index, own, scale=1.0):
        target[0:8, :] = jnp.zeros((8, WIDE), F32)
        target[88:96, :] = jnp.zeros((8, WIDE), F32)
        target[16:80, EDGE : EDGE + COLS] = scale * own
        for row, count, place in edge_parts(index):
            rows, a, b = slice(16 + row, 16 + row + count), first[place : place + count], second[place : place + count]
            target[rows, 0:EDGE] = scale * jnp.where(even, b, a)
            target[rows, EDGE + COLS : WIDE] = scale * jnp.where(even, a, b)
        here = slice(index * HALO, index * HALO + HALO)
        there = slice((6 + index) * HALO, (6 + index) * HALO + HALO)
        for rows, is_first in ((slice(8, 16), odd_row), (slice(80, 88), ~odd_row)):
            target[rows, EDGE : EDGE + COLS] = scale * jnp.where(is_first, row_a[here, :], row_b[here, :])
            a = jnp.where(is_first, corner_a[here, :], corner_b[here, :])
            b = jnp.where(is_first, corner_a[there, :], corner_b[there, :])
            target[rows, 0:EDGE] = scale * jnp.where(even, b, a)
            target[rows, EDGE + COLS : WIDE] = scale * jnp.where(even, a, b)

    fill(level, 0, depth[0], SCALE)
    fill(flow_x, 1, flux[0, 0], FLOW_SCALE)
    fill(flow_y, 2, flux[0, 1], FLOW_SCALE)
    fill(elev, 3, elevation[...], SCALE)
    fill(friction, 4, roughness[...].astype(F32))
    fill(opened, 5, building[...].astype(F32))

    lane = lax.broadcasted_iota(jnp.int32, (8, WIDE), 1)
    inside = jnp.where(
        ((col_place == 0) & (lane < EDGE)) | ((col_place == 3) & (lane >= EDGE + COLS)), 0.0, 1.0
    )
    for k in range(12):
        here = pl.ds(8 * k, 8)
        classes = friction[here, :]
        value = jnp.full((8, WIDE), manning[0], F32)
        for entry in range(1, ROUGH_CLASSES):
            value = jnp.where(classes == float(entry), manning[entry], value)
        friction[here, :] = value
        if k in (0, 11):
            opened[here, :] = jnp.zeros((8, WIDE), F32)
            continue
        free = (1.0 - opened[here, :]) * inside
        if k == 1:
            free = free * jnp.where(row_place == 0, 0.0, 1.0)
        if k == 10:
            free = free * jnp.where(row_place == 3, 0.0, 1.0)
        opened[here, :] = free

    index_s[...] = jnp.full((32, 128), -1, jnp.int32)
    for step in range(FINE_STEPS):
        index_s[4 * step : 4 * step + 4, 0:64] = tiles[0, step]
    index = index_s[...]
    rates = jnp.zeros((32, 128), F32)
    for entry in range(RADAR_TILES):
        rates = jnp.where(index == entry, radar[entry], rates)
    block = lax.broadcasted_iota(jnp.int32, (128, WIDE), 0)
    column = lax.broadcasted_iota(jnp.int32, (128, WIDE), 1) + (COLS * col_place - EDGE)
    rain_s[0:32, :] = (SCALE * TIME_STEP) * split_dot(rates, jnp.where((column >> 6) == block, 1.0, 0.0).astype(BF16))
    means = []
    for half in range(COARSE_STEPS):
        part = rates[16 * half : 16 * half + 16, :]
        means.append((0.25 * SCALE * COARSE_SECONDS) * (part[0:4] + part[4:8] + part[8:12] + part[12:16]))
    coarse_rates = jnp.concatenate(means, axis=0)
    block = lax.broadcasted_iota(jnp.int32, (128, C_WIDE), 0)
    column = lax.broadcasted_iota(jnp.int32, (128, C_WIDE), 1) + (C_COLS * col_place - EDGE // COARSENING)
    padded = jnp.concatenate([coarse_rates, jnp.zeros((8, 128), F32)], axis=0)
    rain_s[32:40, 0:C_WIDE] = split_dot(
        padded, jnp.where((column >> 4) == block, 1.0, 0.0).astype(BF16)
    )[0:8]
    row_above = jnp.maximum(row_place - 1, 0)
    row_below = jnp.minimum(row_place + 1, 3)

    pool = jnp.where(
        lax.broadcasted_iota(jnp.int32, (512, 128), 0) // COARSENING
        == lax.broadcasted_iota(jnp.int32, (512, 128), 1),
        1.0 / 16.0,
        0.0,
    ).astype(BF16)

    def restrict(source, slot):
        for part in range(3):
            take = source[8:88, 512 * part : min(512 * part + 512, WIDE)]
            pooled[part, :, :] = split_dot(take, pool[0 : take.shape[1], :], 1 if slot == 5 else 2)
        for part in range(3):
            cols = slice(128 * part, 128 * part + 128)
            for target, start, count in ((6, 0, 2), (8, 8, 16), (24, 72, 2)):
                total = pooled[part, pl.ds(start, count, stride=4), :]
                for q in range(1, 4):
                    total = total + pooled[part, pl.ds(start + q, count, stride=4), :]
                coarse[slot, target : target + count, cols] = total

    coarse[...] = jnp.zeros(coarse.shape, F32)
    for slot, source in enumerate((level, flow_x, flow_y, elev, friction, opened)):
        restrict(source, slot)

    for k in range(10):
        rows, after, out = pl.ds(8 + 8 * k, 8), pl.ds(9 + 8 * k, 8), pl.ds(8 * k, 8)
        e, f, o = elev[rows, :], friction[rows, :], opened[rows, :]
        gate = o * opened[after, :]
        sill_x[out, :] = jnp.where(gate > 0.0, jnp.maximum(e, elev[after, :]), CLOSED)
        flow_x[rows, :] = gate * flow_x[rows, :]
        rough = 0.5 * (f + friction[after, :])
        drag_x[out, :] = FINE_DRAG * rough * rough
        sill, drag_y[out, :], gate = static_faces(e, f, o, 1, FINE_DRAG)
        sill_y[out, :] = jnp.where(gate > 0.0, sill, CLOSED)
        flow_y[rows, :] = gate * flow_y[rows, :]

    for k in range(12):
        here = pl.ds(8 * k, 8)
        level[here, :] = level[here, :] + elev[here, :]
    sub = lax.broadcasted_iota(jnp.int32, (GROUP, WIDE), 0)

    def fine_step(step, carry):
        rains = [rain_s[pl.ds(4 * step + place, 1), :] for place in (row_above, row_place, row_below)]
        now = level[8 : 8 + GROUP, :]
        up = turn(now, -1, 0)
        west = now
        for k in range(HIGH // GROUP):
            out = slice(GROUP * k, GROUP * k + GROUP)
            rows = slice(8 + GROUP * k, 8 + GROUP * k + GROUP)
            if k + 1 < HIGH // GROUP:
                after = level[8 + GROUP * k + GROUP : 8 + 2 * GROUP + GROUP * k, :]
                up_after = turn(after, -1, 0)
            north = jnp.where(sub == GROUP - 1, up_after, up)
            qx = face(now, north, flow_x[rows, :], sill_x[out, :], drag_x[out, :])
            qy = face(now, turn(now, -1, 1), flow_y[rows, :], sill_y[out, :], drag_y[out, :])
            flow_x[rows, :] = qx
            flow_y[rows, :] = qy
            down = turn(qx, 1, 0)
            gain = (jnp.where(sub == 0, west, down) - qx) + (turn(qy, 1, 1) - qy)
            rain = rains[1]
            if k == 0:
                rain = jnp.where(sub < HALO, rains[0], rain)
            if k + 1 == HIGH // GROUP:
                rain = jnp.where(sub >= GROUP - HALO, rains[2], rain)
            level[rows, :] = now + (gain + rain)
            now, up, west = after, up_after, down
        return carry

    lax.fori_loop(0, FINE_STEPS, fine_step, 0)

    c_elev, c_friction, c_open = coarse[3], coarse[4], coarse[5]
    faces_x = static_faces(c_elev, c_friction, c_open, 0, COARSE_DRAG)
    faces_y = static_faces(c_elev, c_friction, c_open, 1, COARSE_DRAG)
    state = (coarse[0] + c_elev, coarse[1], coarse[2])
    row = lax.broadcasted_iota(jnp.int32, (C_HIGH, C_WIDE), 0)
    for step in range(COARSE_STEPS):
        parts = [rain_s[pl.ds(32 + 4 * step + place, 1), 0:C_WIDE] for place in (row_above, row_place, row_below)]
        rain = jnp.where(row < 8, parts[0], jnp.where(row < 24, parts[1], parts[2]))
        state = whole_step(*state, faces_x, faces_y, rain)
    old = (state[0] - c_elev, state[1], state[2])

    for k in range(10):
        rows = pl.ds(8 + 8 * k, 8)
        level[rows, :] = level[rows, :] - elev[rows, :]
    own = (slice(16, 80), slice(EDGE, EDGE + COLS))
    depth_out[0] = (1.0 / SCALE) * level[own]
    flux_out[0, 0] = (1.0 / FLOW_SCALE) * flow_x[own]
    flux_out[0, 1] = (1.0 / FLOW_SCALE) * flow_y[own]
    for slot, source in enumerate((level, flow_x, flow_y)):
        restrict(source, slot)
    factor = jnp.where(time_place == 0, 0.0, 1.0)
    side = EDGE // COARSENING
    outs = (to0, to1, to2, to3)
    for slot in range(3):
        mine = old[slot][8:24, :]
        old_out[C_ROWS * slot : C_ROWS * slot + C_ROWS, :] = turn(mine, -side, 1)[:, 0:C_COLS]
        value = coarse[slot, 8:24, :] - factor * mine
        for d, out in enumerate(outs):
            window = (x_place + d) % 4
            moved = pltpu.roll(value, (C_WIDE - 64 * window) % C_WIDE, 1)
            out[C_ROWS * slot : C_ROWS * slot + C_ROWS, :] = moved[:, 0:128]
        fixed = pltpu.roll(coarse[3 + slot, 8:24, :], (C_WIDE - 64 * x_place) % C_WIDE, 1)
        ground_s[C_ROWS * slot : C_ROWS * slot + C_ROWS, :] = fixed[:, 0:128]
    ground_out[...] = ground_s[pl.ds(pl.multiple_of(core * PART, PART), PART), :]
    for out in outs:
        out[3 * C_ROWS : BLOCK, :] = coarse_rates


def fine(manning, radar, depth, flux, *rest):
    smem = pl.BlockSpec(memory_space=pltpu.SMEM)
    vmem = pl.BlockSpec(memory_space=pltpu.VMEM)
    message = jax.ShapeDtypeStruct((BLOCK, 128), F32)
    padded = pltpu.VMEM((HIGH + 16, WIDE), F32)
    faces = pltpu.VMEM((HIGH, WIDE), F32)
    return pl.pallas_call(
        fine_kernel,
        in_specs=[smem, smem] + [vmem] * 12,
        out_specs=[vmem] * 8,
        out_shape=(
            jax.ShapeDtypeStruct(depth.shape, F32),
            jax.ShapeDtypeStruct(flux.shape, F32),
            jax.ShapeDtypeStruct((3 * C_ROWS, C_COLS), F32),
            message,
            message,
            message,
            message,
            jax.ShapeDtypeStruct((PART, 128), F32),
        ),
        scratch_shapes=[padded] * 6
        + [faces] * 4
        + [
            pltpu.VMEM((32, 128), jnp.int32),
            pltpu.VMEM((40, WIDE), F32),
            pltpu.VMEM((3, HIGH, 128), F32),
            pltpu.VMEM((6, C_HIGH, C_WIDE), F32),
            pltpu.VMEM((3 * C_ROWS, 128), F32),
        ],
        compiler_params=pltpu.CompilerParams(vmem_limit_bytes=VMEM_LIMIT),
    )(manning, radar, depth, flux, *rest)


HALF = SLICES // 2
TALL = 4 * C_ROWS
NEAR = 3 * C_ROWS
FIELDS = 3 * C_ROWS


def sweep_faces(ground):
    sill, drag, gate = static_faces(*ground, 0, COARSE_DRAG)
    last = lax.broadcasted_iota(jnp.int32, gate.shape, 0) == gate.shape[0] - 1
    gate = jnp.where(last, 0.0, gate)
    return (sill, drag, gate), static_faces(*ground, 1, COARSE_DRAG)


def near_start(row_place):
    return pl.multiple_of(C_ROWS * jnp.clip(row_place - 1, 0, 1), C_ROWS)


def sweep_slices(start, state, change, rain, ground, newest, top, high):
    faces_x, faces_y = sweep_faces(ground)
    rows = pl.ds(top, high)

    def one_slice(moment, state):
        for step in range(COARSE_STEPS):
            wet = jnp.concatenate(
                [
                    jnp.broadcast_to(
                        rain[pl.ds(8 * moment + 4 * step + top // C_ROWS + b, 1), :], (C_ROWS, 128)
                    )
                    for b in range(high // C_ROWS)
                ],
                axis=0,
            )
            state = whole_step(*state, faces_x, faces_y, wet)
        for field in range(3):
            newest[3 * moment + field, 0:high, :] = state[field]
        return tuple(state[field] + change[3 * moment + field, rows, :] for field in range(3))

    return lax.fori_loop(start, HALF, one_slice, state)


def first_kernel(*refs):
    ins, (change, rain, ground, newest, halfway), (rates, state_s, all_s, parts_s) = refs[:8], refs[8:13], refs[13:]
    row_place = lax.axis_index("sx")
    col_place = lax.axis_index("sy")
    time_place = lax.axis_index("tm")
    z_place, x_place, core = time_place // 8, (time_place // 2) % 4, time_place % 2

    for other in range(2):
        for e in range(4):
            ref = ins[4 * other + e]
            source = (row_place, row_place + 1 - 2 * (row_place % 2), 3 - row_place, (row_place + 2) % 4)[e]
            start = pl.multiple_of(C_ROWS * source, C_ROWS)
            rows = pl.ds(start, C_ROWS)
            for d in range(4):
                slice_of = ((x_place + 4 - d) % 4) * 2 + (core + other) % 2
                for field in range(3):
                    base = FIELDS * d + C_ROWS * field
                    change[3 * slice_of + field, rows, :] = ref[base : base + C_ROWS, :]
                if e == 0:
                    base = 4 * FIELDS + PART + 8 * d
                    rates[pl.ds(pl.multiple_of(8 * slice_of, 8), 8), :] = ref[base : base + 8, :]
            half = (core + other) % 2
            base = 4 * FIELDS
            parts_s[pl.ds(pl.multiple_of(half * PART, PART), PART), :] = ref[base : base + PART, :]
            if other == 1:
                twin = ins[e]
                parts_s[pl.ds(pl.multiple_of(core * PART, PART), PART), :] = twin[base : base + PART, :]
                for field in range(3):
                    ground[field, rows, :] = parts_s[C_ROWS * field : C_ROWS * field + C_ROWS, :]

    block = lax.broadcasted_iota(jnp.int32, (128, 128), 0)
    column = lax.broadcasted_iota(jnp.int32, (128, 128), 1)
    column = column + (C_COLS * col_place + 64 * x_place - EDGE // COARSENING)
    rain[...] = split_dot(rates[...], jnp.where((column >> 4) == block, 1.0, 0.0).astype(BF16))

    start = jnp.where(z_place == 0, 1, HALF)
    fixed = (ground[0], ground[1], ground[2])
    state = (change[0] + ground[0], change[1], change[2])
    state = sweep_slices(start, state, change, rain, fixed, newest, 0, TALL)
    near = pl.ds(near_start(row_place), NEAR)
    for field in range(3):
        all_s[field] = state[field]
        state_s[NEAR * field : NEAR * field + NEAR, :] = all_s[field, near, :]
    count = 3 * NEAR // 2
    halfway[...] = state_s[pl.ds(pl.multiple_of(core * count, count), count), :]


def first_sweep(arrays):
    vmem = pl.BlockSpec(memory_space=pltpu.VMEM)
    field = jax.ShapeDtypeStruct((3 * HALF, TALL, 128), F32)
    return pl.pallas_call(
        first_kernel,
        in_specs=[vmem] * 8,
        out_specs=[vmem] * 5,
        out_shape=(
            field,
            jax.ShapeDtypeStruct((8 * HALF, 128), F32),
            jax.ShapeDtypeStruct((3, TALL, 128), F32),
            field,
            jax.ShapeDtypeStruct((3 * NEAR // 2, 128), F32),
        ),
        scratch_shapes=[
            pltpu.VMEM((8 * HALF, 128), F32),
            pltpu.VMEM((3 * NEAR, 128), F32),
            pltpu.VMEM((3, TALL, 128), F32),
            pltpu.VMEM((3 * C_ROWS, 128), F32),
        ],
        compiler_params=pltpu.CompilerParams(vmem_limit_bytes=VMEM_LIMIT),
    )(*arrays)


def second_kernel(change, rain, ground, early, mine, twin, out0, out1, out2, out3, late, state_s):
    row_place = lax.axis_index("sx")
    time_place = lax.axis_index("tm")
    z_place, x_place, core = time_place // 8, (time_place // 2) % 4, time_place % 2
    count = 3 * NEAR // 2
    state_s[pl.ds(pl.multiple_of(core * count, count), count), :] = mine[...]
    state_s[pl.ds(pl.multiple_of((1 - core) * count, count), count), :] = twin[...]
    state = tuple(state_s[NEAR * field : NEAR * field + NEAR, :] for field in range(3))
    start = jnp.where(z_place == 0, HALF, 0)
    top = near_start(row_place)
    fixed = tuple(ground[field, pl.ds(top, NEAR), :] for field in range(3))
    sweep_slices(start, state, change, rain, fixed, late, top, NEAR)
    rows = pl.ds(pl.multiple_of(C_ROWS * row_place, C_ROWS), C_ROWS)
    late_rows = pl.ds(pl.multiple_of(C_ROWS * row_place - top, C_ROWS), C_ROWS)
    for d, out in enumerate((out0, out1, out2, out3)):
        slice_of = ((x_place + d) % 4) * 2 + core
        for field in range(3):
            here = 3 * slice_of + field
            value = jnp.where(z_place == 0, early[here, rows, :], late[here, late_rows, :])
            if field == 0:
                value = value - ground[0, rows, :]
            out[C_ROWS * field : C_ROWS * field + C_ROWS, :] = value


def second_sweep(change, rain, ground, early, mine, twin):
    vmem = pl.BlockSpec(memory_space=pltpu.VMEM)
    out = jax.ShapeDtypeStruct((FIELDS, 128), F32)
    return pl.pallas_call(
        second_kernel,
        in_specs=[vmem] * 6,
        out_specs=[vmem] * 4,
        out_shape=(out,) * 4,
        scratch_shapes=[pltpu.VMEM((3 * HALF, NEAR, 128), F32), pltpu.VMEM((3 * NEAR, 128), F32)],
        compiler_params=pltpu.CompilerParams(vmem_limit_bytes=VMEM_LIMIT),
    )(change, rain, ground, early, mine, twin)


def finish_kernel(depth, flux, old, new0, new1, new2, new3, depth_out, flux_out, parts, spread):
    time_place = lax.axis_index("tm")
    x_place = (time_place // 2) % 4
    for d, ref in enumerate((new0, new1, new2, new3)):
        parts[(x_place + 4 - d) % 4] = ref[...]
    lane = lax.broadcasted_iota(jnp.int32, (3 * C_ROWS, 128), 1)
    halves = [jnp.where(lane < 64, turn(parts[b], -32, 1), turn(parts[b + 1], 32, 1)) for b in (0, 2)]
    delta = jnp.concatenate(halves, axis=1) - old[...]
    delta = jnp.where(time_place == 0, 0.0, delta)
    copies = jnp.where(
        lax.broadcasted_iota(jnp.int32, (C_COLS, COLS), 0)
        == lax.broadcasted_iota(jnp.int32, (C_COLS, COLS), 1) // COARSENING,
        1.0,
        0.0,
    ).astype(BF16)
    scale = jnp.where(
        lax.broadcasted_iota(jnp.int32, (3 * C_ROWS, C_COLS), 0) < C_ROWS, 1.0 / SCALE, 1.0 / FLOW_SCALE
    )
    spread[...] = split_dot(scale * delta, copies)
    low = lax.broadcasted_iota(jnp.int32, (8, COLS), 0) < 4
    for field in range(3):
        for k in range(ROWS // 8):
            row = C_ROWS * field + 2 * k
            add = jnp.where(low, spread[row : row + 1, :], spread[row + 1 : row + 2, :])
            rows = slice(8 * k, 8 * k + 8)
            if field == 0:
                depth_out[0, rows, :] = depth[0, rows, :] + add
            else:
                flux_out[0, field - 1, rows, :] = flux[0, field - 1, rows, :] + add


def finish(depth, flux, old, news):
    vmem = pl.BlockSpec(memory_space=pltpu.VMEM)
    return pl.pallas_call(
        finish_kernel,
        in_specs=[vmem] * 7,
        out_specs=[vmem] * 2,
        out_shape=(jax.ShapeDtypeStruct(depth.shape, F32), jax.ShapeDtypeStruct(flux.shape, F32)),
        scratch_shapes=[pltpu.VMEM((4, 3 * C_ROWS, 128), F32), pltpu.VMEM((3 * C_ROWS, COLS), F32)],
        compiler_params=pltpu.CompilerParams(vmem_limit_bytes=VMEM_LIMIT),
    )(depth, flux, old, *news)


def time_route(move):
    route = []
    for source in range(SLICES):
        z, x, core = move(source // 8, (source // 2) % 4, source % 2)
        route.append((source, (z % 2) * 8 + (x % 4) * 2 + core % 2))
    return route


def with_row(values, flip):
    return lax.ppermute(values, "sx", [(i, i ^ flip) for i in range(4)])


def over_x(values, distance):
    return lax.ppermute(values, "tm", time_route(lambda z, x, core: (z, x + distance, core)))


def on_device(
    depth_start, flux_start, elevation, roughness_class, building, manning, radar_rates, tile_index
):
    fields = (depth_start, flux_start, elevation, roughness_class, building)
    first, second, row_a, row_b = pack(*fields)
    first = lax.ppermute(first, "sy", [(0, 1), (1, 0), (2, 3), (3, 2)])
    second = lax.ppermute(second, "sy", [(1, 2), (2, 1)])
    row_a, row_b = with_row(row_a, 1), with_row(row_b, 3)
    size = 6 * HALO
    tops = jnp.concatenate([first[:size], second[:size]], axis=0)
    bottoms = jnp.concatenate([first[size : 2 * size], second[size : 2 * size]], axis=0)
    even_row = lax.axis_index("sx") % 2 == 0
    corner_a = with_row(jnp.where(even_row, bottoms, tops), 1)
    corner_b = with_row(jnp.where(even_row, tops, bottoms), 3)
    depth, flux, old, own, *away, ground = fine(
        manning, radar_rates, *fields, tile_index, first, second, row_a, row_b, corner_a, corner_b
    )
    parts = [own] + [over_x(away[d - 1], d) for d in (1, 2, 3)]
    column = jnp.concatenate([part[:FIELDS] for part in parts] + [ground], axis=0)
    mine = jnp.concatenate([column] + [part[FIELDS:] for part in parts], axis=0)
    sibling = time_route(lambda z, x, core: (z, x, core + 1))
    arrays = [mine] + [with_row(column, flip) for flip in (1, 3, 2)]
    arrays = arrays + [lax.ppermute(part, "tm", sibling) for part in arrays]
    change, rain, ground, early, halfway = first_sweep(arrays)
    halfway = lax.ppermute(halfway, "tm", time_route(lambda z, x, core: (z + 1, x, core)))
    twin = lax.ppermute(halfway, "tm", sibling)
    news = second_sweep(change, rain, ground, early, halfway, twin)
    news = [news[0]] + [over_x(news[d], d) for d in (1, 2, 3)]
    return finish(depth, flux, old, news)


def solution(mesh):
    placed = (
        P("tm", "sx", "sy"),
        P("tm", None, "sx", "sy"),
        P("sx", "sy"),
        P("sx", "sy"),
        P("sx", "sy"),
        P(),
        P(),
        P("tm", None, None, None),
    )
    return jax.shard_map(
        on_device,
        mesh=mesh,
        in_specs=placed,
        out_specs=(P("tm", "sx", "sy"), P("tm", None, "sx", "sy")),
        check_vma=False,
    )
```

time: 84.3 us -> 68.2 us (0.81)
  waiting for transfers between devices: 30.2 us -> 22.3 us
  Pallas kernels: 21.4 us -> 15 us
  local copies, waits for them, and re-layouts: 2.59 us -> 0.07 us
    pallas_call x4, Pallas kernels: 20.1 us -> 13.7 us  [the longest x1 8.8 us: fine(): pl.pallas_call(fine_kernel, in_specs=[smem, smem] + [vmem] * 12, out_spec...]
    ppermute x10 -> x13, waiting for transfers between devices: 19.4 us -> 15.2 us  [the longest x7 7.9 us: with_row(): return lax.ppermute(values, 'sx', [(i, i ^ flip) for i in range(4)])]
    ppermute x1, waiting for transfers between devices: 3.88 us -> 0.96 us  [on_device(): second = lax.ppermute(second, 'sy', [(1, 2), (2, 1)])]
    unnamed x29 -> x23, local copies, waits for them, and re-layouts: 2.59 us -> 0.06 us
    ppermute x10 -> x13, starting transfers between devices: 13 us -> 14 us  [the longest x7 10.7 us: with_row(): return lax.ppermute(values, 'sx', [(i, i ^ flip) for i in range(4)])]
    ppermute x1, waiting for transfers between devices: 0.93 us -> 0.01 us  [on_device(): first = lax.ppermute(first, 'sy', [(0, 1), (1, 0), (2, 3), (3, 2)])]
  transfers between devices with their start and end apart: 18 -> 21, of which waited for: 13 -> 16; matrix products, arithmetic and copies ran while one was open for 0% -> 0% of each run, Pallas kernels for 0% -> 0%
where the time goes in v2:
time: 68.2 us; the launch traced here: 68 us
  starting transfers between devices  29.8 us (44%)
  waiting for transfers between devices  22.3 us (33%)
  Pallas kernels  15 us (22%)
  between operations  0.8 us (1%)
    ppermute x7, starting transfers between devices, with_row(): return lax.ppermute(values, 'sx', [(i, i ^ flip) for i in range(4)])  10.7 us
    ppermute x6, starting transfers between devices, over_x(): lax.ppermute(values, 'tm', time_route(lambda z, x, core: (z, x + distance...  9.97 us
    pallas_call x1, Pallas kernels, fine(): pl.pallas_call(fine_kernel, in_specs=[smem, smem] + [vmem] * 12, out_spec...  8.8 us
    ppermute x7, waiting for transfers between devices, with_row(): return lax.ppermute(values, 'sx', [(i, i ^ flip) for i in range(4)])  7.9 us
    ppermute x6, waiting for transfers between devices, over_x(): lax.ppermute(values, 'tm', time_route(lambda z, x, core: (z, x + distance...  6.19 us
    ppermute x1, waiting for transfers between devices, on_device(): lax.ppermute(halfway, 'tm', time_route(lambda z, x, core: (z + 1, x, core)))  5.08 us
    ppermute x1, starting transfers between devices, on_device(): second = lax.ppermute(second, 'sy', [(1, 2), (2, 1)])  3.89 us
    ppermute x1, starting transfers between devices, on_device(): lax.ppermute(halfway, 'tm', time_route(lambda z, x, core: (z + 1, x, core)))  2.87 us
  transfers between devices with their start and end apart: 21, of which 16 were waited for; matrix products, arithmetic and copies ran while one was open for 0% of the time, Pallas kernels for 0%

profile of v2, /device:TPU:32, one launch (start us, length us, event | category | flops | bytes accessed | tf_op | source)
XLA Modules:
  0.0 68.0 jit_solution(9109098494014914672)
XLA Ops:
  0.7 2.1 %shard_map.95 = (f32[384,128]{1,0:T(8,128)}, f32[384,128]{1,0:T(8,128)}, f32[48,1024]{1,0:T(8,128)}, f32[48,1024]{1,0:T(8,128)}) custom-call(f32[1,64,1024]{2,1,0:T(8,128)} %depth.1, f32[1,64,1024]{2,1,0:T(8,128)} %depth.1, f32[1,64,1024]{2,1,0:T(8,128)} %depth.1, f32[1,64,1024]{2,1,0:T(8,128)} %depth.1, f32[1,2,64,1024]{3,2,1,0:T(8,128)} %flux.1, ...), custom_call_target="tpu_custom_call" | custom-call | tf_op jit(solution)/shard_map/pallas_call | solution.py:131
  2.8 1.9 %collective-permute-start = (f32[384,128]{1,0:T(8,128)}, f32[384,128]{1,0:T(8,128)S(1)}, u32[]{:S(2)}, u32[]{:S(2)}) collective-permute-start(f32[384,128]{1,0:T(8,128)} %get-tuple-element.23), channel_id=1, source_target_pairs={{0,1},{1,0},{2,3},{3,2},{4,5},{5,4},{6,7},{7,6},{8,9},{9,8},{10,11... | collective-permute-start | bytes 589832 | tf_op jit(solution)/shard_map/ppermute | solution.py:575
  4.7 3.9 %collective-permute-start.1 = (f32[384,128]{1,0:T(8,128)}, f32[384,128]{1,0:T(8,128)S(1)}, u32[]{:S(2)}, u32[]{:S(2)}) collective-permute-start(f32[384,128]{1,0:T(8,128)} %get-tuple-element.24), channel_id=1, source_target_pairs={{1,2},{2,1},{5,6},{6,5},{9,10},{10,9},{13,14},{14,13},{17,18},{18,... | collective-permute-start | bytes 589832 | tf_op jit(solution)/shard_map/ppermute | solution.py:576
  8.6 1.7 %collective-permute-start.2 = (f32[48,1024]{1,0:T(8,128)}, f32[48,1024]{1,0:T(8,128)S(1)}, u32[]{:S(2)}, u32[]{:S(2)}) collective-permute-start(f32[48,1024]{1,0:T(8,128)} %get-tuple-element.25), channel_id=1, source_target_pairs={{0,4},{4,0},{8,12},{12,8},{1,5},{5,1},{9,13},{13,9},{2,6},{6,2},{1... | collective-permute-start | bytes 589832 | tf_op jit(solution)/shard_map/ppermute | solution.py:563
  10.3 2.2 %collective-permute-start.3 = (f32[48,1024]{1,0:T(8,128)}, f32[48,1024]{1,0:T(8,128)S(1)}, u32[]{:S(2)}, u32[]{:S(2)}) collective-permute-start(f32[48,1024]{1,0:T(8,128)} %get-tuple-element.26), channel_id=1, source_target_pairs={{0,12},{4,8},{8,4},{12,0},{1,13},{5,9},{9,5},{13,1},{2,14},{6,10},... | collective-permute-start | bytes 589832 | tf_op jit(solution)/shard_map/ppermute | solution.py:563
  13.5 3.1 %collective-permute-start.5 = (f32[96,128]{1,0:T(8,128)S(1)}, f32[96,128]{1,0:T(8,128)S(1)}, u32[]{:S(2)}, u32[]{:S(2)}) collective-permute-start(f32[96,128]{1,0:T(8,128)S(1)} %get-tuple-element.48), channel_id=1, source_target_pairs={{0,12},{4,8},{8,4},{12,0},{1,13},{5,9},{9,5},{13,1},{2,14},{6,10},... | collective-permute-start | bytes 147464 | tf_op jit(solution)/shard_map/ppermute | solution.py:563
  16.7 1.3 %collective-permute-done.3.row_b = f32[48,1024]{1,0:T(8,128)S(1)} collective-permute-done((f32[48,1024]{1,0:T(8,128)}, f32[48,1024]{1,0:T(8,128)S(1)}, u32[]{:S(2)}, u32[]{:S(2)}) %collective-permute-start.3) | collective-permute-done | bytes 196640 | tf_op jit(solution)/shard_map/ppermute | solution.py:563
  18.9 1.8 %collective-permute-done.4.corner_a = f32[96,128]{1,0:T(8,128)S(1)} collective-permute-done((f32[96,128]{1,0:T(8,128)S(1)}, f32[96,128]{1,0:T(8,128)S(1)}, u32[]{:S(2)}, u32[]{:S(2)}) %collective-permute-start.4) | collective-permute-done | bytes 49184 | tf_op jit(solution)/shard_map/ppermute | solution.py:563
  20.7 8.8 %shard_map.96 = (f32[1,64,1024]{2,1,0:T(8,128)S(1)}, f32[1,2,64,1024]{3,2,1,0:T(8,128)S(1)}, f32[48,256]{1,0:T(8,128)S(1)}, f32[56,128]{1,0:T(8,128)S(1)}, f32[5...) custom-call(f32[8]{0:T(128)S(1)} %copy-done.6, f32[64]{0:T(128)S(1)} %copy-done.7, ...), custom_call_target="tpu_custom_call" | custom-call | tf_op jit(solution)/shard_map/pallas_call | solution.py:336
  29.5 1.6 %collective-permute-start.6 = (f32[56,128]{1,0:T(8,128)S(1)}, f32[56,128]{1,0:T(8,128)S(1)}, u32[]{:S(2)}, u32[]{:S(2)}) collective-permute-start(f32[56,128]{1,0:T(8,128)S(1)} %get-tuple-element.31), channel_id=1, source_target_pairs={{0,32},{16,48},{32,64},{48,80},{64,96},{80,112},{96,0},{112,16},{1... | collective-permute-start | bytes 86024 | tf_op jit(solution)/shard_map/ppermute | solution.py:567
  31.1 2.7 %collective-permute-start.7 = (f32[56,128]{1,0:T(8,128)S(1)}, f32[56,128]{1,0:T(8,128)S(1)}, u32[]{:S(2)}, u32[]{:S(2)}) collective-permute-start(f32[56,128]{1,0:T(8,128)S(1)} %get-tuple-element.32), channel_id=1, source_target_pairs={{0,64},{16,80},{32,96},{48,112},{64,0},{80,16},{96,32},{112,48},{1... | collective-permute-start | bytes 86024 | tf_op jit(solution)/shard_map/ppermute | solution.py:567
  33.8 1.4 %collective-permute-start.8 = (f32[56,128]{1,0:T(8,128)S(1)}, f32[56,128]{1,0:T(8,128)S(1)}, u32[]{:S(2)}, u32[]{:S(2)}) collective-permute-start(f32[56,128]{1,0:T(8,128)S(1)} %get-tuple-element.33), channel_id=1, source_target_pairs={{0,96},{16,112},{32,0},{48,16},{64,32},{80,48},{96,64},{112,80},{1... | collective-permute-start | bytes 86024 | tf_op jit(solution)/shard_map/ppermute | solution.py:567
  35.3 1.2 %collective-permute-done.7 = f32[56,128]{1,0:T(8,128)S(1)} collective-permute-done((f32[56,128]{1,0:T(8,128)S(1)}, f32[56,128]{1,0:T(8,128)S(1)}, u32[]{:S(2)}, u32[]{:S(2)}) %collective-permute-start.7) | collective-permute-done | bytes 28704 | tf_op jit(solution)/shard_map/ppermute | solution.py:567
  36.5 1.2 %collective-permute-done.8 = f32[56,128]{1,0:T(8,128)S(1)} collective-permute-done((f32[56,128]{1,0:T(8,128)S(1)}, f32[56,128]{1,0:T(8,128)S(1)}, u32[]{:S(2)}, u32[]{:S(2)}) %collective-permute-start.8) | collective-permute-done | bytes 28704 | tf_op jit(solution)/shard_map/ppermute | solution.py:567
  38.4 2.2 %collective-permute-start.10 = (f32[216,128]{1,0:T(8,128)S(1)}, f32[216,128]{1,0:T(8,128)S(1)}, u32[]{:S(2)}, u32[]{:S(2)}) collective-permute-start(f32[216,128]{1,0:T(8,128)S(1)} %get-tuple-element.58), channel_id=1, source_target_pairs={{0,12},{4,8},{8,4},{12,0},{1,13},{5,9},{9,5},{13,1},{2,14},{6,10},... | collective-permute-start | bytes 331784 | tf_op jit(solution)/shard_map/ppermute | solution.py:563
  41.4 2.7 %collective-permute-done.11.refs_3_ = f32[216,128]{1,0:T(8,128)S(1)} collective-permute-done((f32[216,128]{1,0:T(8,128)S(1)}, f32[216,128]{1,0:T(8,128)S(1)}, u32[]{:S(2)}, u32[]{:S(2)}) %collective-permute-start.11) | collective-permute-done | bytes 110624 | tf_op jit(solution)/shard_map/ppermute | solution.py:563
  46.7 2.7 %shard_map.97 = (f32[24,64,128]{2,1,0:T(8,128)S(1)}, f32[64,128]{1,0:T(8,128)S(1)}, f32[3,64,128]{2,1,0:T(8,128)S(1)}, f32[24,64,128]{2,1,0:T(8,128)S(1)}, f32[72,128]{1,0:T(8,128)S(1)}) custom-call(f32[248,128]{1,0:T(8,128)S(1)} %constant_dynamic-update-slice_fusion.refs_0_, f32[216,128]{1,0:T(8,128)S(1)} %collective-permute-done.9.refs_1_, ...), custom_call_target="tpu_custom_call" | custom-call | tf_op jit(solution)/shard_map/pallas_call | solution.py:453
  49.4 2.9 %collective-permute-start.16 = (f32[72,128]{1,0:T(8,128)S(1)}, f32[72,128]{1,0:T(8,128)S(1)}, u32[]{:S(2)}, u32[]{:S(2)}) collective-permute-start(f32[72,128]{1,0:T(8,128)S(1)} %get-tuple-element.39), channel_id=1, source_target_pairs={{0,128},{16,144},{32,160},{48,176},{64,192},{80,208},{96,224},{112... | collective-permute-start | bytes 110600 | tf_op jit(solution)/shard_map/ppermute | solution.py:594
  52.3 5.1 %collective-permute-done.16.mine = f32[72,128]{1,0:T(8,128)S(1)} collective-permute-done((f32[72,128]{1,0:T(8,128)S(1)}, f32[72,128]{1,0:T(8,128)S(1)}, u32[]{:S(2)}, u32[]{:S(2)}) %collective-permute-start.16) | collective-permute-done | bytes 36896 | tf_op jit(solution)/shard_map/ppermute | solution.py:594
  57.4 1.2 %collective-permute-done.17.twin = f32[72,128]{1,0:T(8,128)S(1)} collective-permute-done((f32[72,128]{1,0:T(8,128)S(1)}, f32[72,128]{1,0:T(8,128)S(1)}, u32[]{:S(2)}, u32[]{:S(2)}) %collective-permute-start.17) | collective-permute-done | bytes 36896 | tf_op jit(solution)/shard_map/ppermute | solution.py:595
  59.1 3.8 %collective-permute-start.19 = (f32[48,128]{1,0:T(8,128)S(1)}, f32[48,128]{1,0:T(8,128)S(1)}, u32[]{:S(2)}, u32[]{:S(2)}) collective-permute-start(f32[48,128]{1,0:T(8,128)S(1)} %get-tuple-element.42), channel_id=1, source_target_pairs={{0,64},{16,80},{32,96},{48,112},{64,0},{80,16},{96,32},{112,48},{1... | collective-permute-start | bytes 73736 | tf_op jit(solution)/shard_map/ppermute | solution.py:567
  63.8 1.1 %collective-permute-done.19.new2 = f32[48,128]{1,0:T(8,128)S(1)} collective-permute-done((f32[48,128]{1,0:T(8,128)S(1)}, f32[48,128]{1,0:T(8,128)S(1)}, u32[]{:S(2)}, u32[]{:S(2)}) %collective-permute-start.19) | collective-permute-done | bytes 24608 | tf_op jit(solution)/shard_map/ppermute | solution.py:567
  64.9 1.8 %collective-permute-done.20.new3 = f32[48,128]{1,0:T(8,128)S(1)} collective-permute-done((f32[48,128]{1,0:T(8,128)S(1)}, f32[48,128]{1,0:T(8,128)S(1)}, u32[]{:S(2)}, u32[]{:S(2)}) %collective-permute-start.20) | collective-permute-done | bytes 24608 | tf_op jit(solution)/shard_map/ppermute | solution.py:567
  66.7 1.3 %shard_map.99 = (f32[1,64,1024]{2,1,0:T(8,128)}, f32[1,2,64,1024]{3,2,1,0:T(8,128)}) custom-call(f32[1,64,1024]{2,1,0:T(8,128)S(1)} %get-tuple-element.27.depth, f32[1,2,64,1024]{3,2,1,0:T(8,128)S(1)} %get-tuple-element.28.flux, f32[48,256]{1,0:T(8,128)S(1)} %get-tuple-element.29.old, f32[48,128]{1,0:T(8,128)S(1)} %get-tuple-element.40.new0, ...), custom_call_target="tpu_custom_call" | custom-call | tf_op jit(solution)/shard_map/pallas_call | solution.py:544
  (51 shorter events, 7.5 us)
Async XLA Ops:
  0.6 20.0 %copy-start = (f32[1,2,64,1024]{3,2,1,0:T(8,128)S(1)}, f32[1,2,64,1024]{3,2,1,0:T(8,128)}, u32[]{:S(2)}) copy-start(f32[1,2,64,1024]{3,2,1,0:T(8,128)} %flux.1) | copy-start | bytes 1572868
  0.6 20.0 %copy-start.2 = (f32[64,1024]{1,0:T(8,128)S(1)}, f32[64,1024]{1,0:T(8,128)}, u32[]{:S(2)}) copy-start(f32[64,1024]{1,0:T(8,128)} %elevation.1) | copy-start | bytes 786436
  0.7 20.0 %copy-start.3 = (s32[64,1024]{1,0:T(8,128)S(1)}, s32[64,1024]{1,0:T(8,128)}, u32[]{:S(2)}) copy-start(s32[64,1024]{1,0:T(8,128)} %roughness.1) | copy-start | bytes 786436
  2.8 9.7 %collective-permute-start = (f32[384,128]{1,0:T(8,128)}, f32[384,128]{1,0:T(8,128)S(1)}, u32[]{:S(2)}, u32[]{:S(2)}) collective-permute-start(f32[384,128]{1,0:T(8,128)} %get-tuple-element.23), channel_id=1, source_target_pairs={{0,1},{1,0},{2,3},{3,2},{4,5},{5,4},{6,7},{7,6},{8,9},{9,8},{10,11... | collective-permute-start | bytes 589832 | tf_op jit(solution)/shard_map/ppermute | solution.py:575
  4.7 8.7 %collective-permute-start.1 = (f32[384,128]{1,0:T(8,128)}, f32[384,128]{1,0:T(8,128)S(1)}, u32[]{:S(2)}, u32[]{:S(2)}) collective-permute-start(f32[384,128]{1,0:T(8,128)} %get-tuple-element.24), channel_id=1, source_target_pairs={{1,2},{2,1},{5,6},{6,5},{9,10},{10,9},{13,14},{14,13},{17,18},{18,... | collective-permute-start | bytes 589832 | tf_op jit(solution)/shard_map/ppermute | solution.py:576
  8.6 8.1 %collective-permute-start.2 = (f32[48,1024]{1,0:T(8,128)}, f32[48,1024]{1,0:T(8,128)S(1)}, u32[]{:S(2)}, u32[]{:S(2)}) collective-permute-start(f32[48,1024]{1,0:T(8,128)} %get-tuple-element.25), channel_id=1, source_target_pairs={{0,4},{4,0},{8,12},{12,8},{1,5},{5,1},{9,13},{13,9},{2,6},{6,2},{1... | collective-permute-start | bytes 589832 | tf_op jit(solution)/shard_map/ppermute | solution.py:563
  10.3 7.7 %collective-permute-start.3 = (f32[48,1024]{1,0:T(8,128)}, f32[48,1024]{1,0:T(8,128)S(1)}, u32[]{:S(2)}, u32[]{:S(2)}) collective-permute-start(f32[48,1024]{1,0:T(8,128)} %get-tuple-element.26), channel_id=1, source_target_pairs={{0,12},{4,8},{8,4},{12,0},{1,13},{5,9},{9,5},{13,1},{2,14},{6,10},... | collective-permute-start | bytes 589832 | tf_op jit(solution)/shard_map/ppermute | solution.py:563
  13.5 5.4 %collective-permute-start.5 = (f32[96,128]{1,0:T(8,128)S(1)}, f32[96,128]{1,0:T(8,128)S(1)}, u32[]{:S(2)}, u32[]{:S(2)}) collective-permute-start(f32[96,128]{1,0:T(8,128)S(1)} %get-tuple-element.48), channel_id=1, source_target_pairs={{0,12},{4,8},{8,4},{12,0},{1,13},{5,9},{9,5},{13,1},{2,14},{6,10},... | collective-permute-start | bytes 147464 | tf_op jit(solution)/shard_map/ppermute | solution.py:563
  16.6 4.1 %collective-permute-start.4 = (f32[96,128]{1,0:T(8,128)S(1)}, f32[96,128]{1,0:T(8,128)S(1)}, u32[]{:S(2)}, u32[]{:S(2)}) collective-permute-start(f32[96,128]{1,0:T(8,128)S(1)} %get-tuple-element.49), channel_id=1, source_target_pairs={{0,4},{4,0},{8,12},{12,8},{1,5},{5,1},{9,13},{13,9},{2,6},{6,2},{1... | collective-permute-start | bytes 147464 | tf_op jit(solution)/shard_map/ppermute | solution.py:563
  29.5 5.7 %collective-permute-start.6 = (f32[56,128]{1,0:T(8,128)S(1)}, f32[56,128]{1,0:T(8,128)S(1)}, u32[]{:S(2)}, u32[]{:S(2)}) collective-permute-start(f32[56,128]{1,0:T(8,128)S(1)} %get-tuple-element.31), channel_id=1, source_target_pairs={{0,32},{16,48},{32,64},{48,80},{64,96},{80,112},{96,0},{112,16},{1... | collective-permute-start | bytes 86024 | tf_op jit(solution)/shard_map/ppermute | solution.py:567
  31.1 5.4 %collective-permute-start.7 = (f32[56,128]{1,0:T(8,128)S(1)}, f32[56,128]{1,0:T(8,128)S(1)}, u32[]{:S(2)}, u32[]{:S(2)}) collective-permute-start(f32[56,128]{1,0:T(8,128)S(1)} %get-tuple-element.32), channel_id=1, source_target_pairs={{0,64},{16,80},{32,96},{48,112},{64,0},{80,16},{96,32},{112,48},{1... | collective-permute-start | bytes 86024 | tf_op jit(solution)/shard_map/ppermute | solution.py:567
  33.8 3.9 %collective-permute-start.8 = (f32[56,128]{1,0:T(8,128)S(1)}, f32[56,128]{1,0:T(8,128)S(1)}, u32[]{:S(2)}, u32[]{:S(2)}) collective-permute-start(f32[56,128]{1,0:T(8,128)S(1)} %get-tuple-element.33), channel_id=1, source_target_pairs={{0,96},{16,112},{32,0},{48,16},{64,32},{80,48},{96,64},{112,80},{1... | collective-permute-start | bytes 86024 | tf_op jit(solution)/shard_map/ppermute | solution.py:567
  37.7 6.4 %collective-permute-start.11 = (f32[216,128]{1,0:T(8,128)S(1)}, f32[216,128]{1,0:T(8,128)S(1)}, u32[]{:S(2)}, u32[]{:S(2)}) collective-permute-start(f32[216,128]{1,0:T(8,128)S(1)} %get-tuple-element.58), channel_id=1, source_target_pairs={{0,8},{4,12},{8,0},{12,4},{1,9},{5,13},{9,1},{13,5},{2,10},{6,14},... | collective-permute-start | bytes 331784 | tf_op jit(solution)/shard_map/ppermute | solution.py:563
  38.4 6.8 %collective-permute-start.10 = (f32[216,128]{1,0:T(8,128)S(1)}, f32[216,128]{1,0:T(8,128)S(1)}, u32[]{:S(2)}, u32[]{:S(2)}) collective-permute-start(f32[216,128]{1,0:T(8,128)S(1)} %get-tuple-element.58), channel_id=1, source_target_pairs={{0,12},{4,8},{8,4},{12,0},{1,13},{5,9},{9,5},{13,1},{2,14},{6,10},... | collective-permute-start | bytes 331784 | tf_op jit(solution)/shard_map/ppermute | solution.py:563
  40.6 4.7 %collective-permute-start.9 = (f32[216,128]{1,0:T(8,128)S(1)}, f32[216,128]{1,0:T(8,128)S(1)}, u32[]{:S(2)}, u32[]{:S(2)}) collective-permute-start(f32[216,128]{1,0:T(8,128)S(1)} %get-tuple-element.58), channel_id=1, source_target_pairs={{0,4},{4,0},{8,12},{12,8},{1,5},{5,1},{9,13},{13,9},{2,6},{6,2},{1... | collective-permute-start | bytes 331784 | tf_op jit(solution)/shard_map/ppermute | solution.py:563
  41.3 4.5 %collective-permute-start.12 = (f32[248,128]{1,0:T(8,128)S(1)}, f32[248,128]{1,0:T(8,128)S(1)}, u32[]{:S(2)}, u32[]{:S(2)}) collective-permute-start(f32[248,128]{1,0:T(8,128)S(1)} %constant_dynamic-update-slice_fusion.refs_0_), channel_id=1, source_target_pairs={{0,16},{16,0},{32,48},{48,32},{64,80},{80,64},{96,112},{112,96},{1... | collective-permute-start | bytes 380936 | tf_op jit(solution)/shard_map/ppermute | solution.py:592
  44.1 1.6 %collective-permute-start.15 = (f32[216,128]{1,0:T(8,128)S(1)}, f32[216,128]{1,0:T(8,128)S(1)}, u32[]{:S(2)}, u32[]{:S(2)}) collective-permute-start(f32[216,128]{1,0:T(8,128)S(1)} %collective-permute-done.11.refs_3_), channel_id=1, source_target_pairs={{0,16},{16,0},{32,48},{48,32},{64,80},{80,64},{96,112},{112,96},{1... | collective-permute-start | bytes 331784 | tf_op jit(solution)/shard_map/ppermute | solution.py:592
  45.2 1.3 %collective-permute-start.14 = (f32[216,128]{1,0:T(8,128)S(1)}, f32[216,128]{1,0:T(8,128)S(1)}, u32[]{:S(2)}, u32[]{:S(2)}) collective-permute-start(f32[216,128]{1,0:T(8,128)S(1)} %collective-permute-done.10.refs_2_), channel_id=1, source_target_pairs={{0,16},{16,0},{32,48},{48,32},{64,80},{80,64},{96,112},{112,96},{1... | collective-permute-start | bytes 331784 | tf_op jit(solution)/shard_map/ppermute | solution.py:592
  45.4 1.4 %collective-permute-start.13 = (f32[216,128]{1,0:T(8,128)S(1)}, f32[216,128]{1,0:T(8,128)S(1)}, u32[]{:S(2)}, u32[]{:S(2)}) collective-permute-start(f32[216,128]{1,0:T(8,128)S(1)} %collective-permute-done.9.refs_1_), channel_id=1, source_target_pairs={{0,16},{16,0},{32,48},{48,32},{64,80},{80,64},{96,112},{112,96},{1... | collective-permute-start | bytes 331784 | tf_op jit(solution)/shard_map/ppermute | solution.py:592
  49.4 8.0 %collective-permute-start.16 = (f32[72,128]{1,0:T(8,128)S(1)}, f32[72,128]{1,0:T(8,128)S(1)}, u32[]{:S(2)}, u32[]{:S(2)}) collective-permute-start(f32[72,128]{1,0:T(8,128)S(1)} %get-tuple-element.39), channel_id=1, source_target_pairs={{0,128},{16,144},{32,160},{48,176},{64,192},{80,208},{96,224},{112... | collective-permute-start | bytes 110600 | tf_op jit(solution)/shard_map/ppermute | solution.py:594
  57.3 1.2 %collective-permute-start.17 = (f32[72,128]{1,0:T(8,128)S(1)}, f32[72,128]{1,0:T(8,128)S(1)}, u32[]{:S(2)}, u32[]{:S(2)}) collective-permute-start(f32[72,128]{1,0:T(8,128)S(1)} %collective-permute-done.16.mine), channel_id=1, source_target_pairs={{0,16},{16,0},{32,48},{48,32},{64,80},{80,64},{96,112},{112,96},{1... | collective-permute-start | bytes 110600 | tf_op jit(solution)/shard_map/ppermute | solution.py:595
  58.7 5.1 %collective-permute-start.18 = (f32[48,128]{1,0:T(8,128)S(1)}, f32[48,128]{1,0:T(8,128)S(1)}, u32[]{:S(2)}, u32[]{:S(2)}) collective-permute-start(f32[48,128]{1,0:T(8,128)S(1)} %get-tuple-element.41), channel_id=1, source_target_pairs={{0,32},{16,48},{32,64},{48,80},{64,96},{80,112},{96,0},{112,16},{1... | collective-permute-start | bytes 73736 | tf_op jit(solution)/shard_map/ppermute | solution.py:567
  59.1 5.9 %collective-permute-start.19 = (f32[48,128]{1,0:T(8,128)S(1)}, f32[48,128]{1,0:T(8,128)S(1)}, u32[]{:S(2)}, u32[]{:S(2)}) collective-permute-start(f32[48,128]{1,0:T(8,128)S(1)} %get-tuple-element.42), channel_id=1, source_target_pairs={{0,64},{16,80},{32,96},{48,112},{64,0},{80,16},{96,32},{112,48},{1... | collective-permute-start | bytes 73736 | tf_op jit(solution)/shard_map/ppermute | solution.py:567
  62.9 3.8 %collective-permute-start.20 = (f32[48,128]{1,0:T(8,128)S(1)}, f32[48,128]{1,0:T(8,128)S(1)}, u32[]{:S(2)}, u32[]{:S(2)}) collective-permute-start(f32[48,128]{1,0:T(8,128)S(1)} %get-tuple-element.43), channel_id=1, source_target_pairs={{0,96},{16,112},{32,0},{48,16},{64,32},{80,48},{96,64},{112,80},{1... | collective-permute-start | bytes 73736 | tf_op jit(solution)/shard_map/ppermute | solution.py:567
  (5 other events, 59.7 us)

commit v3 on v2

--- a/solution.py
+++ b/solution.py
@@ -42,7 +42,7 @@
 BLOCK = 3 * C_ROWS + 8
 F32 = jnp.float32
 BF16 = jnp.bfloat16
-VMEM_LIMIT = 40 * 1024 * 1024
+VMEM_LIMIT = 24 * 1024 * 1024
 
 
 def face(level, level_next, flux, sill, drag, gate=None):
@@ -82,6 +82,18 @@
     flux_y = face(level, turn(level, -1, 1), flux_y, *faces_y)
     gain = (turn(flux_x, 1, 0) - flux_x) + (turn(flux_y, 1, 1) - flux_y)
     return level + (gain + rain), flux_x, flux_y
+
+
+def both_sides_step(level, fluxes, faces, rain):
+    last_x, next_x, last_y, next_y = fluxes
+    fluxes = (
+        face(turn(level, 1, 0), level, last_x, *faces[0]),
+        face(level, turn(level, -1, 0), next_x, *faces[1]),
+        face(turn(level, 1, 1), level, last_y, *faces[2]),
+        face(level, turn(level, -1, 1), next_y, *faces[3]),
+    )
+    gain = (fluxes[0] - fluxes[1]) + (fluxes[2] - fluxes[3])
+    return level + (gain + rain), fluxes
 
 
 def edge_parts(index):
@@ -137,19 +149,67 @@
     )(*args)
 
 
-def fine_kernel(
-    manning, radar, depth, flux, elevation, roughness, building, tiles, first, second, row_a, row_b, corner_a, corner_b,
-    depth_out, flux_out, old_out, to0, to1, to2, to3, ground_out,
-    level, flow_x, flow_y, elev, friction, opened,
-    sill_x, drag_x, sill_y, drag_y,
-    index_s, rain_s, pooled, coarse, ground_s,
+def roughness_of(classes, manning):
+    value = jnp.full(classes.shape, manning[0], F32)
+    for entry in range(1, ROUGH_CLASSES):
+        value = jnp.where(classes == float(entry), manning[entry], value)
+    return value
+
+
+def pool_matrix():
+    return jnp.where(
+        lax.broadcasted_iota(jnp.int32, (512, 128), 0) // COARSENING
+        == lax.broadcasted_iota(jnp.int32, (512, 128), 1),
+        1.0 / 16.0,
+        0.0,
+    ).astype(BF16)
+
+
+def restrict(sources, take, spans, pooled, coarse):
+    pool = pool_matrix()
+    high = None
+    for part in range(3):
+        cols = slice(512 * part, min(512 * part + 512, WIDE))
+        values = [take(source, cols) for source in sources]
+        high = values[0].shape[0]
+        values = jnp.concatenate(values, axis=0)
+        pooled[part, 0 : values.shape[0], :] = split_dot(values, pool[0 : values.shape[1], :], 2)
+    for slot in range(len(sources)):
+        for part in range(3):
+            cols = slice(128 * part, 128 * part + 128)
+            for target, start, count in spans:
+                first = high * slot + start
+                total = pooled[part, pl.ds(first, count, stride=4), :]
+                for q in range(1, 4):
+                    total = total + pooled[part, pl.ds(first + q, count, stride=4), :]
+                coarse[slot, target : target + count, cols] = total
+
+
+def set_faces(k, elev, friction, opened, sill_x, drag_x, sill_y, drag_y):
+    rows, after, out = pl.ds(8 + 8 * k, 8), pl.ds(9 + 8 * k, 8), pl.ds(8 * k, 8)
+    e, f, o = elev[rows, :], friction[rows, :], opened[rows, :]
+    gate = o * opened[after, :]
+    sill_x[out, :] = jnp.where(gate > 0.0, jnp.maximum(e, elev[after, :]), CLOSED)
+    rough = 0.5 * (f + friction[after, :])
+    drag_x[out, :] = FINE_DRAG * rough * rough
+    sill, drag_y[out, :], gate = static_faces(e, f, o, 1, FINE_DRAG)
+    sill_y[out, :] = jnp.where(gate > 0.0, sill, CLOSED)
+
+
+def places():
+    time_place = lax.axis_index("tm")
+    return lax.axis_index("sx"), lax.axis_index("sy"), time_place, (time_place // 2) % 4, time_place % 2
+
+
+def ready_kernel(
+    manning, radar, depth, flux, elevation, roughness, building, tiles, first, second, row_a, row_b,
+    level, flow_x, flow_y, elev, friction, opened, sill_x, drag_x, sill_y, drag_y, coarse, rain_s, rates_out,
+    index_s, pooled,
 ):
-    row_place = lax.axis_index("sx")
-    col_place = lax.axis_index("sy")
-    time_place = lax.axis_index("tm")
-    x_place, core = (time_place // 2) % 4, time_place % 2
+    row_place, col_place, time_place, x_place, core = places()
     even = col_place % 2 == 0
     odd_row = row_place % 2 == 1
+    none = jnp.zeros((HALO, EDGE), F32)
 
     def fill(target, index, own, scale=1.0):
         target[0:8, :] = jnp.zeros((8, WIDE), F32)
@@ -160,13 +220,10 @@
             target[rows, 0:EDGE] = scale * jnp.where(even, b, a)
             target[rows, EDGE + COLS : WIDE] = scale * jnp.where(even, a, b)
         here = slice(index * HALO, index * HALO + HALO)
-        there = slice((6 + index) * HALO, (6 + index) * HALO + HALO)
         for rows, is_first in ((slice(8, 16), odd_row), (slice(80, 88), ~odd_row)):
             target[rows, EDGE : EDGE + COLS] = scale * jnp.where(is_first, row_a[here, :], row_b[here, :])
-            a = jnp.where(is_first, corner_a[here, :], corner_b[here, :])
-            b = jnp.where(is_first, corner_a[there, :], corner_b[there, :])
-            target[rows, 0:EDGE] = scale * jnp.where(even, b, a)
-            target[rows, EDGE + COLS : WIDE] = scale * jnp.where(even, a, b)
+            target[rows, 0:EDGE] = none
+            target[rows, EDGE + COLS : WIDE] = none
 
     fill(level, 0, depth[0], SCALE)
     fill(flow_x, 1, flux[0, 0], FLOW_SCALE)
@@ -181,11 +238,7 @@
     )
     for k in range(12):
         here = pl.ds(8 * k, 8)
-        classes = friction[here, :]
-        value = jnp.full((8, WIDE), manning[0], F32)
-        for entry in range(1, ROUGH_CLASSES):
-            value = jnp.where(classes == float(entry), manning[entry], value)
-        friction[here, :] = value
+        friction[here, :] = roughness_of(friction[here, :], manning)
         if k in (0, 11):
             opened[here, :] = jnp.zeros((8, WIDE), F32)
             continue
@@ -205,66 +258,78 @@
         rates = jnp.where(index == entry, radar[entry], rates)
     block = lax.broadcasted_iota(jnp.int32, (128, WIDE), 0)
     column = lax.broadcasted_iota(jnp.int32, (128, WIDE), 1) + (COLS * col_place - EDGE)
-    rain_s[0:32, :] = (SCALE * TIME_STEP) * split_dot(rates, jnp.where((column >> 6) == block, 1.0, 0.0).astype(BF16))
+    rain_s[0:32, :] = (SCALE * TIME_STEP) * split_dot(
+        rates, jnp.where((column >> 6) == block, 1.0, 0.0).astype(BF16)
+    )
     means = []
     for half in range(COARSE_STEPS):
         part = rates[16 * half : 16 * half + 16, :]
         means.append((0.25 * SCALE * COARSE_SECONDS) * (part[0:4] + part[4:8] + part[8:12] + part[12:16]))
     coarse_rates = jnp.concatenate(means, axis=0)
+    rates_out[...] = coarse_rates
     block = lax.broadcasted_iota(jnp.int32, (128, C_WIDE), 0)
     column = lax.broadcasted_iota(jnp.int32, (128, C_WIDE), 1) + (C_COLS * col_place - EDGE // COARSENING)
     padded = jnp.concatenate([coarse_rates, jnp.zeros((8, 128), F32)], axis=0)
+    rain_s[32:40, :] = jnp.zeros((8, WIDE), F32)
     rain_s[32:40, 0:C_WIDE] = split_dot(
         padded, jnp.where((column >> 4) == block, 1.0, 0.0).astype(BF16)
     )[0:8]
+
+    coarse[...] = jnp.zeros(coarse.shape, F32)
+    sources = (level, flow_x, flow_y, elev, friction, opened)
+    restrict(sources, lambda source, cols: source[16:80, cols], ((8, 0, 16),), pooled, coarse)
+    for k in range(1, 8):
+        set_faces(k, elev, friction, opened, sill_x, drag_x, sill_y, drag_y)
+
+
+def fine_kernel(*refs):
+    manning, corner_a, corner_b, rain_s, rates = refs[:5]
+    level, flow_x, flow_y, elev, friction, opened, sill_x, drag_x, sill_y, drag_y, coarse = refs[16:27]
+    depth_out, flux_out, old_out, to0, to1, to2, to3, ground_out = refs[27:35]
+    pooled, ground_s, windows = refs[35:]
+    row_place, col_place, time_place, x_place, core = places()
+    even = col_place % 2 == 0
+    odd_row = row_place % 2 == 1
+
+    left, right = slice(0, EDGE), slice(EDGE + COLS, WIDE)
+    grid_row = (jnp.where(row_place == 0, 0.0, 1.0), jnp.where(row_place == 3, 0.0, 1.0))
+    grid_col = (jnp.where(col_place == 0, 0.0, 1.0), jnp.where(col_place == 3, 0.0, 1.0))
+    scales = (SCALE, FLOW_SCALE, FLOW_SCALE, SCALE)
+    for index, target in enumerate((level, flow_x, flow_y, elev, friction, opened)):
+        here = slice(index * HALO, index * HALO + HALO)
+        there = slice((6 + index) * HALO, (6 + index) * HALO + HALO)
+        for r, (rows, is_first) in enumerate(((slice(8, 16), odd_row), (slice(80, 88), ~odd_row))):
+            a = jnp.where(is_first, corner_a[here, :], corner_b[here, :])
+            b = jnp.where(is_first, corner_a[there, :], corner_b[there, :])
+            for c, (cols, value) in enumerate(((left, jnp.where(even, b, a)), (right, jnp.where(even, a, b)))):
+                if index < 4:
+                    value = scales[index] * value
+                elif index == 4:
+                    value = roughness_of(value, manning)
+                else:
+                    value = (1.0 - value) * (grid_row[r] * grid_col[c])
+                target[rows, cols] = value
+
+    sources = (level, flow_x, flow_y, elev, friction, opened)
+    take = lambda source, cols: jnp.concatenate([source[8:16, cols], source[80:88, cols]], axis=0)
+    restrict(sources, take, ((6, 0, 2), (24, 8, 2)), pooled, coarse)
+    for k in (0, 8, 9):
+        set_faces(k, elev, friction, opened, sill_x, drag_x, sill_y, drag_y)
+    for k in range(10):
+        rows, out = pl.ds(8 + 8 * k, 8), pl.ds(8 * k, 8)
+        level[rows, :] = level[rows, :] + elev[rows, :]
+        flow_x[rows, :] = jnp.where(sill_x[out, :] < CLOSED, flow_x[rows, :], 0.0)
+        flow_y[rows, :] = jnp.where(sill_y[out, :] < CLOSED, flow_y[rows, :], 0.0)
     row_above = jnp.maximum(row_place - 1, 0)
     row_below = jnp.minimum(row_place + 1, 3)
 
-    pool = jnp.where(
-        lax.broadcasted_iota(jnp.int32, (512, 128), 0) // COARSENING
-        == lax.broadcasted_iota(jnp.int32, (512, 128), 1),
-        1.0 / 16.0,
-        0.0,
-    ).astype(BF16)
-
-    def restrict(source, slot):
-        for part in range(3):
-            take = source[8:88, 512 * part : min(512 * part + 512, WIDE)]
-            pooled[part, :, :] = split_dot(take, pool[0 : take.shape[1], :], 1 if slot == 5 else 2)
-        for part in range(3):
-            cols = slice(128 * part, 128 * part + 128)
-            for target, start, count in ((6, 0, 2), (8, 8, 16), (24, 72, 2)):
-                total = pooled[part, pl.ds(start, count, stride=4), :]
-                for q in range(1, 4):
-                    total = total + pooled[part, pl.ds(start + q, count, stride=4), :]
-                coarse[slot, target : target + count, cols] = total
-
-    coarse[...] = jnp.zeros(coarse.shape, F32)
-    for slot, source in enumerate((level, flow_x, flow_y, elev, friction, opened)):
-        restrict(source, slot)
-
-    for k in range(10):
-        rows, after, out = pl.ds(8 + 8 * k, 8), pl.ds(9 + 8 * k, 8), pl.ds(8 * k, 8)
-        e, f, o = elev[rows, :], friction[rows, :], opened[rows, :]
-        gate = o * opened[after, :]
-        sill_x[out, :] = jnp.where(gate > 0.0, jnp.maximum(e, elev[after, :]), CLOSED)
-        flow_x[rows, :] = gate * flow_x[rows, :]
-        rough = 0.5 * (f + friction[after, :])
-        drag_x[out, :] = FINE_DRAG * rough * rough
-        sill, drag_y[out, :], gate = static_faces(e, f, o, 1, FINE_DRAG)
-        sill_y[out, :] = jnp.where(gate > 0.0, sill, CLOSED)
-        flow_y[rows, :] = gate * flow_y[rows, :]
-
-    for k in range(12):
-        here = pl.ds(8 * k, 8)
-        level[here, :] = level[here, :] + elev[here, :]
     sub = lax.broadcasted_iota(jnp.int32, (GROUP, WIDE), 0)
 
     def fine_step(step, carry):
         rains = [rain_s[pl.ds(4 * step + place, 1), :] for place in (row_above, row_place, row_below)]
         now = level[8 : 8 + GROUP, :]
         up = turn(now, -1, 0)
-        west = now
+        after, up_after, west = now, up, now
         for k in range(HIGH // GROUP):
             out = slice(GROUP * k, GROUP * k + GROUP)
             rows = slice(8 + GROUP * k, 8 + GROUP * k + GROUP)
@@ -287,7 +352,7 @@
             now, up, west = after, up_after, down
         return carry
 
-    lax.fori_loop(0, FINE_STEPS, fine_step, 0)
+    lax.fori_loop(0, FINE_STEPS, fine_step, 0, unroll=True)
 
     c_elev, c_friction, c_open = coarse[3], coarse[4], coarse[5]
     faces_x = static_faces(c_elev, c_friction, c_open, 0, COARSE_DRAG)
@@ -307,8 +372,8 @@
     depth_out[0] = (1.0 / SCALE) * level[own]
     flux_out[0, 0] = (1.0 / FLOW_SCALE) * flow_x[own]
     flux_out[0, 1] = (1.0 / FLOW_SCALE) * flow_y[own]
-    for slot, source in enumerate((level, flow_x, flow_y)):
-        restrict(source, slot)
+    sources = (level, flow_x, flow_y)
+    restrict(sources, lambda source, cols: source[16:80, cols], ((8, 0, 16),), pooled, coarse)
     factor = jnp.where(time_place == 0, 0.0, 1.0)
     side = EDGE // COARSENING
     outs = (to0, to1, to2, to3)
@@ -316,48 +381,66 @@
         mine = old[slot][8:24, :]
         old_out[C_ROWS * slot : C_ROWS * slot + C_ROWS, :] = turn(mine, -side, 1)[:, 0:C_COLS]
         value = coarse[slot, 8:24, :] - factor * mine
-        for d, out in enumerate(outs):
-            window = (x_place + d) % 4
-            moved = pltpu.roll(value, (C_WIDE - 64 * window) % C_WIDE, 1)
-            out[C_ROWS * slot : C_ROWS * slot + C_ROWS, :] = moved[:, 0:128]
-        fixed = pltpu.roll(coarse[3 + slot, 8:24, :], (C_WIDE - 64 * x_place) % C_WIDE, 1)
-        ground_s[C_ROWS * slot : C_ROWS * slot + C_ROWS, :] = fixed[:, 0:128]
-    ground_out[...] = ground_s[pl.ds(pl.multiple_of(core * PART, PART), PART), :]
-    for out in outs:
-        out[3 * C_ROWS : BLOCK, :] = coarse_rates
-
-
-def fine(manning, radar, depth, flux, *rest):
+        fixed = coarse[3 + slot, 8:24, :]
+        here = slice(C_ROWS * slot, C_ROWS * slot + C_ROWS)
+        for odd, (now, ground_now) in enumerate(((value, fixed), (turn(value, -64, 1), turn(fixed, -64, 1)))):
+            for half in range(2):
+                cols = slice(128 * half, 128 * half + 128)
+                windows[2 * half + odd, here, :] = now[:, cols]
+                ground_s[2 * half + odd, here, :] = ground_now[:, cols]
+    ground_out[...] = ground_s[x_place, pl.ds(pl.multiple_of(core * PART, PART), PART), :]
+    for d, out in enumerate(outs):
+        out[0 : 3 * C_ROWS, :] = windows[(x_place + d) % 4]
+        out[3 * C_ROWS : BLOCK, :] = rates[...]
+
+
+def ready(manning, radar, *rest):
+    smem = pl.BlockSpec(memory_space=pltpu.SMEM)
+    vmem = pl.BlockSpec(memory_space=pltpu.VMEM)
+    padded = jax.ShapeDtypeStruct((HIGH + 16, WIDE), F32)
+    faces = jax.ShapeDtypeStruct((HIGH, WIDE), F32)
+    coarse = jax.ShapeDtypeStruct((6, C_HIGH, C_WIDE), F32)
+    rain = jax.ShapeDtypeStruct((40, WIDE), F32)
+    rates = jax.ShapeDtypeStruct((8, 128), F32)
+    return pl.pallas_call(
+        ready_kernel,
+        in_specs=[smem, smem] + [vmem] * 10,
+        out_specs=[vmem] * 13,
+        out_shape=[padded] * 6 + [faces] * 4 + [coarse, rain, rates],
+        scratch_shapes=[pltpu.VMEM((32, 128), jnp.int32), pltpu.VMEM((3, 6 * ROWS, 128), F32)],
+        cost_estimate=pl.CostEstimate(flops=40_000_000, bytes_accessed=10_000_000, transcendentals=0),
+        compiler_params=pltpu.CompilerParams(vmem_limit_bytes=VMEM_LIMIT),
+    )(manning, radar, *rest)
+
+
+def fine(manning, corner_a, corner_b, rain, rates, arrays):
     smem = pl.BlockSpec(memory_space=pltpu.SMEM)
     vmem = pl.BlockSpec(memory_space=pltpu.VMEM)
     message = jax.ShapeDtypeStruct((BLOCK, 128), F32)
-    padded = pltpu.VMEM((HIGH + 16, WIDE), F32)
-    faces = pltpu.VMEM((HIGH, WIDE), F32)
+    shapes = [jax.ShapeDtypeStruct(array.shape, F32) for array in arrays]
     return pl.pallas_call(
         fine_kernel,
-        in_specs=[smem, smem] + [vmem] * 12,
-        out_specs=[vmem] * 8,
-        out_shape=(
-            jax.ShapeDtypeStruct(depth.shape, F32),
-            jax.ShapeDtypeStruct(flux.shape, F32),
+        in_specs=[smem] + [vmem] * 15,
+        out_specs=[vmem] * 19,
+        out_shape=shapes
+        + [
+            jax.ShapeDtypeStruct((1, ROWS, COLS), F32),
+            jax.ShapeDtypeStruct((1, 2, ROWS, COLS), F32),
             jax.ShapeDtypeStruct((3 * C_ROWS, C_COLS), F32),
             message,
             message,
             message,
             message,
             jax.ShapeDtypeStruct((PART, 128), F32),
-        ),
-        scratch_shapes=[padded] * 6
-        + [faces] * 4
-        + [
-            pltpu.VMEM((32, 128), jnp.int32),
-            pltpu.VMEM((40, WIDE), F32),
-            pltpu.VMEM((3, HIGH, 128), F32),
-            pltpu.VMEM((6, C_HIGH, C_WIDE), F32),
-            pltpu.VMEM((3 * C_ROWS, 128), F32),
+        ],
+        input_output_aliases={5 + place: place for place in range(11)},
+        scratch_shapes=[
+            pltpu.VMEM((3, 3 * ROWS, 128), F32),
+            pltpu.VMEM((4, 3 * C_ROWS, 128), F32),
+            pltpu.VMEM((4, 3 * C_ROWS, 128), F32),
         ],
         compiler_params=pltpu.CompilerParams(vmem_limit_bytes=VMEM_LIMIT),
-    )(manning, radar, depth, flux, *rest)
+    )(manning, corner_a, corner_b, rain, rates, *arrays)[11:]
 
 
 HALF = SLICES // 2
@@ -370,18 +453,23 @@
     sill, drag, gate = static_faces(*ground, 0, COARSE_DRAG)
     last = lax.broadcasted_iota(jnp.int32, gate.shape, 0) == gate.shape[0] - 1
     gate = jnp.where(last, 0.0, gate)
-    return (sill, drag, gate), static_faces(*ground, 1, COARSE_DRAG)
+    faces_x, faces_y = (sill, drag, gate), static_faces(*ground, 1, COARSE_DRAG)
+    moved_x = tuple(turn(part, 1, 0) for part in faces_x)
+    moved_y = tuple(turn(part, 1, 1) for part in faces_y)
+    return moved_x, faces_x, moved_y, faces_y
 
 
 def near_start(row_place):
     return pl.multiple_of(C_ROWS * jnp.clip(row_place - 1, 0, 1), C_ROWS)
 
 
-def sweep_slices(start, state, change, rain, ground, newest, top, high):
-    faces_x, faces_y = sweep_faces(ground)
+def sweep_slices(first, state, change, rain, ground, newest, top, high):
+    faces = sweep_faces(ground)
     rows = pl.ds(top, high)
-
-    def one_slice(moment, state):
+    level, flux_x, flux_y = state
+    fluxes = (turn(flux_x, 1, 0), flux_x, turn(flux_y, 1, 1), flux_y)
+
+    for moment in range(first, HALF):
         for step in range(COARSE_STEPS):
             wet = jnp.concatenate(
                 [
@@ -392,12 +480,15 @@
                 ],
                 axis=0,
             )
-            state = whole_step(*state, faces_x, faces_y, wet)
-        for field in range(3):
-            newest[3 * moment + field, 0:high, :] = state[field]
-        return tuple(state[field] + change[3 * moment + field, rows, :] for field in range(3))
-
-    return lax.fori_loop(start, HALF, one_slice, state)
+            level, fluxes = both_sides_step(level, fluxes, faces, wet)
+        for field, value in enumerate((level, fluxes[1], fluxes[3])):
+            newest[3 * moment + field, 0:high, :] = value
+        add, add_x, add_y = (change[3 * moment + field, rows, :] for field in range(3))
+        level = level + add
+        fluxes = (
+            fluxes[0] + turn(add_x, 1, 0), fluxes[1] + add_x, fluxes[2] + turn(add_y, 1, 1), fluxes[3] + add_y
+        )
+    return level, fluxes[1], fluxes[3]
 
 
 def first_kernel(*refs):
@@ -435,13 +526,18 @@
     column = column + (C_COLS * col_place + 64 * x_place - EDGE // COARSENING)
     rain[...] = split_dot(rates[...], jnp.where((column >> 4) == block, 1.0, 0.0).astype(BF16))
 
-    start = jnp.where(z_place == 0, 1, HALF)
-    fixed = (ground[0], ground[1], ground[2])
-    state = (change[0] + ground[0], change[1], change[2])
-    state = sweep_slices(start, state, change, rain, fixed, newest, 0, TALL)
+    all_s[...] = jnp.zeros(all_s.shape, F32)
+
+    @pl.when(z_place == 0)
+    def _():
+        fixed = (ground[0], ground[1], ground[2])
+        state = (change[0] + ground[0], change[1], change[2])
+        state = sweep_slices(1, state, change, rain, fixed, newest, 0, TALL)
+        for field in range(3):
+            all_s[field] = state[field]
+
     near = pl.ds(near_start(row_place), NEAR)
     for field in range(3):
-        all_s[field] = state[field]
         state_s[NEAR * field : NEAR * field + NEAR, :] = all_s[field, near, :]
     count = 3 * NEAR // 2
     halfway[...] = state_s[pl.ds(pl.multiple_of(core * count, count), count), :]
@@ -475,14 +571,17 @@
     row_place = lax.axis_index("sx")
     time_place = lax.axis_index("tm")
     z_place, x_place, core = time_place // 8, (time_place // 2) % 4, time_place % 2
-    count = 3 * NEAR // 2
-    state_s[pl.ds(pl.multiple_of(core * count, count), count), :] = mine[...]
-    state_s[pl.ds(pl.multiple_of((1 - core) * count, count), count), :] = twin[...]
-    state = tuple(state_s[NEAR * field : NEAR * field + NEAR, :] for field in range(3))
-    start = jnp.where(z_place == 0, HALF, 0)
     top = near_start(row_place)
-    fixed = tuple(ground[field, pl.ds(top, NEAR), :] for field in range(3))
-    sweep_slices(start, state, change, rain, fixed, late, top, NEAR)
+
+    @pl.when(z_place == 1)
+    def _():
+        count = 3 * NEAR // 2
+        state_s[pl.ds(pl.multiple_of(core * count, count), count), :] = mine[...]
+        state_s[pl.ds(pl.multiple_of((1 - core) * count, count), count), :] = twin[...]
+        state = tuple(state_s[NEAR * field : NEAR * field + NEAR, :] for field in range(3))
+        fixed = tuple(ground[field, pl.ds(top, NEAR), :] for field in range(3))
+        sweep_slices(0, state, change, rain, fixed, late, top, NEAR)
+
     rows = pl.ds(pl.multiple_of(C_ROWS * row_place, C_ROWS), C_ROWS)
     late_rows = pl.ds(pl.multiple_of(C_ROWS * row_place - top, C_ROWS), C_ROWS)
     for d, out in enumerate((out0, out1, out2, out3)):
@@ -581,9 +680,10 @@
     even_row = lax.axis_index("sx") % 2 == 0
     corner_a = with_row(jnp.where(even_row, bottoms, tops), 1)
     corner_b = with_row(jnp.where(even_row, tops, bottoms), 3)
-    depth, flux, old, own, *away, ground = fine(
-        manning, radar_rates, *fields, tile_index, first, second, row_a, row_b, corner_a, corner_b
+    *arrays, rain, rates = ready(
+        manning, radar_rates, *fields, tile_index, first, second, row_a, row_b
     )
+    depth, flux, old, own, *away, ground = fine(manning, corner_a, corner_b, rain, rates, arrays)
     parts = [own] + [over_x(away[d - 1], d) for d in (1, 2, 3)]
     column = jnp.concatenate([part[:FIELDS] for part in parts] + [ground], axis=0)
     mine = jnp.concatenate([column] + [part[FIELDS:] for part in parts], axis=0)

time: 68.2 us -> 65.7 us (0.963)
  waiting for transfers between devices: 22.3 us -> 19.5 us
  starting transfers between devices: 29.8 us -> 30.5 us
    ppermute x7, waiting for transfers between devices: 7.9 us -> 5.81 us  [with_row(): return lax.ppermute(values, 'sx', [(i, i ^ flip) for i in range(4)])]
    pallas_call x1, Pallas kernels: 2.67 us -> 1.96 us  [first_sweep(): pl.pallas_call(first_kernel, in_specs=[vmem] * 8, out_specs=[vmem] * 5, o...]
    ppermute x1, starting transfers between devices: 2.87 us -> 3.58 us  [on_device(): lax.ppermute(halfway, 'tm', time_route(lambda z, x, core: (z + 1, x, core)))]
    ppermute x1, waiting for transfers between devices: 5.08 us -> 4.38 us  [on_device(): lax.ppermute(halfway, 'tm', time_route(lambda z, x, core: (z + 1, x, core)))]
    pallas_call x1 -> x2, Pallas kernels: 8.8 us -> 9.2 us  [the longest x1 7.18 us: fine(): pl.pallas_call(fine_kernel, in_specs=[smem] + [vmem] * 15, out_specs=[vme...]
  transfers between devices with their start and end apart: 21 -> 21, of which waited for: 16 -> 15; matrix products, arithmetic and copies ran while one was open for 0% -> 0% of each run, Pallas kernels for 0% -> 3%
where the time goes in v3:
time: 65.7 us; the launch traced here: 65.5 us
  starting transfers between devices  30.5 us (46%)
  waiting for transfers between devices  19.5 us (30%)
  Pallas kernels  14.6 us (22%)
  between operations  0.81 us (1%)
    ppermute x7, starting transfers between devices, with_row(): return lax.ppermute(values, 'sx', [(i, i ^ flip) for i in range(4)])  10.7 us
    ppermute x6, starting transfers between devices, over_x(): lax.ppermute(values, 'tm', time_route(lambda z, x, core: (z, x + distance...  9.97 us
    pallas_call x1, Pallas kernels, fine(): pl.pallas_call(fine_kernel, in_specs=[smem] + [vmem] * 15, out_specs=[vme...  7.18 us
    ppermute x6, waiting for transfers between devices, over_x(): lax.ppermute(values, 'tm', time_route(lambda z, x, core: (z, x + distance...  6.19 us
    ppermute x7, waiting for transfers between devices, with_row(): return lax.ppermute(values, 'sx', [(i, i ^ flip) for i in range(4)])  5.81 us
    ppermute x1, waiting for transfers between devices, on_device(): lax.ppermute(halfway, 'tm', time_route(lambda z, x, core: (z + 1, x, core)))  4.38 us
    ppermute x1, starting transfers between devices, on_device(): second = lax.ppermute(second, 'sy', [(1, 2), (2, 1)])  3.89 us
    ppermute x1, starting transfers between devices, on_device(): lax.ppermute(halfway, 'tm', time_route(lambda z, x, core: (z + 1, x, core)))  3.58 us
  transfers between devices with their start and end apart: 21, of which 15 were waited for; matrix products, arithmetic and copies ran while one was open for 0% of the time, Pallas kernels for 3%

profile of v3, /device:TPU:32, one launch (start us, length us, event | category | flops | bytes accessed | tf_op | source)
XLA Modules:
  0.0 65.5 jit_solution(6542904678504669416)
XLA Ops:
  0.7 2.1 %shard_map.95 = (f32[384,128]{1,0:T(8,128)}, f32[384,128]{1,0:T(8,128)}, f32[48,1024]{1,0:T(8,128)}, f32[48,1024]{1,0:T(8,128)}) custom-call(f32[1,64,1024]{2,1,0:T(8,128)} %depth.1, f32[1,64,1024]{2,1,0:T(8,128)} %depth.1, f32[1,64,1024]{2,1,0:T(8,128)} %depth.1, f32[1,64,1024]{2,1,0:T(8,128)} %depth.1, f32[1,2,64,1024]{3,2,1,0:T(8,128)} %flux.1, ...), custom_call_target="tpu_custom_call" | custom-call | tf_op jit(solution)/shard_map/pallas_call | solution.py:143
  2.8 1.9 %collective-permute-start = (f32[384,128]{1,0:T(8,128)}, f32[384,128]{1,0:T(8,128)S(1)}, u32[]{:S(2)}, u32[]{:S(2)}) collective-permute-start(f32[384,128]{1,0:T(8,128)} %get-tuple-element.36), channel_id=1, source_target_pairs={{0,1},{1,0},{2,3},{3,2},{4,5},{5,4},{6,7},{7,6},{8,9},{9,8},{10,11... | collective-permute-start | bytes 589832 | tf_op jit(solution)/shard_map/ppermute | solution.py:674
  4.7 3.9 %collective-permute-start.1 = (f32[384,128]{1,0:T(8,128)}, f32[384,128]{1,0:T(8,128)S(1)}, u32[]{:S(2)}, u32[]{:S(2)}) collective-permute-start(f32[384,128]{1,0:T(8,128)} %get-tuple-element.37), channel_id=1, source_target_pairs={{1,2},{2,1},{5,6},{6,5},{9,10},{10,9},{13,14},{14,13},{17,18},{18,... | collective-permute-start | bytes 589832 | tf_op jit(solution)/shard_map/ppermute | solution.py:675
  8.6 1.7 %collective-permute-start.4 = (f32[48,1024]{1,0:T(8,128)}, f32[48,1024]{1,0:T(8,128)S(1)}, u32[]{:S(2)}, u32[]{:S(2)}) collective-permute-start(f32[48,1024]{1,0:T(8,128)} %get-tuple-element.38), channel_id=1, source_target_pairs={{0,4},{4,0},{8,12},{12,8},{1,5},{5,1},{9,13},{13,9},{2,6},{6,2},{1... | collective-permute-start | bytes 589832 | tf_op jit(solution)/shard_map/ppermute | solution.py:662
  10.3 2.2 %collective-permute-start.5 = (f32[48,1024]{1,0:T(8,128)}, f32[48,1024]{1,0:T(8,128)S(1)}, u32[]{:S(2)}, u32[]{:S(2)}) collective-permute-start(f32[48,1024]{1,0:T(8,128)} %get-tuple-element.39), channel_id=1, source_target_pairs={{0,12},{4,8},{8,4},{12,0},{1,13},{5,9},{9,5},{13,1},{2,14},{6,10},... | collective-permute-start | bytes 589832 | tf_op jit(solution)/shard_map/ppermute | solution.py:662
  13.5 3.1 %collective-permute-start.3 = (f32[96,128]{1,0:T(8,128)S(1)}, f32[96,128]{1,0:T(8,128)S(1)}, u32[]{:S(2)}, u32[]{:S(2)}) collective-permute-start(f32[96,128]{1,0:T(8,128)S(1)} %get-tuple-element.74), channel_id=1, source_target_pairs={{0,12},{4,8},{8,4},{12,0},{1,13},{5,9},{9,5},{13,1},{2,14},{6,10},... | collective-permute-start | bytes 147464 | tf_op jit(solution)/shard_map/ppermute | solution.py:662
  16.7 1.3 %collective-permute-done.5.row_b = f32[48,1024]{1,0:T(8,128)S(1)} collective-permute-done((f32[48,1024]{1,0:T(8,128)}, f32[48,1024]{1,0:T(8,128)S(1)}, u32[]{:S(2)}, u32[]{:S(2)}) %collective-permute-start.5) | collective-permute-done | bytes 196640 | tf_op jit(solution)/shard_map/ppermute | solution.py:662
  18.1 2.0 %shard_map.96 = (f32[96,1280]{1,0:T(8,128)S(1)}, f32[96,1280]{1,0:T(8,128)S(1)}, f32[96,1280]{1,0:T(8,128)S(1)}, f32[96,1280]{1,0:T(8,128)S(1)}, f32[96,1280]{1,...) custom-call(f32[8]{0:T(128)S(1)} %copy-done.6, ...), custom_call_target="tpu_custom_call" | custom-call | flops 40000000 | bytes 10000000 | tf_op jit(solution)/shard_map/pallas_call | solution.py:405
  20.7 7.2 %shard_map.97 = (f32[96,1280]{1,0:T(8,128)S(1)}, f32[96,1280]{1,0:T(8,128)S(1)}, f32[96,1280]{1,0:T(8,128)S(1)}, f32[96,1280]{1,0:T(8,128)S(1)}, f32[96,1280]{1,...) custom-call(f32[8]{0:T(128)S(1)} %copy-done.6, ...), custom_call_target="tpu_custom_call", output_to_operand_aliasing={{0}: (5, {}), {1}: (6, {}), {2}: (7, {}), {3}: (8, {}), {4}... | custom-call | tf_op jit(solution)/shard_map/pallas_call | solution.py:421
  27.9 1.6 %collective-permute-start.6 = (f32[56,128]{1,0:T(8,128)S(1)}, f32[56,128]{1,0:T(8,128)S(1)}, u32[]{:S(2)}, u32[]{:S(2)}) collective-permute-start(f32[56,128]{1,0:T(8,128)S(1)} %get-tuple-element.57), channel_id=1, source_target_pairs={{0,32},{16,48},{32,64},{48,80},{64,96},{80,112},{96,0},{112,16},{1... | collective-permute-start | bytes 86024 | tf_op jit(solution)/shard_map/ppermute | solution.py:666
  29.4 2.7 %collective-permute-start.7 = (f32[56,128]{1,0:T(8,128)S(1)}, f32[56,128]{1,0:T(8,128)S(1)}, u32[]{:S(2)}, u32[]{:S(2)}) collective-permute-start(f32[56,128]{1,0:T(8,128)S(1)} %get-tuple-element.58), channel_id=1, source_target_pairs={{0,64},{16,80},{32,96},{48,112},{64,0},{80,16},{96,32},{112,48},{1... | collective-permute-start | bytes 86024 | tf_op jit(solution)/shard_map/ppermute | solution.py:666
  32.2 1.4 %collective-permute-start.8 = (f32[56,128]{1,0:T(8,128)S(1)}, f32[56,128]{1,0:T(8,128)S(1)}, u32[]{:S(2)}, u32[]{:S(2)}) collective-permute-start(f32[56,128]{1,0:T(8,128)S(1)} %get-tuple-element.59), channel_id=1, source_target_pairs={{0,96},{16,112},{32,0},{48,16},{64,32},{80,48},{96,64},{112,80},{1... | collective-permute-start | bytes 86024 | tf_op jit(solution)/shard_map/ppermute | solution.py:666
  33.6 1.2 %collective-permute-done.7 = f32[56,128]{1,0:T(8,128)S(1)} collective-permute-done((f32[56,128]{1,0:T(8,128)S(1)}, f32[56,128]{1,0:T(8,128)S(1)}, u32[]{:S(2)}, u32[]{:S(2)}) %collective-permute-start.7) | collective-permute-done | bytes 28704 | tf_op jit(solution)/shard_map/ppermute | solution.py:666
  34.8 1.2 %collective-permute-done.8 = f32[56,128]{1,0:T(8,128)S(1)} collective-permute-done((f32[56,128]{1,0:T(8,128)S(1)}, f32[56,128]{1,0:T(8,128)S(1)}, u32[]{:S(2)}, u32[]{:S(2)}) %collective-permute-start.8) | collective-permute-done | bytes 28704 | tf_op jit(solution)/shard_map/ppermute | solution.py:666
  36.0 1.3 %collective-permute-start.11 = (f32[216,128]{1,0:T(8,128)S(1)}, f32[216,128]{1,0:T(8,128)S(1)}, u32[]{:S(2)}, u32[]{:S(2)}) collective-permute-start(f32[216,128]{1,0:T(8,128)S(1)} %get-tuple-element.84), channel_id=1, source_target_pairs={{0,8},{4,12},{8,0},{12,4},{1,9},{5,13},{9,1},{13,5},{2,10},{6,14},... | collective-permute-start | bytes 331784 | tf_op jit(solution)/shard_map/ppermute | solution.py:662
  37.3 1.6 %collective-permute-start.10 = (f32[216,128]{1,0:T(8,128)S(1)}, f32[216,128]{1,0:T(8,128)S(1)}, u32[]{:S(2)}, u32[]{:S(2)}) collective-permute-start(f32[216,128]{1,0:T(8,128)S(1)} %get-tuple-element.84), channel_id=1, source_target_pairs={{0,12},{4,8},{8,4},{12,0},{1,13},{5,9},{9,5},{13,1},{2,14},{6,10},... | collective-permute-start | bytes 331784 | tf_op jit(solution)/shard_map/ppermute | solution.py:662
  39.7 2.7 %collective-permute-done.11.refs_3_ = f32[216,128]{1,0:T(8,128)S(1)} collective-permute-done((f32[216,128]{1,0:T(8,128)S(1)}, f32[216,128]{1,0:T(8,128)S(1)}, u32[]{:S(2)}, u32[]{:S(2)}) %collective-permute-start.11) | collective-permute-done | bytes 110624 | tf_op jit(solution)/shard_map/ppermute | solution.py:662
  45.0 2.0 %shard_map.98 = (f32[24,64,128]{2,1,0:T(8,128)S(1)}, f32[64,128]{1,0:T(8,128)S(1)}, f32[3,64,128]{2,1,0:T(8,128)S(1)}, f32[24,64,128]{2,1,0:T(8,128)S(1)}, f32[72,128]{1,0:T(8,128)S(1)}) custom-call(f32[248,128]{1,0:T(8,128)S(1)} %constant_dynamic-update-slice_fusion.refs_0_, f32[216,128]{1,0:T(8,128)S(1)} %collective-permute-done.9.refs_1_, ...), custom_call_target="tpu_custom_call" | custom-call | tf_op jit(solution)/shard_map/pallas_call | solution.py:549
  47.0 3.6 %collective-permute-start.16 = (f32[72,128]{1,0:T(8,128)S(1)}, f32[72,128]{1,0:T(8,128)S(1)}, u32[]{:S(2)}, u32[]{:S(2)}) collective-permute-start(f32[72,128]{1,0:T(8,128)S(1)} %get-tuple-element.65), channel_id=1, source_target_pairs={{0,128},{16,144},{32,160},{48,176},{64,192},{80,208},{96,224},{112... | collective-permute-start | bytes 110600 | tf_op jit(solution)/shard_map/ppermute | solution.py:694
  50.6 4.4 %collective-permute-done.16.mine = f32[72,128]{1,0:T(8,128)S(1)} collective-permute-done((f32[72,128]{1,0:T(8,128)S(1)}, f32[72,128]{1,0:T(8,128)S(1)}, u32[]{:S(2)}, u32[]{:S(2)}) %collective-permute-start.16) | collective-permute-done | bytes 36896 | tf_op jit(solution)/shard_map/ppermute | solution.py:694
  55.0 1.2 %collective-permute-done.17.twin = f32[72,128]{1,0:T(8,128)S(1)} collective-permute-done((f32[72,128]{1,0:T(8,128)S(1)}, f32[72,128]{1,0:T(8,128)S(1)}, u32[]{:S(2)}, u32[]{:S(2)}) %collective-permute-start.17) | collective-permute-done | bytes 36896 | tf_op jit(solution)/shard_map/ppermute | solution.py:695
  56.6 3.8 %collective-permute-start.19 = (f32[48,128]{1,0:T(8,128)S(1)}, f32[48,128]{1,0:T(8,128)S(1)}, u32[]{:S(2)}, u32[]{:S(2)}) collective-permute-start(f32[48,128]{1,0:T(8,128)S(1)} %get-tuple-element.68), channel_id=1, source_target_pairs={{0,64},{16,80},{32,96},{48,112},{64,0},{80,16},{96,32},{112,48},{1... | collective-permute-start | bytes 73736 | tf_op jit(solution)/shard_map/ppermute | solution.py:666
  62.4 1.8 %collective-permute-done.20.new3 = f32[48,128]{1,0:T(8,128)S(1)} collective-permute-done((f32[48,128]{1,0:T(8,128)S(1)}, f32[48,128]{1,0:T(8,128)S(1)}, u32[]{:S(2)}, u32[]{:S(2)}) %collective-permute-start.20) | collective-permute-done | bytes 24608 | tf_op jit(solution)/shard_map/ppermute | solution.py:666
  64.2 1.3 %shard_map.100 = (f32[1,64,1024]{2,1,0:T(8,128)}, f32[1,2,64,1024]{3,2,1,0:T(8,128)}) custom-call(f32[1,64,1024]{2,1,0:T(8,128)S(1)} %get-tuple-element.53.depth, f32[1,2,64,1024]{3,2,1,0:T(8,128)S(1)} %get-tuple-element.54.flux, f32[48,256]{1,0:T(8,128)S(1)} %get-tuple-element.55.old, f32[48,128]{1,0:T(8,128)S(1)} %get-tuple-element.66.new0, ...), custom_call_target="tpu_custom_call" | custom-call | tf_op jit(solution)/shard_map/pallas_call | solution.py:643
  (52 shorter events, 7.6 us)
Async XLA Ops:
  0.6 17.4 %copy-start = (f32[1,2,64,1024]{3,2,1,0:T(8,128)S(1)}, f32[1,2,64,1024]{3,2,1,0:T(8,128)}, u32[]{:S(2)}) copy-start(f32[1,2,64,1024]{3,2,1,0:T(8,128)} %flux.1) | copy-start | bytes 1572868
  0.6 17.4 %copy-start.2 = (f32[64,1024]{1,0:T(8,128)S(1)}, f32[64,1024]{1,0:T(8,128)}, u32[]{:S(2)}) copy-start(f32[64,1024]{1,0:T(8,128)} %elevation.1) | copy-start | bytes 786436
  0.7 17.4 %copy-start.3 = (s32[64,1024]{1,0:T(8,128)S(1)}, s32[64,1024]{1,0:T(8,128)}, u32[]{:S(2)}) copy-start(s32[64,1024]{1,0:T(8,128)} %roughness.1) | copy-start | bytes 786436
  2.8 9.7 %collective-permute-start = (f32[384,128]{1,0:T(8,128)}, f32[384,128]{1,0:T(8,128)S(1)}, u32[]{:S(2)}, u32[]{:S(2)}) collective-permute-start(f32[384,128]{1,0:T(8,128)} %get-tuple-element.36), channel_id=1, source_target_pairs={{0,1},{1,0},{2,3},{3,2},{4,5},{5,4},{6,7},{7,6},{8,9},{9,8},{10,11... | collective-permute-start | bytes 589832 | tf_op jit(solution)/shard_map/ppermute | solution.py:674
  4.7 8.7 %collective-permute-start.1 = (f32[384,128]{1,0:T(8,128)}, f32[384,128]{1,0:T(8,128)S(1)}, u32[]{:S(2)}, u32[]{:S(2)}) collective-permute-start(f32[384,128]{1,0:T(8,128)} %get-tuple-element.37), channel_id=1, source_target_pairs={{1,2},{2,1},{5,6},{6,5},{9,10},{10,9},{13,14},{14,13},{17,18},{18,... | collective-permute-start | bytes 589832 | tf_op jit(solution)/shard_map/ppermute | solution.py:675
  8.6 8.1 %collective-permute-start.4 = (f32[48,1024]{1,0:T(8,128)}, f32[48,1024]{1,0:T(8,128)S(1)}, u32[]{:S(2)}, u32[]{:S(2)}) collective-permute-start(f32[48,1024]{1,0:T(8,128)} %get-tuple-element.38), channel_id=1, source_target_pairs={{0,4},{4,0},{8,12},{12,8},{1,5},{5,1},{9,13},{13,9},{2,6},{6,2},{1... | collective-permute-start | bytes 589832 | tf_op jit(solution)/shard_map/ppermute | solution.py:662
  10.3 7.7 %collective-permute-start.5 = (f32[48,1024]{1,0:T(8,128)}, f32[48,1024]{1,0:T(8,128)S(1)}, u32[]{:S(2)}, u32[]{:S(2)}) collective-permute-start(f32[48,1024]{1,0:T(8,128)} %get-tuple-element.39), channel_id=1, source_target_pairs={{0,12},{4,8},{8,4},{12,0},{1,13},{5,9},{9,5},{13,1},{2,14},{6,10},... | collective-permute-start | bytes 589832 | tf_op jit(solution)/shard_map/ppermute | solution.py:662
  13.5 6.6 %collective-permute-start.3 = (f32[96,128]{1,0:T(8,128)S(1)}, f32[96,128]{1,0:T(8,128)S(1)}, u32[]{:S(2)}, u32[]{:S(2)}) collective-permute-start(f32[96,128]{1,0:T(8,128)S(1)} %get-tuple-element.74), channel_id=1, source_target_pairs={{0,12},{4,8},{8,4},{12,0},{1,13},{5,9},{9,5},{13,1},{2,14},{6,10},... | collective-permute-start | bytes 147464 | tf_op jit(solution)/shard_map/ppermute | solution.py:662
  16.6 4.1 %collective-permute-start.2 = (f32[96,128]{1,0:T(8,128)S(1)}, f32[96,128]{1,0:T(8,128)S(1)}, u32[]{:S(2)}, u32[]{:S(2)}) collective-permute-start(f32[96,128]{1,0:T(8,128)S(1)} %get-tuple-element.75), channel_id=1, source_target_pairs={{0,4},{4,0},{8,12},{12,8},{1,5},{5,1},{9,13},{13,9},{2,6},{6,2},{1... | collective-permute-start | bytes 147464 | tf_op jit(solution)/shard_map/ppermute | solution.py:662
  27.9 5.7 %collective-permute-start.6 = (f32[56,128]{1,0:T(8,128)S(1)}, f32[56,128]{1,0:T(8,128)S(1)}, u32[]{:S(2)}, u32[]{:S(2)}) collective-permute-start(f32[56,128]{1,0:T(8,128)S(1)} %get-tuple-element.57), channel_id=1, source_target_pairs={{0,32},{16,48},{32,64},{48,80},{64,96},{80,112},{96,0},{112,16},{1... | collective-permute-start | bytes 86024 | tf_op jit(solution)/shard_map/ppermute | solution.py:666
  29.4 5.4 %collective-permute-start.7 = (f32[56,128]{1,0:T(8,128)S(1)}, f32[56,128]{1,0:T(8,128)S(1)}, u32[]{:S(2)}, u32[]{:S(2)}) collective-permute-start(f32[56,128]{1,0:T(8,128)S(1)} %get-tuple-element.58), channel_id=1, source_target_pairs={{0,64},{16,80},{32,96},{48,112},{64,0},{80,16},{96,32},{112,48},{1... | collective-permute-start | bytes 86024 | tf_op jit(solution)/shard_map/ppermute | solution.py:666
  32.2 3.9 %collective-permute-start.8 = (f32[56,128]{1,0:T(8,128)S(1)}, f32[56,128]{1,0:T(8,128)S(1)}, u32[]{:S(2)}, u32[]{:S(2)}) collective-permute-start(f32[56,128]{1,0:T(8,128)S(1)} %get-tuple-element.59), channel_id=1, source_target_pairs={{0,96},{16,112},{32,0},{48,16},{64,32},{80,48},{96,64},{112,80},{1... | collective-permute-start | bytes 86024 | tf_op jit(solution)/shard_map/ppermute | solution.py:666
  36.0 6.4 %collective-permute-start.11 = (f32[216,128]{1,0:T(8,128)S(1)}, f32[216,128]{1,0:T(8,128)S(1)}, u32[]{:S(2)}, u32[]{:S(2)}) collective-permute-start(f32[216,128]{1,0:T(8,128)S(1)} %get-tuple-element.84), channel_id=1, source_target_pairs={{0,8},{4,12},{8,0},{12,4},{1,9},{5,13},{9,1},{13,5},{2,10},{6,14},... | collective-permute-start | bytes 331784 | tf_op jit(solution)/shard_map/ppermute | solution.py:662
  37.3 6.2 %collective-permute-start.10 = (f32[216,128]{1,0:T(8,128)S(1)}, f32[216,128]{1,0:T(8,128)S(1)}, u32[]{:S(2)}, u32[]{:S(2)}) collective-permute-start(f32[216,128]{1,0:T(8,128)S(1)} %get-tuple-element.84), channel_id=1, source_target_pairs={{0,12},{4,8},{8,4},{12,0},{1,13},{5,9},{9,5},{13,1},{2,14},{6,10},... | collective-permute-start | bytes 331784 | tf_op jit(solution)/shard_map/ppermute | solution.py:662
  38.9 4.7 %collective-permute-start.9 = (f32[216,128]{1,0:T(8,128)S(1)}, f32[216,128]{1,0:T(8,128)S(1)}, u32[]{:S(2)}, u32[]{:S(2)}) collective-permute-start(f32[216,128]{1,0:T(8,128)S(1)} %get-tuple-element.84), channel_id=1, source_target_pairs={{0,4},{4,0},{8,12},{12,8},{1,5},{5,1},{9,13},{13,9},{2,6},{6,2},{1... | collective-permute-start | bytes 331784 | tf_op jit(solution)/shard_map/ppermute | solution.py:662
  39.6 4.5 %collective-permute-start.12 = (f32[248,128]{1,0:T(8,128)S(1)}, f32[248,128]{1,0:T(8,128)S(1)}, u32[]{:S(2)}, u32[]{:S(2)}) collective-permute-start(f32[248,128]{1,0:T(8,128)S(1)} %constant_dynamic-update-slice_fusion.refs_0_), channel_id=1, source_target_pairs={{0,16},{16,0},{32,48},{48,32},{64,80},{80,64},{96,112},{112,96},{1... | collective-permute-start | bytes 380936 | tf_op jit(solution)/shard_map/ppermute | solution.py:692
  42.4 1.7 %collective-permute-start.15 = (f32[216,128]{1,0:T(8,128)S(1)}, f32[216,128]{1,0:T(8,128)S(1)}, u32[]{:S(2)}, u32[]{:S(2)}) collective-permute-start(f32[216,128]{1,0:T(8,128)S(1)} %collective-permute-done.11.refs_3_), channel_id=1, source_target_pairs={{0,16},{16,0},{32,48},{48,32},{64,80},{80,64},{96,112},{112,96},{1... | collective-permute-start | bytes 331784 | tf_op jit(solution)/shard_map/ppermute | solution.py:692
  43.6 1.3 %collective-permute-start.14 = (f32[216,128]{1,0:T(8,128)S(1)}, f32[216,128]{1,0:T(8,128)S(1)}, u32[]{:S(2)}, u32[]{:S(2)}) collective-permute-start(f32[216,128]{1,0:T(8,128)S(1)} %collective-permute-done.10.refs_2_), channel_id=1, source_target_pairs={{0,16},{16,0},{32,48},{48,32},{64,80},{80,64},{96,112},{112,96},{1... | collective-permute-start | bytes 331784 | tf_op jit(solution)/shard_map/ppermute | solution.py:692
  43.7 1.4 %collective-permute-start.13 = (f32[216,128]{1,0:T(8,128)S(1)}, f32[216,128]{1,0:T(8,128)S(1)}, u32[]{:S(2)}, u32[]{:S(2)}) collective-permute-start(f32[216,128]{1,0:T(8,128)S(1)} %collective-permute-done.9.refs_1_), channel_id=1, source_target_pairs={{0,16},{16,0},{32,48},{48,32},{64,80},{80,64},{96,112},{112,96},{1... | collective-permute-start | bytes 331784 | tf_op jit(solution)/shard_map/ppermute | solution.py:692
  47.0 8.0 %collective-permute-start.16 = (f32[72,128]{1,0:T(8,128)S(1)}, f32[72,128]{1,0:T(8,128)S(1)}, u32[]{:S(2)}, u32[]{:S(2)}) collective-permute-start(f32[72,128]{1,0:T(8,128)S(1)} %get-tuple-element.65), channel_id=1, source_target_pairs={{0,128},{16,144},{32,160},{48,176},{64,192},{80,208},{96,224},{112... | collective-permute-start | bytes 110600 | tf_op jit(solution)/shard_map/ppermute | solution.py:694
  55.0 1.2 %collective-permute-start.17 = (f32[72,128]{1,0:T(8,128)S(1)}, f32[72,128]{1,0:T(8,128)S(1)}, u32[]{:S(2)}, u32[]{:S(2)}) collective-permute-start(f32[72,128]{1,0:T(8,128)S(1)} %collective-permute-done.16.mine), channel_id=1, source_target_pairs={{0,16},{16,0},{32,48},{48,32},{64,80},{80,64},{96,112},{112,96},{1... | collective-permute-start | bytes 110600 | tf_op jit(solution)/shard_map/ppermute | solution.py:695
  56.2 5.1 %collective-permute-start.18 = (f32[48,128]{1,0:T(8,128)S(1)}, f32[48,128]{1,0:T(8,128)S(1)}, u32[]{:S(2)}, u32[]{:S(2)}) collective-permute-start(f32[48,128]{1,0:T(8,128)S(1)} %get-tuple-element.67), channel_id=1, source_target_pairs={{0,32},{16,48},{32,64},{48,80},{64,96},{80,112},{96,0},{112,16},{1... | collective-permute-start | bytes 73736 | tf_op jit(solution)/shard_map/ppermute | solution.py:666
  56.6 5.9 %collective-permute-start.19 = (f32[48,128]{1,0:T(8,128)S(1)}, f32[48,128]{1,0:T(8,128)S(1)}, u32[]{:S(2)}, u32[]{:S(2)}) collective-permute-start(f32[48,128]{1,0:T(8,128)S(1)} %get-tuple-element.68), channel_id=1, source_target_pairs={{0,64},{16,80},{32,96},{48,112},{64,0},{80,16},{96,32},{112,48},{1... | collective-permute-start | bytes 73736 | tf_op jit(solution)/shard_map/ppermute | solution.py:666
  60.4 3.8 %collective-permute-start.20 = (f32[48,128]{1,0:T(8,128)S(1)}, f32[48,128]{1,0:T(8,128)S(1)}, u32[]{:S(2)}, u32[]{:S(2)}) collective-permute-start(f32[48,128]{1,0:T(8,128)S(1)} %get-tuple-element.69), channel_id=1, source_target_pairs={{0,96},{16,112},{32,0},{48,16},{64,32},{80,48},{96,64},{112,80},{1... | collective-permute-start | bytes 73736 | tf_op jit(solution)/shard_map/ppermute | solution.py:666
  (5 other events, 46.5 us)

commit v4 on v3

--- a/solution.py
+++ b/solution.py
@@ -539,8 +539,12 @@
     near = pl.ds(near_start(row_place), NEAR)
     for field in range(3):
         state_s[NEAR * field : NEAR * field + NEAR, :] = all_s[field, near, :]
-    count = 3 * NEAR // 2
-    halfway[...] = state_s[pl.ds(pl.multiple_of(core * count, count), count), :]
+    lane = lax.broadcasted_iota(jnp.int32, (C_ROWS, 128), 1)
+    pieces = [state_s[C_ROWS * k : C_ROWS * k + C_ROWS, :] for k in range(9)]
+    for k in range(6):
+        guest = turn(pieces[6 + k // 3], 80 - 32 * (k % 3), 1)
+        halfway[C_ROWS * k : C_ROWS * k + C_ROWS, :] = jnp.where(lane < 96, turn(pieces[k], -16, 1), guest)
+    halfway[6 * C_ROWS : 7 * C_ROWS, :] = turn(pieces[8], -16, 1)
 
 
 def first_sweep(arrays):
@@ -555,7 +559,7 @@
             jax.ShapeDtypeStruct((8 * HALF, 128), F32),
             jax.ShapeDtypeStruct((3, TALL, 128), F32),
             field,
-            jax.ShapeDtypeStruct((3 * NEAR // 2, 128), F32),
+            jax.ShapeDtypeStruct((7 * C_ROWS, 128), F32),
         ),
         scratch_shapes=[
             pltpu.VMEM((8 * HALF, 128), F32),
@@ -567,7 +571,7 @@
     )(*arrays)
 
 
-def second_kernel(change, rain, ground, early, mine, twin, out0, out1, out2, out3, late, state_s):
+def second_kernel(change, rain, ground, early, halfway, out0, out1, out2, out3, late, state_s):
     row_place = lax.axis_index("sx")
     time_place = lax.axis_index("tm")
     z_place, x_place, core = time_place // 8, (time_place // 2) % 4, time_place % 2
@@ -575,9 +579,15 @@
 
     @pl.when(z_place == 1)
     def _():
-        count = 3 * NEAR // 2
-        state_s[pl.ds(pl.multiple_of(core * count, count), count), :] = mine[...]
-        state_s[pl.ds(pl.multiple_of((1 - core) * count, count), count), :] = twin[...]
+        lane = lax.broadcasted_iota(jnp.int32, (C_ROWS, 128), 1)
+        pieces = [halfway[C_ROWS * k : C_ROWS * k + C_ROWS, :] for k in range(7)]
+        for k in range(6):
+            state_s[C_ROWS * k : C_ROWS * k + C_ROWS, :] = turn(pieces[k], 16, 1)
+        for k in range(2):
+            a, b, c = (turn(pieces[3 * k + part], 32 * part - 80, 1) for part in range(3))
+            value = jnp.where(lane < 48, a, jnp.where(lane < 80, b, c))
+            state_s[C_ROWS * (6 + k) : C_ROWS * (7 + k), :] = value
+        state_s[8 * C_ROWS : 9 * C_ROWS, :] = turn(pieces[6], 16, 1)
         state = tuple(state_s[NEAR * field : NEAR * field + NEAR, :] for field in range(3))
         fixed = tuple(ground[field, pl.ds(top, NEAR), :] for field in range(3))
         sweep_slices(0, state, change, rain, fixed, late, top, NEAR)
@@ -594,17 +604,17 @@
             out[C_ROWS * field : C_ROWS * field + C_ROWS, :] = value
 
 
-def second_sweep(change, rain, ground, early, mine, twin):
+def second_sweep(change, rain, ground, early, halfway):
     vmem = pl.BlockSpec(memory_space=pltpu.VMEM)
     out = jax.ShapeDtypeStruct((FIELDS, 128), F32)
     return pl.pallas_call(
         second_kernel,
-        in_specs=[vmem] * 6,
+        in_specs=[vmem] * 5,
         out_specs=[vmem] * 4,
         out_shape=(out,) * 4,
         scratch_shapes=[pltpu.VMEM((3 * HALF, NEAR, 128), F32), pltpu.VMEM((3 * NEAR, 128), F32)],
         compiler_params=pltpu.CompilerParams(vmem_limit_bytes=VMEM_LIMIT),
-    )(change, rain, ground, early, mine, twin)
+    )(change, rain, ground, early, halfway)
 
 
 def finish_kernel(depth, flux, old, new0, new1, new2, new3, depth_out, flux_out, parts, spread):
@@ -692,8 +702,7 @@
     arrays = arrays + [lax.ppermute(part, "tm", sibling) for part in arrays]
     change, rain, ground, early, halfway = first_sweep(arrays)
     halfway = lax.ppermute(halfway, "tm", time_route(lambda z, x, core: (z + 1, x, core)))
-    twin = lax.ppermute(halfway, "tm", sibling)
-    news = second_sweep(change, rain, ground, early, halfway, twin)
+    news = second_sweep(change, rain, ground, early, halfway)
     news = [news[0]] + [over_x(news[d], d) for d in (1, 2, 3)]
     return finish(depth, flux, old, news)
 

time: 65.7 us -> 65 us (0.989)
  waiting for transfers between devices: 19.5 us -> 18.8 us
    ppermute x1 -> x0, waiting for transfers between devices: 1.21 us -> none  [on_device(): twin = lax.ppermute(halfway, 'tm', sibling)]
  transfers between devices with their start and end apart: 21 -> 20, of which waited for: 15 -> 14; matrix products, arithmetic and copies ran while one was open for 0% -> 0% of each run, Pallas kernels for 3% -> 3%
where the time goes in v4:
time: 65 us; the launch traced here: 64.9 us
  starting transfers between devices  30.5 us (47%)
  waiting for transfers between devices  18.8 us (29%)
  Pallas kernels  14.7 us (23%)
  between operations  0.81 us (1%)
    ppermute x7, starting transfers between devices, with_row(): return lax.ppermute(values, 'sx', [(i, i ^ flip) for i in range(4)])  10.7 us
    ppermute x6, starting transfers between devices, over_x(): lax.ppermute(values, 'tm', time_route(lambda z, x, core: (z, x + distance...  9.97 us
    pallas_call x1, Pallas kernels, fine(): pl.pallas_call(fine_kernel, in_specs=[smem] + [vmem] * 15, out_specs=[vme...  7.18 us
    ppermute x6, waiting for transfers between devices, over_x(): lax.ppermute(values, 'tm', time_route(lambda z, x, core: (z, x + distance...  6.18 us
    ppermute x7, waiting for transfers between devices, with_row(): return lax.ppermute(values, 'sx', [(i, i ^ flip) for i in range(4)])  5.81 us
    ppermute x1, waiting for transfers between devices, on_device(): lax.ppermute(halfway, 'tm', time_route(lambda z, x, core: (z + 1, x, core)))  4.85 us
    ppermute x1, starting transfers between devices, on_device(): second = lax.ppermute(second, 'sy', [(1, 2), (2, 1)])  3.89 us
    ppermute x1, starting transfers between devices, on_device(): lax.ppermute(halfway, 'tm', time_route(lambda z, x, core: (z + 1, x, core)))  3.59 us
  transfers between devices with their start and end apart: 20, of which 14 were waited for; matrix products, arithmetic and copies ran while one was open for 0% of the time, Pallas kernels for 3%

profile of v4, /device:TPU:32, one launch (start us, length us, event | category | flops | bytes accessed | tf_op | source)
XLA Modules:
  0.0 64.9 jit_solution(10740432304853971394)
XLA Ops:
  0.7 2.1 %shard_map.95 = (f32[384,128]{1,0:T(8,128)}, f32[384,128]{1,0:T(8,128)}, f32[48,1024]{1,0:T(8,128)}, f32[48,1024]{1,0:T(8,128)}) custom-call(f32[1,64,1024]{2,1,0:T(8,128)} %depth.1, f32[1,64,1024]{2,1,0:T(8,128)} %depth.1, f32[1,64,1024]{2,1,0:T(8,128)} %depth.1, f32[1,64,1024]{2,1,0:T(8,128)} %depth.1, f32[1,2,64,1024]{3,2,1,0:T(8,128)} %flux.1, ...), custom_call_target="tpu_custom_call" | custom-call | tf_op jit(solution)/shard_map/pallas_call | solution.py:143
  2.8 1.9 %collective-permute-start = (f32[384,128]{1,0:T(8,128)}, f32[384,128]{1,0:T(8,128)S(1)}, u32[]{:S(2)}, u32[]{:S(2)}) collective-permute-start(f32[384,128]{1,0:T(8,128)} %get-tuple-element.36), channel_id=1, source_target_pairs={{0,1},{1,0},{2,3},{3,2},{4,5},{5,4},{6,7},{7,6},{8,9},{9,8},{10,11... | collective-permute-start | bytes 589832 | tf_op jit(solution)/shard_map/ppermute | solution.py:684
  4.7 3.9 %collective-permute-start.1 = (f32[384,128]{1,0:T(8,128)}, f32[384,128]{1,0:T(8,128)S(1)}, u32[]{:S(2)}, u32[]{:S(2)}) collective-permute-start(f32[384,128]{1,0:T(8,128)} %get-tuple-element.37), channel_id=1, source_target_pairs={{1,2},{2,1},{5,6},{6,5},{9,10},{10,9},{13,14},{14,13},{17,18},{18,... | collective-permute-start | bytes 589832 | tf_op jit(solution)/shard_map/ppermute | solution.py:685
  8.6 1.7 %collective-permute-start.4 = (f32[48,1024]{1,0:T(8,128)}, f32[48,1024]{1,0:T(8,128)S(1)}, u32[]{:S(2)}, u32[]{:S(2)}) collective-permute-start(f32[48,1024]{1,0:T(8,128)} %get-tuple-element.38), channel_id=1, source_target_pairs={{0,4},{4,0},{8,12},{12,8},{1,5},{5,1},{9,13},{13,9},{2,6},{6,2},{1... | collective-permute-start | bytes 589832 | tf_op jit(solution)/shard_map/ppermute | solution.py:672
  10.3 2.2 %collective-permute-start.5 = (f32[48,1024]{1,0:T(8,128)}, f32[48,1024]{1,0:T(8,128)S(1)}, u32[]{:S(2)}, u32[]{:S(2)}) collective-permute-start(f32[48,1024]{1,0:T(8,128)} %get-tuple-element.39), channel_id=1, source_target_pairs={{0,12},{4,8},{8,4},{12,0},{1,13},{5,9},{9,5},{13,1},{2,14},{6,10},... | collective-permute-start | bytes 589832 | tf_op jit(solution)/shard_map/ppermute | solution.py:672
  13.5 3.1 %collective-permute-start.3 = (f32[96,128]{1,0:T(8,128)S(1)}, f32[96,128]{1,0:T(8,128)S(1)}, u32[]{:S(2)}, u32[]{:S(2)}) collective-permute-start(f32[96,128]{1,0:T(8,128)S(1)} %get-tuple-element.74), channel_id=1, source_target_pairs={{0,12},{4,8},{8,4},{12,0},{1,13},{5,9},{9,5},{13,1},{2,14},{6,10},... | collective-permute-start | bytes 147464 | tf_op jit(solution)/shard_map/ppermute | solution.py:672
  16.7 1.3 %collective-permute-done.5.row_b = f32[48,1024]{1,0:T(8,128)S(1)} collective-permute-done((f32[48,1024]{1,0:T(8,128)}, f32[48,1024]{1,0:T(8,128)S(1)}, u32[]{:S(2)}, u32[]{:S(2)}) %collective-permute-start.5) | collective-permute-done | bytes 196640 | tf_op jit(solution)/shard_map/ppermute | solution.py:672
  18.1 2.0 %shard_map.96 = (f32[96,1280]{1,0:T(8,128)S(1)}, f32[96,1280]{1,0:T(8,128)S(1)}, f32[96,1280]{1,0:T(8,128)S(1)}, f32[96,1280]{1,0:T(8,128)S(1)}, f32[96,1280]{1,...) custom-call(f32[8]{0:T(128)S(1)} %copy-done.6, ...), custom_call_target="tpu_custom_call" | custom-call | flops 40000000 | bytes 10000000 | tf_op jit(solution)/shard_map/pallas_call | solution.py:405
  20.7 7.2 %shard_map.97 = (f32[96,1280]{1,0:T(8,128)S(1)}, f32[96,1280]{1,0:T(8,128)S(1)}, f32[96,1280]{1,0:T(8,128)S(1)}, f32[96,1280]{1,0:T(8,128)S(1)}, f32[96,1280]{1,...) custom-call(f32[8]{0:T(128)S(1)} %copy-done.6, ...), custom_call_target="tpu_custom_call", output_to_operand_aliasing={{0}: (5, {}), {1}: (6, {}), {2}: (7, {}), {3}: (8, {}), {4}... | custom-call | tf_op jit(solution)/shard_map/pallas_call | solution.py:421
  27.9 1.6 %collective-permute-start.6 = (f32[56,128]{1,0:T(8,128)S(1)}, f32[56,128]{1,0:T(8,128)S(1)}, u32[]{:S(2)}, u32[]{:S(2)}) collective-permute-start(f32[56,128]{1,0:T(8,128)S(1)} %get-tuple-element.57), channel_id=1, source_target_pairs={{0,32},{16,48},{32,64},{48,80},{64,96},{80,112},{96,0},{112,16},{1... | collective-permute-start | bytes 86024 | tf_op jit(solution)/shard_map/ppermute | solution.py:676
  29.4 2.7 %collective-permute-start.7 = (f32[56,128]{1,0:T(8,128)S(1)}, f32[56,128]{1,0:T(8,128)S(1)}, u32[]{:S(2)}, u32[]{:S(2)}) collective-permute-start(f32[56,128]{1,0:T(8,128)S(1)} %get-tuple-element.58), channel_id=1, source_target_pairs={{0,64},{16,80},{32,96},{48,112},{64,0},{80,16},{96,32},{112,48},{1... | collective-permute-start | bytes 86024 | tf_op jit(solution)/shard_map/ppermute | solution.py:676
  32.2 1.4 %collective-permute-start.8 = (f32[56,128]{1,0:T(8,128)S(1)}, f32[56,128]{1,0:T(8,128)S(1)}, u32[]{:S(2)}, u32[]{:S(2)}) collective-permute-start(f32[56,128]{1,0:T(8,128)S(1)} %get-tuple-element.59), channel_id=1, source_target_pairs={{0,96},{16,112},{32,0},{48,16},{64,32},{80,48},{96,64},{112,80},{1... | collective-permute-start | bytes 86024 | tf_op jit(solution)/shard_map/ppermute | solution.py:676
  33.6 1.2 %collective-permute-done.7 = f32[56,128]{1,0:T(8,128)S(1)} collective-permute-done((f32[56,128]{1,0:T(8,128)S(1)}, f32[56,128]{1,0:T(8,128)S(1)}, u32[]{:S(2)}, u32[]{:S(2)}) %collective-permute-start.7) | collective-permute-done | bytes 28704 | tf_op jit(solution)/shard_map/ppermute | solution.py:676
  34.8 1.2 %collective-permute-done.8 = f32[56,128]{1,0:T(8,128)S(1)} collective-permute-done((f32[56,128]{1,0:T(8,128)S(1)}, f32[56,128]{1,0:T(8,128)S(1)}, u32[]{:S(2)}, u32[]{:S(2)}) %collective-permute-start.8) | collective-permute-done | bytes 28704 | tf_op jit(solution)/shard_map/ppermute | solution.py:676
  36.0 1.3 %collective-permute-start.11 = (f32[216,128]{1,0:T(8,128)S(1)}, f32[216,128]{1,0:T(8,128)S(1)}, u32[]{:S(2)}, u32[]{:S(2)}) collective-permute-start(f32[216,128]{1,0:T(8,128)S(1)} %get-tuple-element.84), channel_id=1, source_target_pairs={{0,8},{4,12},{8,0},{12,4},{1,9},{5,13},{9,1},{13,5},{2,10},{6,14},... | collective-permute-start | bytes 331784 | tf_op jit(solution)/shard_map/ppermute | solution.py:672
  37.3 1.6 %collective-permute-start.10 = (f32[216,128]{1,0:T(8,128)S(1)}, f32[216,128]{1,0:T(8,128)S(1)}, u32[]{:S(2)}, u32[]{:S(2)}) collective-permute-start(f32[216,128]{1,0:T(8,128)S(1)} %get-tuple-element.84), channel_id=1, source_target_pairs={{0,12},{4,8},{8,4},{12,0},{1,13},{5,9},{9,5},{13,1},{2,14},{6,10},... | collective-permute-start | bytes 331784 | tf_op jit(solution)/shard_map/ppermute | solution.py:672
  39.7 2.7 %collective-permute-done.11.refs_3_ = f32[216,128]{1,0:T(8,128)S(1)} collective-permute-done((f32[216,128]{1,0:T(8,128)S(1)}, f32[216,128]{1,0:T(8,128)S(1)}, u32[]{:S(2)}, u32[]{:S(2)}) %collective-permute-start.11) | collective-permute-done | bytes 110624 | tf_op jit(solution)/shard_map/ppermute | solution.py:672
  42.4 1.2 %collective-permute-done.10.refs_2_ = f32[216,128]{1,0:T(8,128)S(1)} collective-permute-done((f32[216,128]{1,0:T(8,128)S(1)}, f32[216,128]{1,0:T(8,128)S(1)}, u32[]{:S(2)}, u32[]{:S(2)}) %collective-permute-start.10) | collective-permute-done | bytes 110624 | tf_op jit(solution)/shard_map/ppermute | solution.py:672
  45.0 2.0 %shard_map.98 = (f32[24,64,128]{2,1,0:T(8,128)S(1)}, f32[64,128]{1,0:T(8,128)S(1)}, f32[3,64,128]{2,1,0:T(8,128)S(1)}, f32[24,64,128]{2,1,0:T(8,128)S(1)}, f32[112,128]{1,0:T(8,128)S(1)}) custom-call(f32[248,128]{1,0:T(8,128)S(1)} %constant_dynamic-update-slice_fusion.refs_0_, f32[216,128]{1,0:T(8,128)S(1)} %collective-permute-done.9.refs_1_, ...), custom_call_target="tpu_custom_call" | custom-call | tf_op jit(solution)/shard_map/pallas_call | solution.py:553
  47.1 3.6 %collective-permute-start.16 = (f32[112,128]{1,0:T(8,128)S(1)}, f32[112,128]{1,0:T(8,128)S(1)}, u32[]{:S(2)}, u32[]{:S(2)}) collective-permute-start(f32[112,128]{1,0:T(8,128)S(1)} %get-tuple-element.65), channel_id=1, source_target_pairs={{0,128},{16,144},{32,160},{48,176},{64,192},{80,208},{96,224},{112... | collective-permute-start | bytes 172040 | tf_op jit(solution)/shard_map/ppermute | solution.py:704
  50.7 4.8 %collective-permute-done.16.halfway = f32[112,128]{1,0:T(8,128)S(1)} collective-permute-done((f32[112,128]{1,0:T(8,128)S(1)}, f32[112,128]{1,0:T(8,128)S(1)}, u32[]{:S(2)}, u32[]{:S(2)}) %collective-permute-start.16) | collective-permute-done | bytes 57376 | tf_op jit(solution)/shard_map/ppermute | solution.py:704
  55.9 3.8 %collective-permute-start.18 = (f32[48,128]{1,0:T(8,128)S(1)}, f32[48,128]{1,0:T(8,128)S(1)}, u32[]{:S(2)}, u32[]{:S(2)}) collective-permute-start(f32[48,128]{1,0:T(8,128)S(1)} %get-tuple-element.68), channel_id=1, source_target_pairs={{0,64},{16,80},{32,96},{48,112},{64,0},{80,16},{96,32},{112,48},{1... | collective-permute-start | bytes 73736 | tf_op jit(solution)/shard_map/ppermute | solution.py:676
  61.8 1.8 %collective-permute-done.19.new3 = f32[48,128]{1,0:T(8,128)S(1)} collective-permute-done((f32[48,128]{1,0:T(8,128)S(1)}, f32[48,128]{1,0:T(8,128)S(1)}, u32[]{:S(2)}, u32[]{:S(2)}) %collective-permute-start.19) | collective-permute-done | bytes 24608 | tf_op jit(solution)/shard_map/ppermute | solution.py:676
  63.5 1.3 %shard_map.100 = (f32[1,64,1024]{2,1,0:T(8,128)}, f32[1,2,64,1024]{3,2,1,0:T(8,128)}) custom-call(f32[1,64,1024]{2,1,0:T(8,128)S(1)} %get-tuple-element.53.depth, f32[1,2,64,1024]{3,2,1,0:T(8,128)S(1)} %get-tuple-element.54.flux, f32[48,256]{1,0:T(8,128)S(1)} %get-tuple-element.55.old, f32[48,128]{1,0:T(8,128)S(1)} %get-tuple-element.66.new0, ...), custom_call_target="tpu_custom_call" | custom-call | tf_op jit(solution)/shard_map/pallas_call | solution.py:653
  (50 shorter events, 6.4 us)
Async XLA Ops:
  0.6 17.4 %copy-start = (f32[1,2,64,1024]{3,2,1,0:T(8,128)S(1)}, f32[1,2,64,1024]{3,2,1,0:T(8,128)}, u32[]{:S(2)}) copy-start(f32[1,2,64,1024]{3,2,1,0:T(8,128)} %flux.1) | copy-start | bytes 1572868
  0.6 17.4 %copy-start.2 = (f32[64,1024]{1,0:T(8,128)S(1)}, f32[64,1024]{1,0:T(8,128)}, u32[]{:S(2)}) copy-start(f32[64,1024]{1,0:T(8,128)} %elevation.1) | copy-start | bytes 786436
  0.7 17.4 %copy-start.3 = (s32[64,1024]{1,0:T(8,128)S(1)}, s32[64,1024]{1,0:T(8,128)}, u32[]{:S(2)}) copy-start(s32[64,1024]{1,0:T(8,128)} %roughness.1) | copy-start | bytes 786436
  0.7 17.4 %copy-start.4 = (s32[64,1024]{1,0:T(8,128)S(1)}, s32[64,1024]{1,0:T(8,128)}, u32[]{:S(2)}) copy-start(s32[64,1024]{1,0:T(8,128)} %building.1) | copy-start | bytes 786436
  2.8 9.7 %collective-permute-start = (f32[384,128]{1,0:T(8,128)}, f32[384,128]{1,0:T(8,128)S(1)}, u32[]{:S(2)}, u32[]{:S(2)}) collective-permute-start(f32[384,128]{1,0:T(8,128)} %get-tuple-element.36), channel_id=1, source_target_pairs={{0,1},{1,0},{2,3},{3,2},{4,5},{5,4},{6,7},{7,6},{8,9},{9,8},{10,11... | collective-permute-start | bytes 589832 | tf_op jit(solution)/shard_map/ppermute | solution.py:684
  4.7 8.7 %collective-permute-start.1 = (f32[384,128]{1,0:T(8,128)}, f32[384,128]{1,0:T(8,128)S(1)}, u32[]{:S(2)}, u32[]{:S(2)}) collective-permute-start(f32[384,128]{1,0:T(8,128)} %get-tuple-element.37), channel_id=1, source_target_pairs={{1,2},{2,1},{5,6},{6,5},{9,10},{10,9},{13,14},{14,13},{17,18},{18,... | collective-permute-start | bytes 589832 | tf_op jit(solution)/shard_map/ppermute | solution.py:685
  8.6 8.1 %collective-permute-start.4 = (f32[48,1024]{1,0:T(8,128)}, f32[48,1024]{1,0:T(8,128)S(1)}, u32[]{:S(2)}, u32[]{:S(2)}) collective-permute-start(f32[48,1024]{1,0:T(8,128)} %get-tuple-element.38), channel_id=1, source_target_pairs={{0,4},{4,0},{8,12},{12,8},{1,5},{5,1},{9,13},{13,9},{2,6},{6,2},{1... | collective-permute-start | bytes 589832 | tf_op jit(solution)/shard_map/ppermute | solution.py:672
  10.3 7.7 %collective-permute-start.5 = (f32[48,1024]{1,0:T(8,128)}, f32[48,1024]{1,0:T(8,128)S(1)}, u32[]{:S(2)}, u32[]{:S(2)}) collective-permute-start(f32[48,1024]{1,0:T(8,128)} %get-tuple-element.39), channel_id=1, source_target_pairs={{0,12},{4,8},{8,4},{12,0},{1,13},{5,9},{9,5},{13,1},{2,14},{6,10},... | collective-permute-start | bytes 589832 | tf_op jit(solution)/shard_map/ppermute | solution.py:672
  13.5 6.6 %collective-permute-start.3 = (f32[96,128]{1,0:T(8,128)S(1)}, f32[96,128]{1,0:T(8,128)S(1)}, u32[]{:S(2)}, u32[]{:S(2)}) collective-permute-start(f32[96,128]{1,0:T(8,128)S(1)} %get-tuple-element.74), channel_id=1, source_target_pairs={{0,12},{4,8},{8,4},{12,0},{1,13},{5,9},{9,5},{13,1},{2,14},{6,10},... | collective-permute-start | bytes 147464 | tf_op jit(solution)/shard_map/ppermute | solution.py:672
  16.6 4.1 %collective-permute-start.2 = (f32[96,128]{1,0:T(8,128)S(1)}, f32[96,128]{1,0:T(8,128)S(1)}, u32[]{:S(2)}, u32[]{:S(2)}) collective-permute-start(f32[96,128]{1,0:T(8,128)S(1)} %get-tuple-element.75), channel_id=1, source_target_pairs={{0,4},{4,0},{8,12},{12,8},{1,5},{5,1},{9,13},{13,9},{2,6},{6,2},{1... | collective-permute-start | bytes 147464 | tf_op jit(solution)/shard_map/ppermute | solution.py:672
  27.9 5.7 %collective-permute-start.6 = (f32[56,128]{1,0:T(8,128)S(1)}, f32[56,128]{1,0:T(8,128)S(1)}, u32[]{:S(2)}, u32[]{:S(2)}) collective-permute-start(f32[56,128]{1,0:T(8,128)S(1)} %get-tuple-element.57), channel_id=1, source_target_pairs={{0,32},{16,48},{32,64},{48,80},{64,96},{80,112},{96,0},{112,16},{1... | collective-permute-start | bytes 86024 | tf_op jit(solution)/shard_map/ppermute | solution.py:676
  29.4 5.4 %collective-permute-start.7 = (f32[56,128]{1,0:T(8,128)S(1)}, f32[56,128]{1,0:T(8,128)S(1)}, u32[]{:S(2)}, u32[]{:S(2)}) collective-permute-start(f32[56,128]{1,0:T(8,128)S(1)} %get-tuple-element.58), channel_id=1, source_target_pairs={{0,64},{16,80},{32,96},{48,112},{64,0},{80,16},{96,32},{112,48},{1... | collective-permute-start | bytes 86024 | tf_op jit(solution)/shard_map/ppermute | solution.py:676
  32.2 3.9 %collective-permute-start.8 = (f32[56,128]{1,0:T(8,128)S(1)}, f32[56,128]{1,0:T(8,128)S(1)}, u32[]{:S(2)}, u32[]{:S(2)}) collective-permute-start(f32[56,128]{1,0:T(8,128)S(1)} %get-tuple-element.59), channel_id=1, source_target_pairs={{0,96},{16,112},{32,0},{48,16},{64,32},{80,48},{96,64},{112,80},{1... | collective-permute-start | bytes 86024 | tf_op jit(solution)/shard_map/ppermute | solution.py:676
  36.0 6.4 %collective-permute-start.11 = (f32[216,128]{1,0:T(8,128)S(1)}, f32[216,128]{1,0:T(8,128)S(1)}, u32[]{:S(2)}, u32[]{:S(2)}) collective-permute-start(f32[216,128]{1,0:T(8,128)S(1)} %get-tuple-element.84), channel_id=1, source_target_pairs={{0,8},{4,12},{8,0},{12,4},{1,9},{5,13},{9,1},{13,5},{2,10},{6,14},... | collective-permute-start | bytes 331784 | tf_op jit(solution)/shard_map/ppermute | solution.py:672
  37.3 6.2 %collective-permute-start.10 = (f32[216,128]{1,0:T(8,128)S(1)}, f32[216,128]{1,0:T(8,128)S(1)}, u32[]{:S(2)}, u32[]{:S(2)}) collective-permute-start(f32[216,128]{1,0:T(8,128)S(1)} %get-tuple-element.84), channel_id=1, source_target_pairs={{0,12},{4,8},{8,4},{12,0},{1,13},{5,9},{9,5},{13,1},{2,14},{6,10},... | collective-permute-start | bytes 331784 | tf_op jit(solution)/shard_map/ppermute | solution.py:672
  38.9 4.7 %collective-permute-start.9 = (f32[216,128]{1,0:T(8,128)S(1)}, f32[216,128]{1,0:T(8,128)S(1)}, u32[]{:S(2)}, u32[]{:S(2)}) collective-permute-start(f32[216,128]{1,0:T(8,128)S(1)} %get-tuple-element.84), channel_id=1, source_target_pairs={{0,4},{4,0},{8,12},{12,8},{1,5},{5,1},{9,13},{13,9},{2,6},{6,2},{1... | collective-permute-start | bytes 331784 | tf_op jit(solution)/shard_map/ppermute | solution.py:672
  39.6 4.5 %collective-permute-start.12 = (f32[248,128]{1,0:T(8,128)S(1)}, f32[248,128]{1,0:T(8,128)S(1)}, u32[]{:S(2)}, u32[]{:S(2)}) collective-permute-start(f32[248,128]{1,0:T(8,128)S(1)} %constant_dynamic-update-slice_fusion.refs_0_), channel_id=1, source_target_pairs={{0,16},{16,0},{32,48},{48,32},{64,80},{80,64},{96,112},{112,96},{1... | collective-permute-start | bytes 380936 | tf_op jit(solution)/shard_map/ppermute | solution.py:702
  42.4 1.7 %collective-permute-start.15 = (f32[216,128]{1,0:T(8,128)S(1)}, f32[216,128]{1,0:T(8,128)S(1)}, u32[]{:S(2)}, u32[]{:S(2)}) collective-permute-start(f32[216,128]{1,0:T(8,128)S(1)} %collective-permute-done.11.refs_3_), channel_id=1, source_target_pairs={{0,16},{16,0},{32,48},{48,32},{64,80},{80,64},{96,112},{112,96},{1... | collective-permute-start | bytes 331784 | tf_op jit(solution)/shard_map/ppermute | solution.py:702
  43.6 1.3 %collective-permute-start.14 = (f32[216,128]{1,0:T(8,128)S(1)}, f32[216,128]{1,0:T(8,128)S(1)}, u32[]{:S(2)}, u32[]{:S(2)}) collective-permute-start(f32[216,128]{1,0:T(8,128)S(1)} %collective-permute-done.10.refs_2_), channel_id=1, source_target_pairs={{0,16},{16,0},{32,48},{48,32},{64,80},{80,64},{96,112},{112,96},{1... | collective-permute-start | bytes 331784 | tf_op jit(solution)/shard_map/ppermute | solution.py:702
  43.7 1.4 %collective-permute-start.13 = (f32[216,128]{1,0:T(8,128)S(1)}, f32[216,128]{1,0:T(8,128)S(1)}, u32[]{:S(2)}, u32[]{:S(2)}) collective-permute-start(f32[216,128]{1,0:T(8,128)S(1)} %collective-permute-done.9.refs_1_), channel_id=1, source_target_pairs={{0,16},{16,0},{32,48},{48,32},{64,80},{80,64},{96,112},{112,96},{1... | collective-permute-start | bytes 331784 | tf_op jit(solution)/shard_map/ppermute | solution.py:702
  47.1 8.4 %collective-permute-start.16 = (f32[112,128]{1,0:T(8,128)S(1)}, f32[112,128]{1,0:T(8,128)S(1)}, u32[]{:S(2)}, u32[]{:S(2)}) collective-permute-start(f32[112,128]{1,0:T(8,128)S(1)} %get-tuple-element.65), channel_id=1, source_target_pairs={{0,128},{16,144},{32,160},{48,176},{64,192},{80,208},{96,224},{112... | collective-permute-start | bytes 172040 | tf_op jit(solution)/shard_map/ppermute | solution.py:704
  55.5 5.4 %collective-permute-start.17 = (f32[48,128]{1,0:T(8,128)S(1)}, f32[48,128]{1,0:T(8,128)S(1)}, u32[]{:S(2)}, u32[]{:S(2)}) collective-permute-start(f32[48,128]{1,0:T(8,128)S(1)} %get-tuple-element.67), channel_id=1, source_target_pairs={{0,32},{16,48},{32,64},{48,80},{64,96},{80,112},{96,0},{112,16},{1... | collective-permute-start | bytes 73736 | tf_op jit(solution)/shard_map/ppermute | solution.py:676
  55.9 5.9 %collective-permute-start.18 = (f32[48,128]{1,0:T(8,128)S(1)}, f32[48,128]{1,0:T(8,128)S(1)}, u32[]{:S(2)}, u32[]{:S(2)}) collective-permute-start(f32[48,128]{1,0:T(8,128)S(1)} %get-tuple-element.68), channel_id=1, source_target_pairs={{0,64},{16,80},{32,96},{48,112},{64,0},{80,16},{96,32},{112,48},{1... | collective-permute-start | bytes 73736 | tf_op jit(solution)/shard_map/ppermute | solution.py:676
  59.7 3.8 %collective-permute-start.19 = (f32[48,128]{1,0:T(8,128)S(1)}, f32[48,128]{1,0:T(8,128)S(1)}, u32[]{:S(2)}, u32[]{:S(2)}) collective-permute-start(f32[48,128]{1,0:T(8,128)S(1)} %get-tuple-element.69), channel_id=1, source_target_pairs={{0,96},{16,112},{32,0},{48,16},{64,32},{80,48},{96,64},{112,80},{1... | collective-permute-start | bytes 73736 | tf_op jit(solution)/shard_map/ppermute | solution.py:676
  (4 other events, 29.1 us)

commit v5 on v4

--- a/solution.py
+++ b/solution.py
@@ -280,6 +280,10 @@
     restrict(sources, lambda source, cols: source[16:80, cols], ((8, 0, 16),), pooled, coarse)
     for k in range(1, 8):
         set_faces(k, elev, friction, opened, sill_x, drag_x, sill_y, drag_y)
+        rows, out = pl.ds(8 + 8 * k, 8), pl.ds(8 * k, 8)
+        level[rows, :] = level[rows, :] + elev[rows, :]
+        flow_x[rows, :] = jnp.where(sill_x[out, :] < CLOSED, flow_x[rows, :], 0.0)
+        flow_y[rows, :] = jnp.where(sill_y[out, :] < CLOSED, flow_y[rows, :], 0.0)
 
 
 def fine_kernel(*refs):
@@ -315,7 +319,7 @@
     restrict(sources, take, ((6, 0, 2), (24, 8, 2)), pooled, coarse)
     for k in (0, 8, 9):
         set_faces(k, elev, friction, opened, sill_x, drag_x, sill_y, drag_y)
-    for k in range(10):
+    for k in (0, 8, 9):
         rows, out = pl.ds(8 + 8 * k, 8), pl.ds(8 * k, 8)
         level[rows, :] = level[rows, :] + elev[rows, :]
         flow_x[rows, :] = jnp.where(sill_x[out, :] < CLOSED, flow_x[rows, :], 0.0)
@@ -635,7 +639,7 @@
     scale = jnp.where(
         lax.broadcasted_iota(jnp.int32, (3 * C_ROWS, C_COLS), 0) < C_ROWS, 1.0 / SCALE, 1.0 / FLOW_SCALE
     )
-    spread[...] = split_dot(scale * delta, copies)
+    spread[...] = split_dot(scale * delta, copies, 2)
     low = lax.broadcasted_iota(jnp.int32, (8, COLS), 0) < 4
     for field in range(3):
         for k in range(ROWS // 8):

time: 65 us -> 64.9 us (level)
  no operation moved by 1% of the time
where the time goes in v5:
time: 64.9 us; the launch traced here: 64.8 us
  starting transfers between devices  30.5 us (47%)
  waiting for transfers between devices  18.7 us (29%)
  Pallas kernels  14.7 us (23%)
  between operations  0.81 us (1%)
    ppermute x7, starting transfers between devices, with_row(): return lax.ppermute(values, 'sx', [(i, i ^ flip) for i in range(4)])  10.7 us
    ppermute x6, starting transfers between devices, over_x(): lax.ppermute(values, 'tm', time_route(lambda z, x, core: (z, x + distance...  9.97 us
    pallas_call x1, Pallas kernels, fine(): pl.pallas_call(fine_kernel, in_specs=[smem] + [vmem] * 15, out_specs=[vme...  7.16 us
    ppermute x6, waiting for transfers between devices, over_x(): lax.ppermute(values, 'tm', time_route(lambda z, x, core: (z, x + distance...  6.19 us
    ppermute x7, waiting for transfers between devices, with_row(): return lax.ppermute(values, 'sx', [(i, i ^ flip) for i in range(4)])  5.77 us
    ppermute x1, waiting for transfers between devices, on_device(): lax.ppermute(halfway, 'tm', time_route(lambda z, x, core: (z + 1, x, core)))  4.85 us
    ppermute x1, starting transfers between devices, on_device(): second = lax.ppermute(second, 'sy', [(1, 2), (2, 1)])  3.89 us
    ppermute x1, starting transfers between devices, on_device(): lax.ppermute(halfway, 'tm', time_route(lambda z, x, core: (z + 1, x, core)))  3.59 us
  transfers between devices with their start and end apart: 20, of which 14 were waited for; matrix products, arithmetic and copies ran while one was open for 0% of the time, Pallas kernels for 3%

profile of v5, /device:TPU:32, one launch (start us, length us, event | category | flops | bytes accessed | tf_op | source)
XLA Modules:
  0.0 64.8 jit_solution(5446997702301000823)
XLA Ops:
  0.7 2.1 %shard_map.95 = (f32[384,128]{1,0:T(8,128)}, f32[384,128]{1,0:T(8,128)}, f32[48,1024]{1,0:T(8,128)}, f32[48,1024]{1,0:T(8,128)}) custom-call(f32[1,64,1024]{2,1,0:T(8,128)} %depth.1, f32[1,64,1024]{2,1,0:T(8,128)} %depth.1, f32[1,64,1024]{2,1,0:T(8,128)} %depth.1, f32[1,64,1024]{2,1,0:T(8,128)} %depth.1, f32[1,2,64,1024]{3,2,1,0:T(8,128)} %flux.1, ...), custom_call_target="tpu_custom_call" | custom-call | tf_op jit(solution)/shard_map/pallas_call | solution.py:143
  2.8 1.9 %collective-permute-start = (f32[384,128]{1,0:T(8,128)}, f32[384,128]{1,0:T(8,128)S(1)}, u32[]{:S(2)}, u32[]{:S(2)}) collective-permute-start(f32[384,128]{1,0:T(8,128)} %get-tuple-element.36), channel_id=1, source_target_pairs={{0,1},{1,0},{2,3},{3,2},{4,5},{5,4},{6,7},{7,6},{8,9},{9,8},{10,11... | collective-permute-start | bytes 589832 | tf_op jit(solution)/shard_map/ppermute | solution.py:688
  4.7 3.9 %collective-permute-start.1 = (f32[384,128]{1,0:T(8,128)}, f32[384,128]{1,0:T(8,128)S(1)}, u32[]{:S(2)}, u32[]{:S(2)}) collective-permute-start(f32[384,128]{1,0:T(8,128)} %get-tuple-element.37), channel_id=1, source_target_pairs={{1,2},{2,1},{5,6},{6,5},{9,10},{10,9},{13,14},{14,13},{17,18},{18,... | collective-permute-start | bytes 589832 | tf_op jit(solution)/shard_map/ppermute | solution.py:689
  8.6 1.7 %collective-permute-start.4 = (f32[48,1024]{1,0:T(8,128)}, f32[48,1024]{1,0:T(8,128)S(1)}, u32[]{:S(2)}, u32[]{:S(2)}) collective-permute-start(f32[48,1024]{1,0:T(8,128)} %get-tuple-element.38), channel_id=1, source_target_pairs={{0,4},{4,0},{8,12},{12,8},{1,5},{5,1},{9,13},{13,9},{2,6},{6,2},{1... | collective-permute-start | bytes 589832 | tf_op jit(solution)/shard_map/ppermute | solution.py:676
  10.3 2.2 %collective-permute-start.5 = (f32[48,1024]{1,0:T(8,128)}, f32[48,1024]{1,0:T(8,128)S(1)}, u32[]{:S(2)}, u32[]{:S(2)}) collective-permute-start(f32[48,1024]{1,0:T(8,128)} %get-tuple-element.39), channel_id=1, source_target_pairs={{0,12},{4,8},{8,4},{12,0},{1,13},{5,9},{9,5},{13,1},{2,14},{6,10},... | collective-permute-start | bytes 589832 | tf_op jit(solution)/shard_map/ppermute | solution.py:676
  13.5 3.1 %collective-permute-start.3 = (f32[96,128]{1,0:T(8,128)S(1)}, f32[96,128]{1,0:T(8,128)S(1)}, u32[]{:S(2)}, u32[]{:S(2)}) collective-permute-start(f32[96,128]{1,0:T(8,128)S(1)} %get-tuple-element.74), channel_id=1, source_target_pairs={{0,12},{4,8},{8,4},{12,0},{1,13},{5,9},{9,5},{13,1},{2,14},{6,10},... | collective-permute-start | bytes 147464 | tf_op jit(solution)/shard_map/ppermute | solution.py:676
  16.7 1.3 %collective-permute-done.5.row_b = f32[48,1024]{1,0:T(8,128)S(1)} collective-permute-done((f32[48,1024]{1,0:T(8,128)}, f32[48,1024]{1,0:T(8,128)S(1)}, u32[]{:S(2)}, u32[]{:S(2)}) %collective-permute-start.5) | collective-permute-done | bytes 196640 | tf_op jit(solution)/shard_map/ppermute | solution.py:676
  18.1 2.1 %shard_map.96 = (f32[96,1280]{1,0:T(8,128)S(1)}, f32[96,1280]{1,0:T(8,128)S(1)}, f32[96,1280]{1,0:T(8,128)S(1)}, f32[96,1280]{1,0:T(8,128)S(1)}, f32[96,1280]{1,...) custom-call(f32[8]{0:T(128)S(1)} %copy-done.6, ...), custom_call_target="tpu_custom_call" | custom-call | flops 40000000 | bytes 10000000 | tf_op jit(solution)/shard_map/pallas_call | solution.py:409
  20.7 7.2 %shard_map.97 = (f32[96,1280]{1,0:T(8,128)S(1)}, f32[96,1280]{1,0:T(8,128)S(1)}, f32[96,1280]{1,0:T(8,128)S(1)}, f32[96,1280]{1,0:T(8,128)S(1)}, f32[96,1280]{1,...) custom-call(f32[8]{0:T(128)S(1)} %copy-done.6, ...), custom_call_target="tpu_custom_call", output_to_operand_aliasing={{0}: (5, {}), {1}: (6, {}), {2}: (7, {}), {3}: (8, {}), {4}... | custom-call | tf_op jit(solution)/shard_map/pallas_call | solution.py:425
  27.8 1.6 %collective-permute-start.6 = (f32[56,128]{1,0:T(8,128)S(1)}, f32[56,128]{1,0:T(8,128)S(1)}, u32[]{:S(2)}, u32[]{:S(2)}) collective-permute-start(f32[56,128]{1,0:T(8,128)S(1)} %get-tuple-element.57), channel_id=1, source_target_pairs={{0,32},{16,48},{32,64},{48,80},{64,96},{80,112},{96,0},{112,16},{1... | collective-permute-start | bytes 86024 | tf_op jit(solution)/shard_map/ppermute | solution.py:680
  29.4 2.7 %collective-permute-start.7 = (f32[56,128]{1,0:T(8,128)S(1)}, f32[56,128]{1,0:T(8,128)S(1)}, u32[]{:S(2)}, u32[]{:S(2)}) collective-permute-start(f32[56,128]{1,0:T(8,128)S(1)} %get-tuple-element.58), channel_id=1, source_target_pairs={{0,64},{16,80},{32,96},{48,112},{64,0},{80,16},{96,32},{112,48},{1... | collective-permute-start | bytes 86024 | tf_op jit(solution)/shard_map/ppermute | solution.py:680
  32.1 1.4 %collective-permute-start.8 = (f32[56,128]{1,0:T(8,128)S(1)}, f32[56,128]{1,0:T(8,128)S(1)}, u32[]{:S(2)}, u32[]{:S(2)}) collective-permute-start(f32[56,128]{1,0:T(8,128)S(1)} %get-tuple-element.59), channel_id=1, source_target_pairs={{0,96},{16,112},{32,0},{48,16},{64,32},{80,48},{96,64},{112,80},{1... | collective-permute-start | bytes 86024 | tf_op jit(solution)/shard_map/ppermute | solution.py:680
  33.6 1.2 %collective-permute-done.7 = f32[56,128]{1,0:T(8,128)S(1)} collective-permute-done((f32[56,128]{1,0:T(8,128)S(1)}, f32[56,128]{1,0:T(8,128)S(1)}, u32[]{:S(2)}, u32[]{:S(2)}) %collective-permute-start.7) | collective-permute-done | bytes 28704 | tf_op jit(solution)/shard_map/ppermute | solution.py:680
  34.8 1.2 %collective-permute-done.8 = f32[56,128]{1,0:T(8,128)S(1)} collective-permute-done((f32[56,128]{1,0:T(8,128)S(1)}, f32[56,128]{1,0:T(8,128)S(1)}, u32[]{:S(2)}, u32[]{:S(2)}) %collective-permute-start.8) | collective-permute-done | bytes 28704 | tf_op jit(solution)/shard_map/ppermute | solution.py:680
  36.0 1.4 %collective-permute-start.11 = (f32[216,128]{1,0:T(8,128)S(1)}, f32[216,128]{1,0:T(8,128)S(1)}, u32[]{:S(2)}, u32[]{:S(2)}) collective-permute-start(f32[216,128]{1,0:T(8,128)S(1)} %get-tuple-element.84), channel_id=1, source_target_pairs={{0,8},{4,12},{8,0},{12,4},{1,9},{5,13},{9,1},{13,5},{2,10},{6,14},... | collective-permute-start | bytes 331784 | tf_op jit(solution)/shard_map/ppermute | solution.py:676
  37.4 1.6 %collective-permute-start.10 = (f32[216,128]{1,0:T(8,128)S(1)}, f32[216,128]{1,0:T(8,128)S(1)}, u32[]{:S(2)}, u32[]{:S(2)}) collective-permute-start(f32[216,128]{1,0:T(8,128)S(1)} %get-tuple-element.84), channel_id=1, source_target_pairs={{0,12},{4,8},{8,4},{12,0},{1,13},{5,9},{9,5},{13,1},{2,14},{6,10},... | collective-permute-start | bytes 331784 | tf_op jit(solution)/shard_map/ppermute | solution.py:676
  39.7 2.7 %collective-permute-done.11.refs_3_ = f32[216,128]{1,0:T(8,128)S(1)} collective-permute-done((f32[216,128]{1,0:T(8,128)S(1)}, f32[216,128]{1,0:T(8,128)S(1)}, u32[]{:S(2)}, u32[]{:S(2)}) %collective-permute-start.11) | collective-permute-done | bytes 110624 | tf_op jit(solution)/shard_map/ppermute | solution.py:676
  42.4 1.2 %collective-permute-done.10.refs_2_ = f32[216,128]{1,0:T(8,128)S(1)} collective-permute-done((f32[216,128]{1,0:T(8,128)S(1)}, f32[216,128]{1,0:T(8,128)S(1)}, u32[]{:S(2)}, u32[]{:S(2)}) %collective-permute-start.10) | collective-permute-done | bytes 110624 | tf_op jit(solution)/shard_map/ppermute | solution.py:676
  45.0 2.0 %shard_map.98 = (f32[24,64,128]{2,1,0:T(8,128)S(1)}, f32[64,128]{1,0:T(8,128)S(1)}, f32[3,64,128]{2,1,0:T(8,128)S(1)}, f32[24,64,128]{2,1,0:T(8,128)S(1)}, f32[112,128]{1,0:T(8,128)S(1)}) custom-call(f32[248,128]{1,0:T(8,128)S(1)} %constant_dynamic-update-slice_fusion.refs_0_, f32[216,128]{1,0:T(8,128)S(1)} %collective-permute-done.9.refs_1_, ...), custom_call_target="tpu_custom_call" | custom-call | tf_op jit(solution)/shard_map/pallas_call | solution.py:557
  47.1 3.6 %collective-permute-start.16 = (f32[112,128]{1,0:T(8,128)S(1)}, f32[112,128]{1,0:T(8,128)S(1)}, u32[]{:S(2)}, u32[]{:S(2)}) collective-permute-start(f32[112,128]{1,0:T(8,128)S(1)} %get-tuple-element.65), channel_id=1, source_target_pairs={{0,128},{16,144},{32,160},{48,176},{64,192},{80,208},{96,224},{112... | collective-permute-start | bytes 172040 | tf_op jit(solution)/shard_map/ppermute | solution.py:708
  50.6 4.8 %collective-permute-done.16.halfway = f32[112,128]{1,0:T(8,128)S(1)} collective-permute-done((f32[112,128]{1,0:T(8,128)S(1)}, f32[112,128]{1,0:T(8,128)S(1)}, u32[]{:S(2)}, u32[]{:S(2)}) %collective-permute-start.16) | collective-permute-done | bytes 57376 | tf_op jit(solution)/shard_map/ppermute | solution.py:708
  55.9 3.8 %collective-permute-start.18 = (f32[48,128]{1,0:T(8,128)S(1)}, f32[48,128]{1,0:T(8,128)S(1)}, u32[]{:S(2)}, u32[]{:S(2)}) collective-permute-start(f32[48,128]{1,0:T(8,128)S(1)} %get-tuple-element.68), channel_id=1, source_target_pairs={{0,64},{16,80},{32,96},{48,112},{64,0},{80,16},{96,32},{112,48},{1... | collective-permute-start | bytes 73736 | tf_op jit(solution)/shard_map/ppermute | solution.py:680
  61.8 1.8 %collective-permute-done.19.new3 = f32[48,128]{1,0:T(8,128)S(1)} collective-permute-done((f32[48,128]{1,0:T(8,128)S(1)}, f32[48,128]{1,0:T(8,128)S(1)}, u32[]{:S(2)}, u32[]{:S(2)}) %collective-permute-start.19) | collective-permute-done | bytes 24608 | tf_op jit(solution)/shard_map/ppermute | solution.py:680
  63.5 1.3 %shard_map.100 = (f32[1,64,1024]{2,1,0:T(8,128)}, f32[1,2,64,1024]{3,2,1,0:T(8,128)}) custom-call(f32[1,64,1024]{2,1,0:T(8,128)S(1)} %get-tuple-element.53.depth, f32[1,2,64,1024]{3,2,1,0:T(8,128)S(1)} %get-tuple-element.54.flux, f32[48,256]{1,0:T(8,128)S(1)} %get-tuple-element.55.old, f32[48,128]{1,0:T(8,128)S(1)} %get-tuple-element.66.new0, ...), custom_call_target="tpu_custom_call" | custom-call | tf_op jit(solution)/shard_map/pallas_call | solution.py:657
  (50 shorter events, 6.3 us)
Async XLA Ops:
  0.6 17.4 %copy-start = (f32[1,2,64,1024]{3,2,1,0:T(8,128)S(1)}, f32[1,2,64,1024]{3,2,1,0:T(8,128)}, u32[]{:S(2)}) copy-start(f32[1,2,64,1024]{3,2,1,0:T(8,128)} %flux.1) | copy-start | bytes 1572868
  0.6 17.4 %copy-start.2 = (f32[64,1024]{1,0:T(8,128)S(1)}, f32[64,1024]{1,0:T(8,128)}, u32[]{:S(2)}) copy-start(f32[64,1024]{1,0:T(8,128)} %elevation.1) | copy-start | bytes 786436
  0.7 17.4 %copy-start.3 = (s32[64,1024]{1,0:T(8,128)S(1)}, s32[64,1024]{1,0:T(8,128)}, u32[]{:S(2)}) copy-start(s32[64,1024]{1,0:T(8,128)} %roughness.1) | copy-start | bytes 786436
  0.7 17.4 %copy-start.4 = (s32[64,1024]{1,0:T(8,128)S(1)}, s32[64,1024]{1,0:T(8,128)}, u32[]{:S(2)}) copy-start(s32[64,1024]{1,0:T(8,128)} %building.1) | copy-start | bytes 786436
  2.8 9.7 %collective-permute-start = (f32[384,128]{1,0:T(8,128)}, f32[384,128]{1,0:T(8,128)S(1)}, u32[]{:S(2)}, u32[]{:S(2)}) collective-permute-start(f32[384,128]{1,0:T(8,128)} %get-tuple-element.36), channel_id=1, source_target_pairs={{0,1},{1,0},{2,3},{3,2},{4,5},{5,4},{6,7},{7,6},{8,9},{9,8},{10,11... | collective-permute-start | bytes 589832 | tf_op jit(solution)/shard_map/ppermute | solution.py:688
  4.7 8.7 %collective-permute-start.1 = (f32[384,128]{1,0:T(8,128)}, f32[384,128]{1,0:T(8,128)S(1)}, u32[]{:S(2)}, u32[]{:S(2)}) collective-permute-start(f32[384,128]{1,0:T(8,128)} %get-tuple-element.37), channel_id=1, source_target_pairs={{1,2},{2,1},{5,6},{6,5},{9,10},{10,9},{13,14},{14,13},{17,18},{18,... | collective-permute-start | bytes 589832 | tf_op jit(solution)/shard_map/ppermute | solution.py:689
  8.6 8.1 %collective-permute-start.4 = (f32[48,1024]{1,0:T(8,128)}, f32[48,1024]{1,0:T(8,128)S(1)}, u32[]{:S(2)}, u32[]{:S(2)}) collective-permute-start(f32[48,1024]{1,0:T(8,128)} %get-tuple-element.38), channel_id=1, source_target_pairs={{0,4},{4,0},{8,12},{12,8},{1,5},{5,1},{9,13},{13,9},{2,6},{6,2},{1... | collective-permute-start | bytes 589832 | tf_op jit(solution)/shard_map/ppermute | solution.py:676
  10.3 7.7 %collective-permute-start.5 = (f32[48,1024]{1,0:T(8,128)}, f32[48,1024]{1,0:T(8,128)S(1)}, u32[]{:S(2)}, u32[]{:S(2)}) collective-permute-start(f32[48,1024]{1,0:T(8,128)} %get-tuple-element.39), channel_id=1, source_target_pairs={{0,12},{4,8},{8,4},{12,0},{1,13},{5,9},{9,5},{13,1},{2,14},{6,10},... | collective-permute-start | bytes 589832 | tf_op jit(solution)/shard_map/ppermute | solution.py:676
  13.5 6.7 %collective-permute-start.3 = (f32[96,128]{1,0:T(8,128)S(1)}, f32[96,128]{1,0:T(8,128)S(1)}, u32[]{:S(2)}, u32[]{:S(2)}) collective-permute-start(f32[96,128]{1,0:T(8,128)S(1)} %get-tuple-element.74), channel_id=1, source_target_pairs={{0,12},{4,8},{8,4},{12,0},{1,13},{5,9},{9,5},{13,1},{2,14},{6,10},... | collective-permute-start | bytes 147464 | tf_op jit(solution)/shard_map/ppermute | solution.py:676
  16.6 4.1 %collective-permute-start.2 = (f32[96,128]{1,0:T(8,128)S(1)}, f32[96,128]{1,0:T(8,128)S(1)}, u32[]{:S(2)}, u32[]{:S(2)}) collective-permute-start(f32[96,128]{1,0:T(8,128)S(1)} %get-tuple-element.75), channel_id=1, source_target_pairs={{0,4},{4,0},{8,12},{12,8},{1,5},{5,1},{9,13},{13,9},{2,6},{6,2},{1... | collective-permute-start | bytes 147464 | tf_op jit(solution)/shard_map/ppermute | solution.py:676
  27.8 5.7 %collective-permute-start.6 = (f32[56,128]{1,0:T(8,128)S(1)}, f32[56,128]{1,0:T(8,128)S(1)}, u32[]{:S(2)}, u32[]{:S(2)}) collective-permute-start(f32[56,128]{1,0:T(8,128)S(1)} %get-tuple-element.57), channel_id=1, source_target_pairs={{0,32},{16,48},{32,64},{48,80},{64,96},{80,112},{96,0},{112,16},{1... | collective-permute-start | bytes 86024 | tf_op jit(solution)/shard_map/ppermute | solution.py:680
  29.4 5.4 %collective-permute-start.7 = (f32[56,128]{1,0:T(8,128)S(1)}, f32[56,128]{1,0:T(8,128)S(1)}, u32[]{:S(2)}, u32[]{:S(2)}) collective-permute-start(f32[56,128]{1,0:T(8,128)S(1)} %get-tuple-element.58), channel_id=1, source_target_pairs={{0,64},{16,80},{32,96},{48,112},{64,0},{80,16},{96,32},{112,48},{1... | collective-permute-start | bytes 86024 | tf_op jit(solution)/shard_map/ppermute | solution.py:680
  32.1 3.9 %collective-permute-start.8 = (f32[56,128]{1,0:T(8,128)S(1)}, f32[56,128]{1,0:T(8,128)S(1)}, u32[]{:S(2)}, u32[]{:S(2)}) collective-permute-start(f32[56,128]{1,0:T(8,128)S(1)} %get-tuple-element.59), channel_id=1, source_target_pairs={{0,96},{16,112},{32,0},{48,16},{64,32},{80,48},{96,64},{112,80},{1... | collective-permute-start | bytes 86024 | tf_op jit(solution)/shard_map/ppermute | solution.py:680
  36.0 6.4 %collective-permute-start.11 = (f32[216,128]{1,0:T(8,128)S(1)}, f32[216,128]{1,0:T(8,128)S(1)}, u32[]{:S(2)}, u32[]{:S(2)}) collective-permute-start(f32[216,128]{1,0:T(8,128)S(1)} %get-tuple-element.84), channel_id=1, source_target_pairs={{0,8},{4,12},{8,0},{12,4},{1,9},{5,13},{9,1},{13,5},{2,10},{6,14},... | collective-permute-start | bytes 331784 | tf_op jit(solution)/shard_map/ppermute | solution.py:676
  37.4 6.2 %collective-permute-start.10 = (f32[216,128]{1,0:T(8,128)S(1)}, f32[216,128]{1,0:T(8,128)S(1)}, u32[]{:S(2)}, u32[]{:S(2)}) collective-permute-start(f32[216,128]{1,0:T(8,128)S(1)} %get-tuple-element.84), channel_id=1, source_target_pairs={{0,12},{4,8},{8,4},{12,0},{1,13},{5,9},{9,5},{13,1},{2,14},{6,10},... | collective-permute-start | bytes 331784 | tf_op jit(solution)/shard_map/ppermute | solution.py:676
  39.0 4.7 %collective-permute-start.9 = (f32[216,128]{1,0:T(8,128)S(1)}, f32[216,128]{1,0:T(8,128)S(1)}, u32[]{:S(2)}, u32[]{:S(2)}) collective-permute-start(f32[216,128]{1,0:T(8,128)S(1)} %get-tuple-element.84), channel_id=1, source_target_pairs={{0,4},{4,0},{8,12},{12,8},{1,5},{5,1},{9,13},{13,9},{2,6},{6,2},{1... | collective-permute-start | bytes 331784 | tf_op jit(solution)/shard_map/ppermute | solution.py:676
  39.6 4.5 %collective-permute-start.12 = (f32[248,128]{1,0:T(8,128)S(1)}, f32[248,128]{1,0:T(8,128)S(1)}, u32[]{:S(2)}, u32[]{:S(2)}) collective-permute-start(f32[248,128]{1,0:T(8,128)S(1)} %constant_dynamic-update-slice_fusion.refs_0_), channel_id=1, source_target_pairs={{0,16},{16,0},{32,48},{48,32},{64,80},{80,64},{96,112},{112,96},{1... | collective-permute-start | bytes 380936 | tf_op jit(solution)/shard_map/ppermute | solution.py:706
  42.4 1.7 %collective-permute-start.15 = (f32[216,128]{1,0:T(8,128)S(1)}, f32[216,128]{1,0:T(8,128)S(1)}, u32[]{:S(2)}, u32[]{:S(2)}) collective-permute-start(f32[216,128]{1,0:T(8,128)S(1)} %collective-permute-done.11.refs_3_), channel_id=1, source_target_pairs={{0,16},{16,0},{32,48},{48,32},{64,80},{80,64},{96,112},{112,96},{1... | collective-permute-start | bytes 331784 | tf_op jit(solution)/shard_map/ppermute | solution.py:706
  43.5 1.3 %collective-permute-start.14 = (f32[216,128]{1,0:T(8,128)S(1)}, f32[216,128]{1,0:T(8,128)S(1)}, u32[]{:S(2)}, u32[]{:S(2)}) collective-permute-start(f32[216,128]{1,0:T(8,128)S(1)} %collective-permute-done.10.refs_2_), channel_id=1, source_target_pairs={{0,16},{16,0},{32,48},{48,32},{64,80},{80,64},{96,112},{112,96},{1... | collective-permute-start | bytes 331784 | tf_op jit(solution)/shard_map/ppermute | solution.py:706
  43.7 1.3 %collective-permute-start.13 = (f32[216,128]{1,0:T(8,128)S(1)}, f32[216,128]{1,0:T(8,128)S(1)}, u32[]{:S(2)}, u32[]{:S(2)}) collective-permute-start(f32[216,128]{1,0:T(8,128)S(1)} %collective-permute-done.9.refs_1_), channel_id=1, source_target_pairs={{0,16},{16,0},{32,48},{48,32},{64,80},{80,64},{96,112},{112,96},{1... | collective-permute-start | bytes 331784 | tf_op jit(solution)/shard_map/ppermute | solution.py:706
  47.1 8.4 %collective-permute-start.16 = (f32[112,128]{1,0:T(8,128)S(1)}, f32[112,128]{1,0:T(8,128)S(1)}, u32[]{:S(2)}, u32[]{:S(2)}) collective-permute-start(f32[112,128]{1,0:T(8,128)S(1)} %get-tuple-element.65), channel_id=1, source_target_pairs={{0,128},{16,144},{32,160},{48,176},{64,192},{80,208},{96,224},{112... | collective-permute-start | bytes 172040 | tf_op jit(solution)/shard_map/ppermute | solution.py:708
  55.5 5.4 %collective-permute-start.17 = (f32[48,128]{1,0:T(8,128)S(1)}, f32[48,128]{1,0:T(8,128)S(1)}, u32[]{:S(2)}, u32[]{:S(2)}) collective-permute-start(f32[48,128]{1,0:T(8,128)S(1)} %get-tuple-element.67), channel_id=1, source_target_pairs={{0,32},{16,48},{32,64},{48,80},{64,96},{80,112},{96,0},{112,16},{1... | collective-permute-start | bytes 73736 | tf_op jit(solution)/shard_map/ppermute | solution.py:680
  55.9 5.9 %collective-permute-start.18 = (f32[48,128]{1,0:T(8,128)S(1)}, f32[48,128]{1,0:T(8,128)S(1)}, u32[]{:S(2)}, u32[]{:S(2)}) collective-permute-start(f32[48,128]{1,0:T(8,128)S(1)} %get-tuple-element.68), channel_id=1, source_target_pairs={{0,64},{16,80},{32,96},{48,112},{64,0},{80,16},{96,32},{112,48},{1... | collective-permute-start | bytes 73736 | tf_op jit(solution)/shard_map/ppermute | solution.py:680
  59.7 3.8 %collective-permute-start.19 = (f32[48,128]{1,0:T(8,128)S(1)}, f32[48,128]{1,0:T(8,128)S(1)}, u32[]{:S(2)}, u32[]{:S(2)}) collective-permute-start(f32[48,128]{1,0:T(8,128)S(1)} %get-tuple-element.69), channel_id=1, source_target_pairs={{0,96},{16,112},{32,0},{48,16},{64,32},{80,48},{96,64},{112,80},{1... | collective-permute-start | bytes 73736 | tf_op jit(solution)/shard_map/ppermute | solution.py:680
  (4 other events, 29.1 us)
